TPU v7x, 32 devices: a whole 2x2x4 slice. The times are simulated.
32 devices in a mesh: rep: 2 (over x), attn: 16 (over z, y, core).
Axes of the slice: x: 2, y: 2, z: 4, core: 2. Of those that a mesh axis runs over, the one named last changes fastest.
Arguments:
- moe_input: bfloat16 [768, 7168], P(('rep', 'attn')), parts along dimension 0, may hold values from -6 to 6
- expert_ids: int32 [768, 2], P(('rep', 'attn')), parts along dimension 0, may hold values from 0 to 7, all different within a row; in each aligned block of 24 rows (0 to 23, 24 to 47, ...) at most 9 rows name the same one
- route_scores: float32 [768, 2], P(('rep', 'attn')), parts along dimension 0, may hold values from 0.05 to 1
- gate_weight: bfloat16 [7168, 8192], P(None, 'attn'), may hold values from -0.0625 to 0.0625
- up_weight: bfloat16 [7168, 8192], P(None, 'attn'), may hold values from -0.0625 to 0.0625
- down_weight: bfloat16 [8192, 7168], P('attn'), may hold values from -0.1875 to 0.1875
- q_latent: bfloat16 [192, 4, 32768], P(('rep', 'attn')), parts along dimension 0, may hold values from -6 to 6
- q_rope: bfloat16 [192, 4, 4096], P(('rep', 'attn')), parts along dimension 0, may hold values from -450 to 450
- latent_cache: bfloat16 [192, 256, 512], P(('rep', 'attn')), parts along dimension 0, may hold values from -6 to 6
- rope_cache: bfloat16 [192, 256, 64], P(('rep', 'attn')), parts along dimension 0, may hold values from -6 to 6
- cache_lengths: int32 [192], P(('rep', 'attn')), parts along dimension 0, may hold values from 6 to 256, as said below
Outputs:
- moe_output: bfloat16 [768, 7168], P(('rep', 'attn')), parts along dimension 0
- attn_output: bfloat16 [192, 4, 32768], P(('rep', 'attn')), parts along dimension 0
There are 2 independent parts, one for each index of `rep`. A program takes and returns all parts, laid end to end along the dimension named above; an argument that names none is the same for every part. Nothing has to cross between parts.
Inputs may be any that keep to these rules, and one draw needn't show every extreme that they name: `expert_ids`: each row names 2 different experts. In each aligned block of 24 rows no expert is named by more than 9 rows, and in some block an expert is named by exactly 9 rows. `cache_lengths`: some sequence fills all 256 positions.
All inputs are finite; a program needn't handle non-finite values.
Results may differ from a plain program's by a relative error of at most 0.012.
Values may be sent and summed in bfloat16 or wider, within the bound.
No kernel may reach another device: no remote copies, remote signals or barrier semaphores. Data moves between devices by JAX's collectives and lax.ppermute only.
A program may use at most 128 MiB of HBM per device.

v0:
```python
import jax
import jax.numpy as jnp
from jax import lax
from jax.sharding import PartitionSpec as P

EXPERTS = 8
CAP = 9


score_factor = 192.0 ** (-0.5)
route_factor = 2.5


def slot_table(block_ids):
    flat = block_ids.reshape(-1)
    picks = block_ids.shape[1]
    onehot = (flat[:, None] == jnp.arange(EXPERTS, dtype=jnp.int32)[None, :]).astype(jnp.int32)
    before = jnp.cumsum(onehot, axis=0) - onehot
    slot = jnp.sum(before * onehot, axis=1)
    place = flat * CAP + slot
    source = jnp.arange(flat.shape[0], dtype=jnp.int32) // picks + 1
    owner = jnp.zeros((EXPERTS * CAP,), jnp.int32).at[place].set(source) - 1
    return (place, owner)


def expert_rows(received, gate_weight, up_weight, down_weight):
    features = received.shape[-1]
    flat_rows = received.reshape(-1, features)
    gate_part = jnp.dot(flat_rows, gate_weight, preferred_element_type=jnp.float32)
    up_part = jnp.dot(flat_rows, up_weight, preferred_element_type=jnp.float32)
    hidden = (jax.nn.silu(gate_part) * up_part).astype(jnp.bfloat16)
    partial_value = jnp.dot(hidden, down_weight, preferred_element_type=jnp.float32)
    return partial_value.astype(jnp.bfloat16).reshape(received.shape)


def attend(q_latent, q_rope, latent_cache, rope_cache, cache_lengths):
    seq_count, step_count, _ = q_latent.shape
    cache_len = latent_cache.shape[1]
    latent_width = latent_cache.shape[2]
    rope_width = rope_cache.shape[2]
    head_count = q_latent.shape[2] // latent_width
    query_lat = q_latent.reshape(seq_count, step_count, head_count, latent_width)
    query_rot = q_rope.reshape(seq_count, step_count, head_count, rope_width)
    scores = jnp.einsum(
        "bthc,bpc->bthp", query_lat, latent_cache, preferred_element_type=jnp.float32
    )
    scores = scores + jnp.einsum(
        "bthc,bpc->bthp", query_rot, rope_cache, preferred_element_type=jnp.float32
    )
    scores = scores * score_factor
    position = jnp.arange(cache_len, dtype=jnp.int32)
    limit = cache_lengths[:, None] - step_count + jnp.arange(step_count, dtype=jnp.int32)[None, :]
    allowed = position[None, None, None, :] <= limit[:, :, None, None]
    scores = jnp.where(allowed, scores, -jnp.inf)
    largest = jnp.max(scores, axis=-1, keepdims=True)
    weights = jnp.exp(scores - largest)
    probs = (weights / jnp.sum(weights, axis=-1, keepdims=True)).astype(jnp.bfloat16)
    attn = jnp.einsum("bthp,bpc->bthc", probs, latent_cache, preferred_element_type=jnp.float32)
    return attn.astype(jnp.bfloat16).reshape(seq_count, step_count, head_count * latent_width)


def body(
    moe_input,
    expert_ids,
    route_scores,
    gate_weight,
    up_weight,
    down_weight,
    q_latent,
    q_rope,
    latent_cache,
    rope_cache,
    cache_lengths,
):
    members = lax.axis_size("attn")
    shards = members // EXPERTS
    features = moe_input.shape[1]
    place, owner = slot_table(expert_ids)
    picked = moe_input[jnp.maximum(owner, 0)]
    slot_rows = jnp.where((owner >= 0)[:, None], picked, jnp.zeros_like(picked))
    outbound = jnp.broadcast_to(
        slot_rows.reshape(EXPERTS, 1, CAP, features), (EXPERTS, shards, CAP, features)
    )
    outbound = outbound.reshape(members, CAP, features)
    partial_value = expert_rows(
        lax.all_to_all(outbound, "attn", split_axis=0, concat_axis=0, tiled=True),
        gate_weight,
        up_weight,
        down_weight,
    )
    returned = lax.all_to_all(partial_value, "attn", split_axis=0, concat_axis=0, tiled=True)
    attn_output = attend(q_latent, q_rope, latent_cache, rope_cache, cache_lengths)
    grouped = returned.reshape((EXPERTS, shards) + returned.shape[1:]).astype(jnp.float32)
    expert_out = jnp.sum(grouped, axis=1).astype(jnp.bfloat16)
    combine = route_factor * route_scores / jnp.sum(route_scores, axis=1, keepdims=True)
    token_count, picks = expert_ids.shape
    values = expert_out.reshape(EXPERTS * CAP, features)[place].astype(jnp.float32)
    values = values.reshape(token_count, picks, features)
    moe_output = jnp.sum(values * combine[:, :, None], axis=1).astype(jnp.bfloat16)
    return (moe_output, attn_output)


def solution(mesh):
    placed = (
        P(("rep", "attn"), None),
        P(("rep", "attn"), None),
        P(("rep", "attn"), None),
        P(None, "attn"),
        P(None, "attn"),
        P("attn", None),
        P(("rep", "attn"), None, None),
        P(("rep", "attn"), None, None),
        P(("rep", "attn"), None, None),
        P(("rep", "attn"), None, None),
        P(("rep", "attn")),
    )
    return jax.shard_map(
        body,
        mesh=mesh,
        in_specs=placed,
        out_specs=(P(("rep", "attn"), None), P(("rep", "attn"), None, None)),
        check_vma=False,
    )
```

profile of v0, /device:TPU:13, one launch (start us, length us, event | category | flops | bytes accessed | tf_op | source)
XLA Modules:
  0.0 218.9 jit_solution(15632825984696318028)
XLA Ops:
  0.6 0.9 copy.17
  1.5 0.7 broadcast_multiply_fusion
  2.8 0.7 scatter_custom_fusion
  3.6 4.1 %gather_fusion = bf16[72,7168]{1,0:T(8,128)(2,1)} fusion(bf16[24,7168]{1,0:T(8,128)(2,1)} %param.11, s32[1024]{0:T(1024)S(1)} %pad_clamp_fusion.1), kind=kCustom, calls=%fused_computation | custom fusion | bytes 2064672 | tf_op jit(solution)/shard_map/gather | solution.py:79
  7.7 1.7 gather.9
  10.2 87.5 %all_to_all.10 = bf16[16,9,7168]{2,1,0:T(8,128)(2,1)} all-to-all(bf16[16,9,7168]{2,1,0:T(8,128)(2,1)S(1)} %bitcast.34), channel_id=1, replica_groups=mesh['rep'=2,'attn'=16] {'attn'}, dimensions={0} | all-to-all | bytes 4128768 | tf_op jit(solution)/shard_map/all_to_all | solution.py:86
  97.7 3.5 %reshape.110 = bf16[144,7168]{1,0:T(8,128)(2,1)} reshape(bf16[16,9,7168]{2,1,0:T(8,128)(2,1)} %all_to_all.10) | data formatting | bytes 4128768 | tf_op jit(solution)/shard_map/reshape | solution.py:28
  101.2 4.9 %fusion.26 = f32[144,512]{1,0:T(8,128)S(1)} fusion(bf16[144,7168]{1,0:T(8,128)(2,1)} %reshape.110, bf16[7168,512]{1,0:T(8,128)(2,1)} %param.14), kind=kOutput, calls=%fused_computation.52 | convolution fusion | flops 1056964608 | bytes 9699328 | tf_op jit(solution)/shard_map/dot_general | solution.py:29
  106.2 9.5 %convolution_convert_fusion = bf16[144,7168]{1,0:T(8,128)(2,1)} fusion(bf16[512,7168]{1,0:T(8,128)(2,1)} %param.16, bf16[144,7168]{1,0:T(8,128)(2,1)} %reshape.110, bf16[7168,512]{1,0:T(8,128)(2,1)} %param.15, f32[144,512]{1,0:T(8,128)S(1)} %fusion.26), kind=kOutput, calls=%fused_computation.4 | convolution fusion | flops 2115403776 | bytes 19103744 | tf_op jit(solution)/shard_map/dot_general | solution.py:32
  115.7 3.5 %reshape.111 = bf16[16,9,7168]{2,1,0:T(8,128)(2,1)} reshape(bf16[144,7168]{1,0:T(8,128)(2,1)} %convolution_convert_fusion) | data formatting | bytes 4128768 | tf_op jit(solution)/shard_map/reshape | solution.py:33
  119.2 5.4 %all-to-all-start.1 = ((bf16[16,9,7168]{2,1,0:T(8,128)(2,1)}), bf16[16,9,7168]{2,1,0:T(8,128)(2,1)}, u32[]{:S(2)}, u32[]{:S(2)}) async-start(bf16[16,9,7168]{2,1,0:T(8,128)(2,1)} %reshape.111), calls=%async_computation.1 | async-start | bytes 7340032 | tf_op jit(solution)/shard_map/all_to_all | solution.py:91
  125.1 2.9 %reshape.114 = bf16[6,4,64,512]{3,2,1,0:T(8,128)(2,1)S(1)} reshape(bf16[6,4,32768]{2,1,0:T(4,128)(2,1)} %param.17) | data formatting | bytes 3145728 | tf_op jit(solution)/shard_map/reshape | solution.py:42
  127.9 0.7 broadcast_add_fusion
  128.8 1.3 fusion.15
  130.0 0.6 multiply_select_fusion
  130.7 1.1 copy-done.1
  132.3 4.7 %convolution_convert_fusion.1 = bf16[6,4,64,512]{3,2,1,0:T(8,128)(2,1)S(1)} fusion(bf16[6,256,512]{2,1,0:T(8,128)(2,1)S(1)} %copy-done, f32[6,4,64]{2,1,0:T(4,128)S(1)} %fusion.25, f32[6,4,64,256]{3,2,1,0:T(8,128)} %copy-done.1), kind=kOutput, calls=%fused_computation.8 | convolution fusion | flops 404621056 | bytes 4724736 | tf_op jit(solution)/shard_map/bthp,bpc->bthc/dot_general | solution.py:58
  137.0 2.4 %reshape.116 = bf16[6,4,32768]{2,1,0:T(4,128)(2,1)} reshape(bf16[6,4,64,512]{3,2,1,0:T(8,128)(2,1)S(1)} %convolution_convert_fusion.1) | data formatting | bytes 3145728 | tf_op jit(solution)/shard_map/reshape | solution.py:59
  139.4 66.4 %all-to-all-done.1 = bf16[16,9,7168]{2,1,0:T(8,128)(2,1)} async-done(((bf16[16,9,7168]{2,1,0:T(8,128)(2,1)}), bf16[16,9,7168]{2,1,0:T(8,128)(2,1)}, u32[]{:S(2)}, u32[]{:S(2)}) %all-to-all-start.1) | async-done | bytes 2064416 | tf_op jit(solution)/shard_map/all_to_all | solution.py:91
  205.8 4.6 %bitcast_reduce_fusion = bf16[8,9,7168]{2,1,0:T(8,128)(2,1)} fusion(bf16[16,9,7168]{2,1,0:T(8,128)(2,1)} %all-to-all-done.1), kind=kLoop, calls=%fused_computation.5 | loop fusion | flops 516096 | bytes 3096576 | tf_op jit(solution)/shard_map/reduce_sum | solution.py:94
  210.5 2.0 reshape.113
  212.4 1.8 gather_fusion.1
  214.3 2.0 reshape.117
  216.3 2.6 %multiply_reduce_fusion = bf16[24,7168]{1,0:T(8,128)(2,1)} fusion(f32[24,2,7168]{2,1,0:T(2,128)S(1)} %reshape.117, f32[24,2]{1,0:T(8,128)S(1)} %copy.18), kind=kLoop, calls=%fused_computation.15 | loop fusion | flops 516096 | bytes 1720512 | tf_op jit(solution)/shard_map/reduce_sum | solution.py:99
  (29 shorter events, 2.5 us)
Async XLA Ops:
  0.6 129.4 %copy-start = (bf16[6,256,512]{2,1,0:T(8,128)(2,1)S(1)}, bf16[6,256,512]{2,1,0:T(8,128)(2,1)}, u32[]{:S(2)}) copy-start(bf16[6,256,512]{2,1,0:T(8,128)(2,1)} %param.19) | copy-start | bytes 4718596
  119.2 5.4 %copy-start.3 = (f32[24,2]{0,1:T(2,128)S(1)}, f32[24,2]{0,1:T(2,128)}, u32[]{:S(2)}) copy-start(f32[24,2]{0,1:T(2,128)} %param.13) | copy-start | bytes 580
  119.2 5.5 %copy-start.2 = (bf16[6,4,4096]{2,1,0:T(4,128)(2,1)S(1)}, bf16[6,4,4096]{2,1,0:T(4,128)(2,1)}, u32[]{:S(2)}) copy-start(bf16[6,4,4096]{2,1,0:T(4,128)(2,1)} %param.18) | copy-start | bytes 589828
  119.2 86.6 %all-to-all-start.1 = ((bf16[16,9,7168]{2,1,0:T(8,128)(2,1)}), bf16[16,9,7168]{2,1,0:T(8,128)(2,1)}, u32[]{:S(2)}, u32[]{:S(2)}) async-start(bf16[16,9,7168]{2,1,0:T(8,128)(2,1)} %reshape.111), calls=%async_computation.1 | async-start | bytes 7340032 | tf_op jit(solution)/shard_map/all_to_all | solution.py:91
  130.7 1.1 copy-start.1
where the time goes:
time: 219 us
  blocking collectives  87.5 us (40%)
  waiting for transfers between devices  66.4 us (30%)
  local copies, waits for them, and re-layouts  28 us (13%)
  matrix products  21.1 us (10%)
  other arithmetic  9.76 us (4%)
  starting transfers between devices  5.36 us (2%)
    all_to_all x1, blocking collectives, body(): lax.all_to_all(outbound, 'attn', split_axis=0, concat_axis=0, tiled=True)  87.5 us
    all_to_all x1, waiting for transfers between devices, body(): lax.all_to_all(partial_value, 'attn', split_axis=0, concat_axis=0, tiled=...  66.4 us
    dot_general x1, matrix products, expert_rows(): jnp.dot(hidden, down_weight, preferred_element_type=jnp.float32)  9.54 us
    gather x2, local copies, waits for them, and re-layouts, body(): picked = moe_input[jnp.maximum(owner, 0)]  5.82 us
    all_to_all x1, starting transfers between devices, body(): lax.all_to_all(partial_value, 'attn', split_axis=0, concat_axis=0, tiled=...  5.36 us
    dot_general x1, matrix products, expert_rows(): jnp.dot(flat_rows, gate_weight, preferred_element_type=jnp.float32)  4.94 us
    dot_general x1, matrix products, attend(): jnp.einsum('bthp,bpc->bthc', probs, latent_cache, preferred_element_type=...  4.71 us
    reduce_sum x1, other arithmetic, body(): expert_out = jnp.sum(grouped, axis=1).astype(jnp.bfloat16)  4.62 us
  transfers between devices with their start and end apart: 1, of which 1 were waited for; matrix products, arithmetic and copies ran while one was open for 6% of the time, Pallas kernels for 0%

commit v1 on v0

--- a/solution.py
+++ b/solution.py
@@ -1,24 +1,210 @@
+import functools
+
 import jax
 import jax.numpy as jnp
 from jax import lax
+from jax.experimental import pallas as pl
+from jax.experimental.pallas import tpu as pltpu
 from jax.sharding import PartitionSpec as P
 
 EXPERTS = 8
 CAP = 9
-
+SUB = 8
+MIB = 1 << 20
 
 score_factor = 192.0 ** (-0.5)
 route_factor = 2.5
+
+f32 = jnp.float32
+bf16 = jnp.bfloat16
+
+
+def dot(a, b):
+    return jnp.dot(a, b, preferred_element_type=f32)
+
+
+def dot_t(a, b):
+    return lax.dot_general(a, b, (((0,), (0,)), ((), ())), preferred_element_type=f32)
+
+
+def routing(ids, chip):
+    rows = ids.shape[0]
+    col = lax.broadcasted_iota(jnp.int32, (rows, EXPERTS * SUB), 1)
+    expert = jnp.bitwise_xor(col // SUB, chip)
+    first = ids[:, 0:1] == expert
+    hit = first | (ids[:, 1:2] == expert)
+    r = lax.broadcasted_iota(jnp.int32, (rows, rows), 0)
+    c = lax.broadcasted_iota(jnp.int32, (rows, rows), 1)
+    slot = dot((c < r).astype(f32).astype(bf16), hit.astype(f32).astype(bf16)).astype(jnp.int32)
+    return hit, slot, first, col % SUB
+
+
+def pack_kernel(chip_ref, ids_ref, x_ref, *outs):
+    features = x_ref.shape[1]
+    tail = features // SUB
+    hit, slot, _, s = routing(ids_ref[...], chip_ref[0])
+    zero = jnp.zeros(hit.shape, f32)
+    pick = jnp.where(hit & (slot == s), 1.0, zero).astype(bf16)
+    main = dot_t(pick, x_ref[...]).astype(bf16)
+    last = jnp.zeros((EXPERTS * SUB, tail), f32)
+    for i in range(SUB):
+        pick = jnp.where(hit & (slot == SUB) & (s == i), 1.0, zero).astype(bf16)
+        last = last + dot_t(pick, x_ref[:, i * tail:(i + 1) * tail])
+    last = last.astype(bf16)
+    for m, out in enumerate(outs):
+        out[:, :features] = main[m * SUB:(m + 1) * SUB]
+        out[:, features:] = last[m * SUB:(m + 1) * SUB]
+
+
+def pack(chip, ids, x):
+    features = x.shape[1]
+    wide = features + features // SUB
+    return pl.pallas_call(
+        pack_kernel,
+        out_shape=[jax.ShapeDtypeStruct((SUB, wide), bf16)] * EXPERTS,
+        in_specs=[pl.BlockSpec(memory_space=pltpu.SMEM)] + [pl.BlockSpec(memory_space=pltpu.VMEM)] * 2,
+        out_specs=[pl.BlockSpec(memory_space=pltpu.VMEM)] * EXPERTS,
+        compiler_params=pltpu.CompilerParams(vmem_limit_bytes=12 * MIB),
+        name="pack",
+    )(chip, ids, x)
+
+
+def spread(i, count):
+    j = lax.broadcasted_iota(jnp.int32, (count, count * SUB), 0)
+    c = lax.broadcasted_iota(jnp.int32, (count, count * SUB), 1)
+    return jnp.where(c == j * SUB + i, 1.0, jnp.zeros((count, count * SUB), f32)).astype(bf16)
+
+
+def expert_kernel(count, *refs):
+    ins, (gate_ref, up_ref, down_ref) = refs[:count], refs[count:count + 3]
+    outs, (rows_ref, tail_ref, acc_ref) = refs[count + 3:2 * count + 3], refs[2 * count + 3:]
+    features, units = gate_ref.shape
+    tail = features // SUB
+    top = count * SUB
+    for j, ref in enumerate(ins):
+        rows_ref[j * SUB:(j + 1) * SUB, :] = ref[:, :features]
+        tail_ref[j * SUB:(j + 1) * SUB, :] = ref[:, features:]
+    folded = tail_ref[...]
+    for i in range(SUB):
+        rows_ref[top:, i * tail:(i + 1) * tail] = dot(spread(i, count), folded).astype(bf16)
+    acc_ref[...] = jnp.zeros_like(acc_ref)
+    step = 1024
+
+    def contract(k, carry):
+        at = pl.ds(pl.multiple_of(k * step, step), step)
+        a = rows_ref[:, at]
+        acc_ref[:, :units] += dot(a, gate_ref[at, :])
+        acc_ref[:, units:] += dot(a, up_ref[at, :])
+        return carry
+
+    lax.fori_loop(0, features // step, contract, 0)
+    hidden = (jax.nn.silu(acc_ref[:, :units]) * acc_ref[:, units:]).astype(bf16)
+    folded = jnp.zeros((top, tail), f32)
+    for k in range(SUB // 2):
+        part = dot(hidden, down_ref[:, 2 * k * tail:2 * (k + 1) * tail]).astype(bf16)
+        for j, out in enumerate(outs):
+            out[:, 2 * k * tail:2 * (k + 1) * tail] = part[j * SUB:(j + 1) * SUB]
+        folded = folded + dot_t(spread(2 * k, count), part[top:, :tail])
+        folded = folded + dot_t(spread(2 * k + 1, count), part[top:, tail:])
+    folded = folded.astype(bf16)
+    for j, out in enumerate(outs):
+        out[:, features:] = folded[j * SUB:(j + 1) * SUB]
+
+
+def experts(buffers, gate_weight, up_weight, down_weight):
+    count = len(buffers)
+    features, units = gate_weight.shape
+    vmem = pl.BlockSpec(memory_space=pltpu.VMEM)
+    return pl.pallas_call(
+        functools.partial(expert_kernel, count),
+        out_shape=[jax.ShapeDtypeStruct(buffers[0].shape, bf16)] * count,
+        in_specs=[vmem] * (count + 3),
+        out_specs=[vmem] * count,
+        scratch_shapes=[
+            pltpu.VMEM((count * CAP, features), bf16),
+            pltpu.VMEM((count * SUB, features // SUB), bf16),
+            pltpu.VMEM((count * CAP, 2 * units), f32),
+        ],
+        compiler_params=pltpu.CompilerParams(vmem_limit_bytes=36 * MIB),
+        name="experts",
+    )(*buffers, gate_weight, up_weight, down_weight)
+
+
+def combine_kernel(chip_ref, ids_ref, scores_ref, *refs):
+    ins, out_ref, (rows_ref, tail_ref) = refs[:EXPERTS], refs[EXPERTS], refs[EXPERTS + 1:]
+    features = out_ref.shape[1]
+    tail = features // SUB
+    hit, slot, first, s = routing(ids_ref[...], chip_ref[0])
+    scores = scores_ref[...]
+    weight = route_factor * scores / (scores[:, 0:1] + scores[:, 1:2])
+    weight = jnp.where(first, weight[:, 0:1], weight[:, 1:2])
+    zero = jnp.zeros(hit.shape, f32)
+    for m, ref in enumerate(ins):
+        rows_ref[m * SUB:(m + 1) * SUB, :] = ref[:, :features]
+        tail_ref[m * SUB:(m + 1) * SUB, :] = ref[:, features:]
+
+    def parts(mask):
+        w = jnp.where(mask, weight, zero)
+        high = w.astype(bf16)
+        return high, (w - high.astype(f32)).astype(bf16)
+
+    high, low = parts(hit & (slot == s))
+    folded = tail_ref[...]
+    for i in range(SUB):
+        at = slice(i * tail, (i + 1) * tail)
+        last_high, last_low = parts(hit & (slot == SUB) & (s == i))
+        total = dot(high, rows_ref[:, at]) + dot(low, rows_ref[:, at])
+        total = total + dot(last_high, folded) + dot(last_low, folded)
+        out_ref[:, at] = total.astype(bf16)
+
+
+def combine(chip, ids, scores, buffers, features):
+    vmem = pl.BlockSpec(memory_space=pltpu.VMEM)
+    return pl.pallas_call(
+        combine_kernel,
+        out_shape=jax.ShapeDtypeStruct((ids.shape[0], features), bf16),
+        in_specs=[pl.BlockSpec(memory_space=pltpu.SMEM)] + [vmem] * (2 + EXPERTS),
+        out_specs=vmem,
+        scratch_shapes=[
+            pltpu.VMEM((EXPERTS * SUB, features), bf16),
+            pltpu.VMEM((EXPERTS * SUB, features // SUB), bf16),
+        ],
+        compiler_params=pltpu.CompilerParams(vmem_limit_bytes=12 * MIB),
+        name="combine",
+    )(chip, ids, scores, *buffers)
+
+
+def moe_by_chips(moe_input, expert_ids, route_scores, gate_weight, up_weight, down_weight):
+    features = moe_input.shape[1]
+    members = lax.axis_size("attn")
+    chip = (lax.axis_index("attn") // 2).astype(jnp.int32).reshape(1)
+
+    def across(value, m):
+        return lax.ppermute(value, "attn", [(i, i ^ (2 * m)) for i in range(members)])
+
+    def sibling(value):
+        return lax.ppermute(value, "attn", [(i, i ^ 1) for i in range(members)])
+
+    sent = pack(chip, expert_ids, moe_input)
+    mine = [sent[0]] + [across(sent[m], m) for m in range(1, EXPERTS)]
+    theirs = [sibling(value) for value in mine]
+    partial = experts(mine + theirs, gate_weight, up_weight, down_weight)
+    other = [sibling(value) for value in partial[EXPERTS:]]
+    total = [(a.astype(f32) + b.astype(f32)).astype(bf16) for a, b in zip(partial[:EXPERTS], other)]
+    back = [total[0]] + [across(total[m], m) for m in range(1, EXPERTS)]
+    return combine(chip, expert_ids, route_scores, back, features)
 
 
 def slot_table(block_ids):
     flat = block_ids.reshape(-1)
     picks = block_ids.shape[1]
+    count = flat.shape[0]
     onehot = (flat[:, None] == jnp.arange(EXPERTS, dtype=jnp.int32)[None, :]).astype(jnp.int32)
-    before = jnp.cumsum(onehot, axis=0) - onehot
-    slot = jnp.sum(before * onehot, axis=1)
+    earlier = jnp.arange(count)[:, None] > jnp.arange(count)[None, :]
+    same = flat[:, None] == flat[None, :]
+    slot = jnp.sum((earlier & same).astype(jnp.int32), axis=1)
     place = flat * CAP + slot
-    source = jnp.arange(flat.shape[0], dtype=jnp.int32) // picks + 1
+    source = jnp.arange(count, dtype=jnp.int32) // picks + 1
     owner = jnp.zeros((EXPERTS * CAP,), jnp.int32).at[place].set(source) - 1
     return (place, owner)
 
@@ -31,6 +217,33 @@
     hidden = (jax.nn.silu(gate_part) * up_part).astype(jnp.bfloat16)
     partial_value = jnp.dot(hidden, down_weight, preferred_element_type=jnp.float32)
     return partial_value.astype(jnp.bfloat16).reshape(received.shape)
+
+
+def moe_by_slots(moe_input, expert_ids, route_scores, gate_weight, up_weight, down_weight):
+    members = lax.axis_size("attn")
+    shards = members // EXPERTS
+    features = moe_input.shape[1]
+    place, owner = slot_table(expert_ids)
+    picked = moe_input[jnp.maximum(owner, 0)]
+    slot_rows = jnp.where((owner >= 0)[:, None], picked, jnp.zeros_like(picked))
+    outbound = jnp.broadcast_to(
+        slot_rows.reshape(EXPERTS, 1, CAP, features), (EXPERTS, shards, CAP, features)
+    )
+    outbound = outbound.reshape(members, CAP, features)
+    partial_value = expert_rows(
+        lax.all_to_all(outbound, "attn", split_axis=0, concat_axis=0, tiled=True),
+        gate_weight,
+        up_weight,
+        down_weight,
+    )
+    returned = lax.all_to_all(partial_value, "attn", split_axis=0, concat_axis=0, tiled=True)
+    grouped = returned.reshape((EXPERTS, shards) + returned.shape[1:]).astype(jnp.float32)
+    expert_out = jnp.sum(grouped, axis=1).astype(jnp.bfloat16)
+    combine_weight = route_factor * route_scores / jnp.sum(route_scores, axis=1, keepdims=True)
+    token_count, picks = expert_ids.shape
+    values = expert_out.reshape(EXPERTS * CAP, features)[place].astype(jnp.float32)
+    values = values.reshape(token_count, picks, features)
+    return jnp.sum(values * combine_weight[:, :, None], axis=1).astype(jnp.bfloat16)
 
 
 def attend(q_latent, q_rope, latent_cache, rope_cache, cache_lengths):
@@ -72,31 +285,9 @@
     rope_cache,
     cache_lengths,
 ):
-    members = lax.axis_size("attn")
-    shards = members // EXPERTS
-    features = moe_input.shape[1]
-    place, owner = slot_table(expert_ids)
-    picked = moe_input[jnp.maximum(owner, 0)]
-    slot_rows = jnp.where((owner >= 0)[:, None], picked, jnp.zeros_like(picked))
-    outbound = jnp.broadcast_to(
-        slot_rows.reshape(EXPERTS, 1, CAP, features), (EXPERTS, shards, CAP, features)
-    )
-    outbound = outbound.reshape(members, CAP, features)
-    partial_value = expert_rows(
-        lax.all_to_all(outbound, "attn", split_axis=0, concat_axis=0, tiled=True),
-        gate_weight,
-        up_weight,
-        down_weight,
-    )
-    returned = lax.all_to_all(partial_value, "attn", split_axis=0, concat_axis=0, tiled=True)
+    moe = moe_by_chips if lax.axis_size("attn") == 2 * EXPERTS else moe_by_slots
+    moe_output = moe(moe_input, expert_ids, route_scores, gate_weight, up_weight, down_weight)
     attn_output = attend(q_latent, q_rope, latent_cache, rope_cache, cache_lengths)
-    grouped = returned.reshape((EXPERTS, shards) + returned.shape[1:]).astype(jnp.float32)
-    expert_out = jnp.sum(grouped, axis=1).astype(jnp.bfloat16)
-    combine = route_factor * route_scores / jnp.sum(route_scores, axis=1, keepdims=True)
-    token_count, picks = expert_ids.shape
-    values = expert_out.reshape(EXPERTS * CAP, features)[place].astype(jnp.float32)
-    values = values.reshape(token_count, picks, features)
-    moe_output = jnp.sum(values * combine[:, :, None], axis=1).astype(jnp.bfloat16)
     return (moe_output, attn_output)
 
 

time: 219 us -> 98 us (0.45)
  the two profiles are of different devices: /device:TPU:13 before, /device:TPU:0 now
where the time goes in v1:
time: 98 us; the launch traced here: 97.7 us
  starting transfers between devices  38.9 us (40%)
  local copies, waits for them, and re-layouts  19.4 us (20%)
  Pallas kernels  14.6 us (15%)
  waiting for transfers between devices  14 us (14%)
  matrix products  7.99 us (8%)
  other arithmetic  1.82 us (2%)
    ppermute x14, starting transfers between devices, across(): return lax.ppermute(value, 'attn', [(i, i ^ 2 * m) for i in range(members)])  35.2 us
    ppermute x14, waiting for transfers between devices, across(): return lax.ppermute(value, 'attn', [(i, i ^ 2 * m) for i in range(members)])  13.5 us
    pallas_call x1, Pallas kernels, experts(): pl.pallas_call(functools.partial(expert_kernel, count), out_shape=[jax.Sh...  12.1 us
    unnamed x44, local copies, waits for them, and re-layouts  9.62 us
    dot_general x1, matrix products, attend(): jnp.einsum('bthp,bpc->bthc', probs, latent_cache, preferred_element_type=...  5.88 us
    reshape x1, local copies, waits for them, and re-layouts, attend(): attn.astype(jnp.bfloat16)  3.92 us
    reshape x1, local copies, waits for them, and re-layouts, attend(): q_latent.reshape(seq_count, step_count, head_count, latent_width)  3.86 us
    ppermute x16, starting transfers between devices, sibling(): return lax.ppermute(value, 'attn', [(i, i ^ 1) for i in range(members)])  3.78 us
  transfers between devices with their start and end apart: 30, of which 9 were waited for; matrix products, arithmetic and copies ran while one was open for 20% of the time, Pallas kernels for 0%

profile of v1, /device:TPU:0, one launch (start us, length us, event | category | flops | bytes accessed | tf_op | source)
XLA Modules:
  0.0 97.7 jit_solution(11479955958070513115)
XLA Ops:
  1.5 1.0 copy-done.2
  3.4 4.0 %collective-permute-start.2 = (bf16[8,8064]{1,0:T(8,128)(2,1)S(1)}, bf16[8,8064]{1,0:T(8,128)(2,1)S(1)}, u32[]{:S(2)}, u32[]{:S(2)}) collective-permute-start(bf16[8,8064]{1,0:T(8,128)(2,1)S(1)} %get-tuple-element.29), channel_id=1, source_target_pairs={{0,6},{1,7},{2,4},{3,5},{4,2},{5,3},{6,0},{7,1},{8,14},{9,15},{10,... | collective-permute-start | bytes 387080 | tf_op jit(solution)/shard_map/ppermute | solution.py:183
  7.4 2.6 %collective-permute-start.3 = (bf16[8,8064]{1,0:T(8,128)(2,1)S(1)}, bf16[8,8064]{1,0:T(8,128)(2,1)S(1)}, u32[]{:S(2)}, u32[]{:S(2)}) collective-permute-start(bf16[8,8064]{1,0:T(8,128)(2,1)S(1)} %get-tuple-element.30), channel_id=1, source_target_pairs={{0,8},{1,9},{2,10},{3,11},{4,12},{5,13},{6,14},{7,15},{8,0},{9,1},... | collective-permute-start | bytes 387080 | tf_op jit(solution)/shard_map/ppermute | solution.py:183
  10.3 2.5 %collective-permute-start.5 = (bf16[8,8064]{1,0:T(8,128)(2,1)S(1)}, bf16[8,8064]{1,0:T(8,128)(2,1)S(1)}, u32[]{:S(2)}, u32[]{:S(2)}) collective-permute-start(bf16[8,8064]{1,0:T(8,128)(2,1)S(1)} %get-tuple-element.32), channel_id=1, source_target_pairs={{0,12},{1,13},{2,14},{3,15},{4,8},{5,9},{6,10},{7,11},{8,4},{9,5},... | collective-permute-start | bytes 387080 | tf_op jit(solution)/shard_map/ppermute | solution.py:183
  12.8 2.3 %collective-permute-start.6 = (bf16[8,8064]{1,0:T(8,128)(2,1)S(1)}, bf16[8,8064]{1,0:T(8,128)(2,1)S(1)}, u32[]{:S(2)}, u32[]{:S(2)}) collective-permute-start(bf16[8,8064]{1,0:T(8,128)(2,1)S(1)} %get-tuple-element.33), channel_id=1, source_target_pairs={{0,14},{1,15},{2,12},{3,13},{4,10},{5,11},{6,8},{7,9},{8,6},{9,7},... | collective-permute-start | bytes 387080 | tf_op jit(solution)/shard_map/ppermute | solution.py:183
  15.1 2.0 %reshape.49 = bf16[6,4,64,64]{3,2,1,0:T(8,128)(2,1)} reshape(bf16[6,4,4096]{2,1,0:T(4,128)(2,1)} %param.18) | data formatting | bytes 393216 | tf_op jit(solution)/shard_map/reshape | solution.py:256
  17.1 3.9 %reshape.48 = bf16[6,4,64,512]{3,2,1,0:T(8,128)(2,1)} reshape(bf16[6,4,32768]{2,1,0:T(4,128)(2,1)} %param.17) | data formatting | bytes 3145728 | tf_op jit(solution)/shard_map/reshape | solution.py:255
  21.0 1.4 %fusion.9 = f32[6,4,64,256]{3,2,1,0:T(8,128)S(1)} fusion(bf16[6,4,64,64]{3,2,1,0:T(8,128)(2,1)} %reshape.49, bf16[6,256,64]{1,2,0:T(8,128)(2,1)S(1)} %copy-done.18), kind=kOutput, calls=%fused_computation.18 | convolution fusion | flops 50331648 | bytes 1966080 | tf_op jit(solution)/shard_map/bthc,bpc->bthp/dot_general | solution.py:260
  23.1 2.3 %collective-permute-done.3.refs_4_ = bf16[8,8064]{1,0:T(8,128)(2,1)S(1)} collective-permute-done((bf16[8,8064]{1,0:T(8,128)(2,1)S(1)}, bf16[8,8064]{1,0:T(8,128)(2,1)S(1)}, u32[]{:S(2)}, u32[]{:S(2)}) %collective-permute-start.3) | collective-permute-done | bytes 129056 | tf_op jit(solution)/shard_map/ppermute | solution.py:183
  25.4 2.1 %collective-permute-done.4.refs_5_ = bf16[8,8064]{1,0:T(8,128)(2,1)S(1)} collective-permute-done((bf16[8,8064]{1,0:T(8,128)(2,1)S(1)}, bf16[8,8064]{1,0:T(8,128)(2,1)S(1)}, u32[]{:S(2)}, u32[]{:S(2)}) %collective-permute-start.4) | collective-permute-done | bytes 129056 | tf_op jit(solution)/shard_map/ppermute | solution.py:183
  32.4 3.1 %copy-done.1 = bf16[7168,512]{1,0:T(8,128)(2,1)S(1)} copy-done((bf16[7168,512]{1,0:T(8,128)(2,1)S(1)}, bf16[7168,512]{1,0:T(8,128)(2,1)}, u32[]{:S(2)}) %copy-start.1) | copy-done | bytes 7340056
  35.5 12.1 %experts.1 = (bf16[8,8064]{1,0:T(8,128)(2,1)S(1)}, bf16[8,8064]{1,0:T(8,128)(2,1)S(1)}, bf16[8,8064]{1,0:T(8,128)(2,1)S(1)}, bf16[8,8064]{1,0:T(8,128)(2,1)S(1)}...) custom-call(bf16[8,8064]{1,0:T(8,128)(2,1)S(1)} %get-tuple-element.2, ...), custom_call_target="tpu_custom_call" | custom-call | tf_op jit(solution)/shard_map/experts/pallas_call | solution.py:118
  52.5 5.9 %convolution_convert_fusion = bf16[6,4,64,512]{3,2,1,0:T(8,128)(2,1)} fusion(bf16[6,256,512]{2,1,0:T(8,128)(2,1)S(1)} %copy-done, f32[6,4,64]{2,1,0:T(4,128)S(1)} %fusion.12, f32[6,4,64,256]{3,2,1,0:T(8,128)} %copy-done.16), kind=kOutput, calls=%fused_computation.2 | convolution fusion | flops 404621056 | bytes 4724736 | tf_op jit(solution)/shard_map/bthp,bpc->bthc/dot_general | solution.py:271
  58.5 3.9 %reshape.50 = bf16[6,4,32768]{2,1,0:T(4,128)(2,1)} reshape(bf16[6,4,64,512]{3,2,1,0:T(8,128)(2,1)} %convolution_convert_fusion) | data formatting | bytes 3145728 | tf_op jit(solution)/shard_map/reshape | solution.py:272
  65.3 3.2 %collective-permute-start.29 = (bf16[8,8064]{1,0:T(8,128)(2,1)S(1)}, bf16[8,8064]{1,0:T(8,128)(2,1)S(1)}, u32[]{:S(2)}, u32[]{:S(2)}) collective-permute-start(bf16[8,8064]{1,0:T(8,128)(2,1)S(1)} %add_convert_fusion), channel_id=1, source_target_pairs={{0,14},{1,15},{2,12},{3,13},{4,10},{5,11},{6,8},{7,9},{8,6},{9,7},... | collective-permute-start | bytes 387080 | tf_op jit(solution)/shard_map/ppermute | solution.py:183
  68.6 1.2 %collective-permute-start.27 = (bf16[8,8064]{1,0:T(8,128)(2,1)S(1)}, bf16[8,8064]{1,0:T(8,128)(2,1)S(1)}, u32[]{:S(2)}, u32[]{:S(2)}) collective-permute-start(bf16[8,8064]{1,0:T(8,128)(2,1)S(1)} %add_convert_fusion.1), channel_id=1, source_target_pairs={{0,12},{1,13},{2,14},{3,15},{4,8},{5,9},{6,10},{7,11},{8,4},{9,5},... | collective-permute-start | bytes 387080 | tf_op jit(solution)/shard_map/ppermute | solution.py:183
  69.8 3.8 %collective-permute-start.25 = (bf16[8,8064]{1,0:T(8,128)(2,1)S(1)}, bf16[8,8064]{1,0:T(8,128)(2,1)S(1)}, u32[]{:S(2)}, u32[]{:S(2)}) collective-permute-start(bf16[8,8064]{1,0:T(8,128)(2,1)S(1)} %add_convert_fusion.2), channel_id=1, source_target_pairs={{0,10},{1,11},{2,8},{3,9},{4,14},{5,15},{6,12},{7,13},{8,2},{9,3},... | collective-permute-start | bytes 387080 | tf_op jit(solution)/shard_map/ppermute | solution.py:183
  73.9 2.9 %collective-permute-start.21 = (bf16[8,8064]{1,0:T(8,128)(2,1)S(1)}, bf16[8,8064]{1,0:T(8,128)(2,1)S(1)}, u32[]{:S(2)}, u32[]{:S(2)}) collective-permute-start(bf16[8,8064]{1,0:T(8,128)(2,1)S(1)} %add_convert_fusion.4), channel_id=1, source_target_pairs={{0,6},{1,7},{2,4},{3,5},{4,2},{5,3},{6,0},{7,1},{8,14},{9,15},{10,... | collective-permute-start | bytes 387080 | tf_op jit(solution)/shard_map/ppermute | solution.py:183
  76.8 10.4 %collective-permute-start.19 = (bf16[8,8064]{1,0:T(8,128)(2,1)S(1)}, bf16[8,8064]{1,0:T(8,128)(2,1)S(1)}, u32[]{:S(2)}, u32[]{:S(2)}) collective-permute-start(bf16[8,8064]{1,0:T(8,128)(2,1)S(1)} %add_convert_fusion.5), channel_id=1, source_target_pairs={{0,4},{1,5},{2,6},{3,7},{4,0},{5,1},{6,2},{7,3},{8,12},{9,13},{10,... | collective-permute-start | bytes 387080 | tf_op jit(solution)/shard_map/ppermute | solution.py:183
  87.2 1.3 %collective-permute-start.17 = (bf16[8,8064]{1,0:T(8,128)(2,1)S(1)}, bf16[8,8064]{1,0:T(8,128)(2,1)S(1)}, u32[]{:S(2)}, u32[]{:S(2)}) collective-permute-start(bf16[8,8064]{1,0:T(8,128)(2,1)S(1)} %add_convert_fusion.6), channel_id=1, source_target_pairs={{0,2},{1,3},{2,0},{3,1},{4,6},{5,7},{6,4},{7,5},{8,10},{9,11},{10,... | collective-permute-start | bytes 387080 | tf_op jit(solution)/shard_map/ppermute | solution.py:183
  88.5 2.8 %collective-permute-done.25.refs_5_ = bf16[8,8064]{1,0:T(8,128)(2,1)S(1)} collective-permute-done((bf16[8,8064]{1,0:T(8,128)(2,1)S(1)}, bf16[8,8064]{1,0:T(8,128)(2,1)S(1)}, u32[]{:S(2)}, u32[]{:S(2)}) %collective-permute-start.25) | collective-permute-done | bytes 129056 | tf_op jit(solution)/shard_map/ppermute | solution.py:183
  91.2 2.5 %collective-permute-done.23.refs_4_ = bf16[8,8064]{1,0:T(8,128)(2,1)S(1)} collective-permute-done((bf16[8,8064]{1,0:T(8,128)(2,1)S(1)}, bf16[8,8064]{1,0:T(8,128)(2,1)S(1)}, u32[]{:S(2)}, u32[]{:S(2)}) %collective-permute-start.23) | collective-permute-done | bytes 129056 | tf_op jit(solution)/shard_map/ppermute | solution.py:183
  93.8 2.2 %collective-permute-done.19.refs_2_ = bf16[8,8064]{1,0:T(8,128)(2,1)S(1)} collective-permute-done((bf16[8,8064]{1,0:T(8,128)(2,1)S(1)}, bf16[8,8064]{1,0:T(8,128)(2,1)S(1)}, u32[]{:S(2)}, u32[]{:S(2)}) %collective-permute-start.19) | collective-permute-done | bytes 129056 | tf_op jit(solution)/shard_map/ppermute | solution.py:183
  96.0 1.7 %combine.1 = bf16[24,7168]{1,0:T(8,128)(2,1)} custom-call(s32[1]{0:T(128)} %bitcast.chip_ref, s32[24,2]{1,0:T(8,128)S(1)} %copy.14.ids_ref, f32[24,2]{1,0:T(8,128)S(1)} %copy.15.scores_ref, bf16[8,8064]{1,0:T(8,128)(2,1)S(1)} %add_convert_fusion.7.refs_0_, bf16[8,8064]{1,0:T(8,128)(2,1)S(1)} %collective-permute-done.17.refs_1_, ...), custom_call_target="tpu_custom_call" | custom-call | tf_op jit(solution)/shard_map/combine/pallas_call | solution.py:163
  (101 shorter events, 15.8 us)
Async XLA Ops:
  3.4 19.2 %collective-permute-start.2 = (bf16[8,8064]{1,0:T(8,128)(2,1)S(1)}, bf16[8,8064]{1,0:T(8,128)(2,1)S(1)}, u32[]{:S(2)}, u32[]{:S(2)}) collective-permute-start(bf16[8,8064]{1,0:T(8,128)(2,1)S(1)} %get-tuple-element.29), channel_id=1, source_target_pairs={{0,6},{1,7},{2,4},{3,5},{4,2},{5,3},{6,0},{7,1},{8,14},{9,15},{10,... | collective-permute-start | bytes 387080 | tf_op jit(solution)/shard_map/ppermute | solution.py:183
  7.4 18.0 %collective-permute-start.3 = (bf16[8,8064]{1,0:T(8,128)(2,1)S(1)}, bf16[8,8064]{1,0:T(8,128)(2,1)S(1)}, u32[]{:S(2)}, u32[]{:S(2)}) collective-permute-start(bf16[8,8064]{1,0:T(8,128)(2,1)S(1)} %get-tuple-element.30), channel_id=1, source_target_pairs={{0,8},{1,9},{2,10},{3,11},{4,12},{5,13},{6,14},{7,15},{8,0},{9,1},... | collective-permute-start | bytes 387080 | tf_op jit(solution)/shard_map/ppermute | solution.py:183
  10.0 17.5 %collective-permute-start.4 = (bf16[8,8064]{1,0:T(8,128)(2,1)S(1)}, bf16[8,8064]{1,0:T(8,128)(2,1)S(1)}, u32[]{:S(2)}, u32[]{:S(2)}) collective-permute-start(bf16[8,8064]{1,0:T(8,128)(2,1)S(1)} %get-tuple-element.31), channel_id=1, source_target_pairs={{0,10},{1,11},{2,8},{3,9},{4,14},{5,15},{6,12},{7,13},{8,2},{9,3},... | collective-permute-start | bytes 387080 | tf_op jit(solution)/shard_map/ppermute | solution.py:183
  10.3 17.2 %collective-permute-start.5 = (bf16[8,8064]{1,0:T(8,128)(2,1)S(1)}, bf16[8,8064]{1,0:T(8,128)(2,1)S(1)}, u32[]{:S(2)}, u32[]{:S(2)}) collective-permute-start(bf16[8,8064]{1,0:T(8,128)(2,1)S(1)} %get-tuple-element.32), channel_id=1, source_target_pairs={{0,12},{1,13},{2,14},{3,15},{4,8},{5,9},{6,10},{7,11},{8,4},{9,5},... | collective-permute-start | bytes 387080 | tf_op jit(solution)/shard_map/ppermute | solution.py:183
  12.8 15.2 %collective-permute-start.6 = (bf16[8,8064]{1,0:T(8,128)(2,1)S(1)}, bf16[8,8064]{1,0:T(8,128)(2,1)S(1)}, u32[]{:S(2)}, u32[]{:S(2)}) collective-permute-start(bf16[8,8064]{1,0:T(8,128)(2,1)S(1)} %get-tuple-element.33), channel_id=1, source_target_pairs={{0,14},{1,15},{2,12},{3,13},{4,10},{5,11},{6,8},{7,9},{8,6},{9,7},... | collective-permute-start | bytes 387080 | tf_op jit(solution)/shard_map/ppermute | solution.py:183
  22.6 7.0 %collective-permute-start = (bf16[8,8064]{1,0:T(8,128)(2,1)S(1)}, bf16[8,8064]{1,0:T(8,128)(2,1)S(1)}, u32[]{:S(2)}, u32[]{:S(2)}) collective-permute-start(bf16[8,8064]{1,0:T(8,128)(2,1)S(1)} %get-tuple-element.27), channel_id=1, source_target_pairs={{0,2},{1,3},{2,0},{3,1},{4,6},{5,7},{6,4},{7,5},{8,10},{9,11},{10,... | collective-permute-start | bytes 387080 | tf_op jit(solution)/shard_map/ppermute | solution.py:183
  25.4 4.9 %collective-permute-start.1 = (bf16[8,8064]{1,0:T(8,128)(2,1)S(1)}, bf16[8,8064]{1,0:T(8,128)(2,1)S(1)}, u32[]{:S(2)}, u32[]{:S(2)}) collective-permute-start(bf16[8,8064]{1,0:T(8,128)(2,1)S(1)} %get-tuple-element.28), channel_id=1, source_target_pairs={{0,4},{1,5},{2,6},{3,7},{4,0},{5,1},{6,2},{7,3},{8,12},{9,13},{10,... | collective-permute-start | bytes 387080 | tf_op jit(solution)/shard_map/ppermute | solution.py:183
  27.5 2.9 %collective-permute-start.7 = (bf16[8,8064]{1,0:T(8,128)(2,1)S(1)}, bf16[8,8064]{1,0:T(8,128)(2,1)S(1)}, u32[]{:S(2)}, u32[]{:S(2)}) collective-permute-start(bf16[8,8064]{1,0:T(8,128)(2,1)S(1)} %get-tuple-element.26.refs_0_), channel_id=1, source_target_pairs={{0,1},{1,0},{2,3},{3,2},{4,5},{5,4},{6,7},{7,6},{8,9},{9,8},{10,11... | collective-permute-start | bytes 387080 | tf_op jit(solution)/shard_map/ppermute | solution.py:186
  27.5 3.4 %collective-permute-start.10 = (bf16[8,8064]{1,0:T(8,128)(2,1)S(1)}, bf16[8,8064]{1,0:T(8,128)(2,1)S(1)}, u32[]{:S(2)}, u32[]{:S(2)}) collective-permute-start(bf16[8,8064]{1,0:T(8,128)(2,1)S(1)} %collective-permute-done.2.refs_3_), channel_id=1, source_target_pairs={{0,1},{1,0},{2,3},{3,2},{4,5},{5,4},{6,7},{7,6},{8,9},{9,8},{10,11... | collective-permute-start | bytes 387080 | tf_op jit(solution)/shard_map/ppermute | solution.py:186
  28.0 3.0 %collective-permute-start.11 = (bf16[8,8064]{1,0:T(8,128)(2,1)S(1)}, bf16[8,8064]{1,0:T(8,128)(2,1)S(1)}, u32[]{:S(2)}, u32[]{:S(2)}) collective-permute-start(bf16[8,8064]{1,0:T(8,128)(2,1)S(1)} %collective-permute-done.3.refs_4_), channel_id=1, source_target_pairs={{0,1},{1,0},{2,3},{3,2},{4,5},{5,4},{6,7},{7,6},{8,9},{9,8},{10,11... | collective-permute-start | bytes 387080 | tf_op jit(solution)/shard_map/ppermute | solution.py:186
  52.2 11.3 %collective-permute-start.28 = (bf16[8,8064]{1,0:T(8,128)(2,1)}, bf16[8,8064]{1,0:T(8,128)(2,1)}, u32[]{:S(2)}, u32[]{:S(2)}) collective-permute-start(bf16[8,8064]{1,0:T(8,128)(2,1)} %get-tuple-element.49), channel_id=1, source_target_pairs={{0,1},{1,0},{2,3},{3,2},{4,5},{5,4},{6,7},{7,6},{8,9},{9,8},{10,11... | collective-permute-start | bytes 387080 | tf_op jit(solution)/shard_map/ppermute | solution.py:186
  62.6 2.4 %collective-permute-start.24 = (bf16[8,8064]{1,0:T(8,128)(2,1)S(1)}, bf16[8,8064]{1,0:T(8,128)(2,1)S(1)}, u32[]{:S(2)}, u32[]{:S(2)}) collective-permute-start(bf16[8,8064]{1,0:T(8,128)(2,1)S(1)} %copy-done.14), channel_id=1, source_target_pairs={{0,1},{1,0},{2,3},{3,2},{4,5},{5,4},{6,7},{7,6},{8,9},{9,8},{10,11... | collective-permute-start | bytes 387080 | tf_op jit(solution)/shard_map/ppermute | solution.py:186
  62.9 2.4 %collective-permute-start.22 = (bf16[8,8064]{1,0:T(8,128)(2,1)S(1)}, bf16[8,8064]{1,0:T(8,128)(2,1)S(1)}, u32[]{:S(2)}, u32[]{:S(2)}) collective-permute-start(bf16[8,8064]{1,0:T(8,128)(2,1)S(1)} %copy-done.12), channel_id=1, source_target_pairs={{0,1},{1,0},{2,3},{3,2},{4,5},{5,4},{6,7},{7,6},{8,9},{9,8},{10,11... | collective-permute-start | bytes 387080 | tf_op jit(solution)/shard_map/ppermute | solution.py:186
  63.1 5.5 %collective-permute-start.20 = (bf16[8,8064]{1,0:T(8,128)(2,1)S(1)}, bf16[8,8064]{1,0:T(8,128)(2,1)S(1)}, u32[]{:S(2)}, u32[]{:S(2)}) collective-permute-start(bf16[8,8064]{1,0:T(8,128)(2,1)S(1)} %copy-done.10), channel_id=1, source_target_pairs={{0,1},{1,0},{2,3},{3,2},{4,5},{5,4},{6,7},{7,6},{8,9},{9,8},{10,11... | collective-permute-start | bytes 387080 | tf_op jit(solution)/shard_map/ppermute | solution.py:186
  63.4 6.4 %collective-permute-start.18 = (bf16[8,8064]{1,0:T(8,128)(2,1)S(1)}, bf16[8,8064]{1,0:T(8,128)(2,1)S(1)}, u32[]{:S(2)}, u32[]{:S(2)}) collective-permute-start(bf16[8,8064]{1,0:T(8,128)(2,1)S(1)} %copy-done.8), channel_id=1, source_target_pairs={{0,1},{1,0},{2,3},{3,2},{4,5},{5,4},{6,7},{7,6},{8,9},{9,8},{10,11... | collective-permute-start | bytes 387080 | tf_op jit(solution)/shard_map/ppermute | solution.py:186
  64.6 9.1 %collective-permute-start.16 = (bf16[8,8064]{1,0:T(8,128)(2,1)S(1)}, bf16[8,8064]{1,0:T(8,128)(2,1)S(1)}, u32[]{:S(2)}, u32[]{:S(2)}) collective-permute-start(bf16[8,8064]{1,0:T(8,128)(2,1)S(1)} %copy-done.6), channel_id=1, source_target_pairs={{0,1},{1,0},{2,3},{3,2},{4,5},{5,4},{6,7},{7,6},{8,9},{9,8},{10,11... | collective-permute-start | bytes 387080 | tf_op jit(solution)/shard_map/ppermute | solution.py:186
  65.0 8.8 %collective-permute-start.15 = (bf16[8,8064]{1,0:T(8,128)(2,1)S(1)}, bf16[8,8064]{1,0:T(8,128)(2,1)S(1)}, u32[]{:S(2)}, u32[]{:S(2)}) collective-permute-start(bf16[8,8064]{1,0:T(8,128)(2,1)S(1)} %copy-done.4), channel_id=1, source_target_pairs={{0,1},{1,0},{2,3},{3,2},{4,5},{5,4},{6,7},{7,6},{8,9},{9,8},{10,11... | collective-permute-start | bytes 387080 | tf_op jit(solution)/shard_map/ppermute | solution.py:186
  65.3 11.4 %collective-permute-start.29 = (bf16[8,8064]{1,0:T(8,128)(2,1)S(1)}, bf16[8,8064]{1,0:T(8,128)(2,1)S(1)}, u32[]{:S(2)}, u32[]{:S(2)}) collective-permute-start(bf16[8,8064]{1,0:T(8,128)(2,1)S(1)} %add_convert_fusion), channel_id=1, source_target_pairs={{0,14},{1,15},{2,12},{3,13},{4,10},{5,11},{6,8},{7,9},{8,6},{9,7},... | collective-permute-start | bytes 387080 | tf_op jit(solution)/shard_map/ppermute | solution.py:183
  68.6 18.6 %collective-permute-start.27 = (bf16[8,8064]{1,0:T(8,128)(2,1)S(1)}, bf16[8,8064]{1,0:T(8,128)(2,1)S(1)}, u32[]{:S(2)}, u32[]{:S(2)}) collective-permute-start(bf16[8,8064]{1,0:T(8,128)(2,1)S(1)} %add_convert_fusion.1), channel_id=1, source_target_pairs={{0,12},{1,13},{2,14},{3,15},{4,8},{5,9},{6,10},{7,11},{8,4},{9,5},... | collective-permute-start | bytes 387080 | tf_op jit(solution)/shard_map/ppermute | solution.py:183
  69.8 21.4 %collective-permute-start.25 = (bf16[8,8064]{1,0:T(8,128)(2,1)S(1)}, bf16[8,8064]{1,0:T(8,128)(2,1)S(1)}, u32[]{:S(2)}, u32[]{:S(2)}) collective-permute-start(bf16[8,8064]{1,0:T(8,128)(2,1)S(1)} %add_convert_fusion.2), channel_id=1, source_target_pairs={{0,10},{1,11},{2,8},{3,9},{4,14},{5,15},{6,12},{7,13},{8,2},{9,3},... | collective-permute-start | bytes 387080 | tf_op jit(solution)/shard_map/ppermute | solution.py:183
  73.7 20.1 %collective-permute-start.23 = (bf16[8,8064]{1,0:T(8,128)(2,1)S(1)}, bf16[8,8064]{1,0:T(8,128)(2,1)S(1)}, u32[]{:S(2)}, u32[]{:S(2)}) collective-permute-start(bf16[8,8064]{1,0:T(8,128)(2,1)S(1)} %add_convert_fusion.3), channel_id=1, source_target_pairs={{0,8},{1,9},{2,10},{3,11},{4,12},{5,13},{6,14},{7,15},{8,0},{9,1},... | collective-permute-start | bytes 387080 | tf_op jit(solution)/shard_map/ppermute | solution.py:183
  73.9 19.9 %collective-permute-start.21 = (bf16[8,8064]{1,0:T(8,128)(2,1)S(1)}, bf16[8,8064]{1,0:T(8,128)(2,1)S(1)}, u32[]{:S(2)}, u32[]{:S(2)}) collective-permute-start(bf16[8,8064]{1,0:T(8,128)(2,1)S(1)} %add_convert_fusion.4), channel_id=1, source_target_pairs={{0,6},{1,7},{2,4},{3,5},{4,2},{5,3},{6,0},{7,1},{8,14},{9,15},{10,... | collective-permute-start | bytes 387080 | tf_op jit(solution)/shard_map/ppermute | solution.py:183
  76.8 19.2 %collective-permute-start.19 = (bf16[8,8064]{1,0:T(8,128)(2,1)S(1)}, bf16[8,8064]{1,0:T(8,128)(2,1)S(1)}, u32[]{:S(2)}, u32[]{:S(2)}) collective-permute-start(bf16[8,8064]{1,0:T(8,128)(2,1)S(1)} %add_convert_fusion.5), channel_id=1, source_target_pairs={{0,4},{1,5},{2,6},{3,7},{4,0},{5,1},{6,2},{7,3},{8,12},{9,13},{10,... | collective-permute-start | bytes 387080 | tf_op jit(solution)/shard_map/ppermute | solution.py:183
  87.2 8.8 %collective-permute-start.17 = (bf16[8,8064]{1,0:T(8,128)(2,1)S(1)}, bf16[8,8064]{1,0:T(8,128)(2,1)S(1)}, u32[]{:S(2)}, u32[]{:S(2)}) collective-permute-start(bf16[8,8064]{1,0:T(8,128)(2,1)S(1)} %add_convert_fusion.6), channel_id=1, source_target_pairs={{0,2},{1,3},{2,0},{3,1},{4,6},{5,7},{6,4},{7,5},{8,10},{9,11},{10,... | collective-permute-start | bytes 387080 | tf_op jit(solution)/shard_map/ppermute | solution.py:183
  (27 other events, 101.9 us)

commit v2 on v1

v2 whole, which is shorter than its diff:
```python
import functools

import jax
import jax.numpy as jnp
from jax import lax
from jax.experimental import pallas as pl
from jax.experimental.pallas import tpu as pltpu
from jax.sharding import PartitionSpec as P

EXPERTS = 8
CAP = 9
SUB = 8
FOLD = SUB // 2
MIB = 1 << 20
ORDER = (7, 6, 5, 4, 3, 2, 1)
VMEM = pl.BlockSpec(memory_space=pltpu.VMEM)

score_factor = 192.0 ** (-0.5)
route_factor = 2.5

f32 = jnp.float32
bf16 = jnp.bfloat16


def dot(a, b):
    return jnp.dot(a, b, preferred_element_type=f32)


def dot_t(a, b):
    return lax.dot_general(a, b, (((0,), (0,)), ((), ())), preferred_element_type=f32)


def routing(ids, chip):
    rows = ids.shape[1]
    shape = (EXPERTS * SUB, rows)
    at = lax.broadcasted_iota(jnp.int32, shape, 0)
    expert = jnp.bitwise_xor(at // SUB, chip)
    first = ids[0:1, :] == expert
    hit = first | (ids[1:2, :] == expert)
    r = lax.broadcasted_iota(jnp.int32, (rows, rows), 0)
    c = lax.broadcasted_iota(jnp.int32, (rows, rows), 1)
    slot = dot(hit.astype(f32).astype(bf16), (r < c).astype(f32).astype(bf16)).astype(jnp.int32)
    return hit, slot, first, at % SUB


def ones(mask):
    return jnp.where(mask, 1.0, jnp.zeros(mask.shape, f32)).astype(bf16)


def pack_kernel(chip_ref, ids_ref, x_ref, *outs):
    features = x_ref.shape[1]
    tail = features // SUB
    hit, slot, _, q = routing(ids_ref[...], chip_ref[0])
    main = dot(ones(hit & (slot == q)), x_ref[...]).astype(bf16)
    last = jnp.zeros((EXPERTS * SUB, tail), f32)
    for i in range(SUB):
        last = last + dot(ones(hit & (slot == SUB) & (q == i)), x_ref[:, i * tail:(i + 1) * tail])
    last = last.astype(bf16)
    for m, out in enumerate(outs):
        out[:, :features] = main[m * SUB:(m + 1) * SUB]
        out[:, features:] = last[m * SUB:(m + 1) * SUB]


def pack(chip, ids, x):
    features = x.shape[1]
    return pl.pallas_call(
        pack_kernel,
        out_shape=[jax.ShapeDtypeStruct((SUB, features + features // SUB), bf16)] * EXPERTS,
        in_specs=[pl.BlockSpec(memory_space=pltpu.SMEM)] + [VMEM] * 2,
        out_specs=[VMEM] * EXPERTS,
        compiler_params=pltpu.CompilerParams(vmem_limit_bytes=12 * MIB),
        name="pack",
    )(chip, ids, x)


def spread(i, count):
    j = lax.broadcasted_iota(jnp.int32, (count, count * SUB), 0)
    c = lax.broadcasted_iota(jnp.int32, (count, count * SUB), 1)
    return ones(c == j * SUB + i)


def expert_kernel(groups, *refs):
    ins, (gate_hbm, up_hbm, down_hbm) = refs[:groups], refs[groups:groups + 3]
    mine_ref, theirs_ref = refs[groups + 3:groups + 5]
    gate_ref, up_ref, down_ref, rows_ref, tail_ref, acc_ref, sems = refs[groups + 5:]
    features, units = gate_ref.shape
    tail = features // SUB
    top = tail_ref.shape[0]
    count = top // SUB
    wide = 2 * tail
    copies = []
    for k in range(FOLD):
        rows = pl.ds(k * wide, wide)
        for ref, to in ((gate_hbm, gate_ref), (up_hbm, up_ref)):
            copies.append(pltpu.make_async_copy(ref.at[rows], to.at[rows], sems.at[len(copies)]))
    for k in range(FOLD):
        columns = pl.ds(k * wide, wide)
        copies.append(pltpu.make_async_copy(down_hbm.at[:, columns], down_ref.at[:, columns], sems.at[len(copies)]))
    for copy in copies:
        copy.start()
    start = 0
    for ref in ins:
        rows = slice(start, start + ref.shape[0])
        rows_ref[rows, :] = ref[:, :features]
        tail_ref[rows, :] = ref[:, features:]
        start += ref.shape[0]
    folded = tail_ref[...]
    for i in range(SUB):
        rows_ref[top:, i * tail:(i + 1) * tail] = dot(spread(i, count), folded).astype(bf16)
    for k in range(FOLD):
        at = slice(k * wide, (k + 1) * wide)
        for n, ref in enumerate((gate_ref, up_ref)):
            copies[2 * k + n].wait()
            columns = slice(n * units, (n + 1) * units)
            product = dot(rows_ref[:, at], ref[at, :])
            acc_ref[:, columns] = product if k == 0 else acc_ref[:, columns] + product
    hidden = (jax.nn.silu(acc_ref[:, :units]) * acc_ref[:, units:]).astype(bf16)
    folded = jnp.zeros((top, tail), f32)
    for k in range(FOLD):
        copies[2 * FOLD + k].wait()
        at = slice(k * wide, (k + 1) * wide)
        part = dot(hidden, down_ref[:, at]).astype(bf16)
        mine_ref[:, at] = part[:top // 2]
        theirs_ref[:, at] = part[top // 2:top]
        folded = folded + dot_t(spread(2 * k, count), part[top:, :tail])
        folded = folded + dot_t(spread(2 * k + 1, count), part[top:, tail:])
    folded = folded.astype(bf16)
    mine_ref[:, features:] = folded[:top // 2]
    theirs_ref[:, features:] = folded[top // 2:]


def experts(groups, gate_weight, up_weight, down_weight):
    features, units = gate_weight.shape
    top = sum(group.shape[0] for group in groups)
    rows = top + top // SUB
    wide = groups[0].shape[1]
    return pl.pallas_call(
        functools.partial(expert_kernel, len(groups)),
        out_shape=[jax.ShapeDtypeStruct((top // 2, wide), bf16)] * 2,
        in_specs=[VMEM] * len(groups) + [pl.BlockSpec(memory_space=pltpu.HBM)] * 3,
        out_specs=[VMEM] * 2,
        scratch_shapes=[
            pltpu.VMEM(gate_weight.shape, bf16),
            pltpu.VMEM(up_weight.shape, bf16),
            pltpu.VMEM(down_weight.shape, bf16),
            pltpu.VMEM((rows, features), bf16),
            pltpu.VMEM((top, features // SUB), bf16),
            pltpu.VMEM((rows, 2 * units), f32),
            pltpu.SemaphoreType.DMA((3 * FOLD,)),
        ],
        compiler_params=pltpu.CompilerParams(vmem_limit_bytes=36 * MIB),
        cost_estimate=pl.CostEstimate(
            flops=6 * rows * features * units, bytes_accessed=6 * features * units, transcendentals=0
        ),
        name="experts",
    )(*groups, gate_weight, up_weight, down_weight)


def add_kernel(a_ref, b_ref, *outs):
    for m, out in enumerate(outs):
        rows = slice(m * SUB, (m + 1) * SUB)
        out[...] = (a_ref[rows, :].astype(f32) + b_ref[rows, :].astype(f32)).astype(bf16)


def add(a, b):
    return pl.pallas_call(
        add_kernel,
        out_shape=[jax.ShapeDtypeStruct((SUB, a.shape[1]), bf16)] * EXPERTS,
        in_specs=[VMEM] * 2,
        out_specs=[VMEM] * EXPERTS,
        compiler_params=pltpu.CompilerParams(vmem_limit_bytes=6 * MIB),
        name="add",
    )(a, b)


def combine_kernel(chip_ref, ids_ref, scores_ref, *refs):
    ins, out_ref, rows_ref = refs[:EXPERTS], refs[EXPERTS], refs[EXPERTS + 1]
    features = out_ref.shape[1]
    tail = features // SUB
    hit, slot, first, q = routing(ids_ref[...], chip_ref[0])
    scores = scores_ref[...]
    weight = route_factor * scores / (scores[0:1, :] + scores[1:2, :])
    weight = jnp.where(first, weight[0:1, :], weight[1:2, :])
    for m, ref in zip(ORDER + (0,), ins):
        rows_ref[m * SUB:(m + 1) * SUB, :] = ref[...]

    def weighted(mask, values):
        w = jnp.where(mask, weight, jnp.zeros_like(weight))
        high = w.astype(bf16)
        low = (w - high.astype(f32)).astype(bf16)
        return dot_t(high, values) + dot_t(low, values)

    folded = rows_ref[:, features:]
    for i in range(SUB):
        at = slice(i * tail, (i + 1) * tail)
        total = weighted(hit & (slot == q), rows_ref[:, at])
        total = total + weighted(hit & (slot == SUB) & (q == i), folded)
        out_ref[:, at] = total.astype(bf16)


def combine(chip, ids, scores, buffers, features):
    return pl.pallas_call(
        combine_kernel,
        out_shape=jax.ShapeDtypeStruct((ids.shape[1], features), bf16),
        in_specs=[pl.BlockSpec(memory_space=pltpu.SMEM)] + [VMEM] * (2 + EXPERTS),
        out_specs=VMEM,
        scratch_shapes=[pltpu.VMEM((EXPERTS * SUB, features + features // SUB), bf16)],
        compiler_params=pltpu.CompilerParams(vmem_limit_bytes=12 * MIB),
        name="combine",
    )(chip, ids, scores, *buffers)


def after(values, *others):
    return lax.optimization_barrier((values, others))[0]


def moe_by_chips(moe_input, expert_ids, route_scores, gate_weight, up_weight, down_weight, attention):
    features = moe_input.shape[1]
    members = lax.axis_size("attn")
    chip = (lax.axis_index("attn") // 2).astype(jnp.int32).reshape(1)
    ids, scores = expert_ids.T, route_scores.T
    weights = [
        pltpu.with_memory_space_constraint(w, pltpu.HBM) for w in (gate_weight, up_weight, down_weight)
    ]
    probs, finish = attention

    def sibling(value):
        return lax.ppermute(value, "attn", [(i, i ^ 1) for i in range(members)])

    def exchange(sent):
        got = {0: sent[0]}
        for m in ORDER:
            got[m] = lax.ppermute(sent[m], "attn", [(i, i ^ (2 * m)) for i in range(members)])
        return got

    got = exchange(pack(chip, ids, moe_input))
    order = (0,) + ORDER[FOLD:] + ORDER[:FOLD]
    first = jnp.concatenate([got[m] for m in order[:FOLD]], axis=0)
    second = jnp.concatenate([got[m] for m in order[FOLD:]], axis=0)
    second = after(second, probs)
    mine, theirs = experts([first, second, sibling(first), sibling(second)], *weights)
    total = add(mine, sibling(theirs))
    attn_output = finish(after(probs, *total))
    back = exchange({m: total[place] for place, m in enumerate(order)})
    moe_output = combine(chip, ids, scores, [back[m] for m in ORDER + (0,)], features)
    return moe_output, attn_output


def slot_table(block_ids):
    flat = block_ids.reshape(-1)
    picks = block_ids.shape[1]
    count = flat.shape[0]
    onehot = (flat[:, None] == jnp.arange(EXPERTS, dtype=jnp.int32)[None, :]).astype(jnp.int32)
    earlier = jnp.arange(count)[:, None] > jnp.arange(count)[None, :]
    same = flat[:, None] == flat[None, :]
    slot = jnp.sum((earlier & same).astype(jnp.int32), axis=1)
    place = flat * CAP + slot
    source = jnp.arange(count, dtype=jnp.int32) // picks + 1
    owner = jnp.zeros((EXPERTS * CAP,), jnp.int32).at[place].set(source) - 1
    return (place, owner)


def expert_rows(received, gate_weight, up_weight, down_weight):
    features = received.shape[-1]
    flat_rows = received.reshape(-1, features)
    gate_part = jnp.dot(flat_rows, gate_weight, preferred_element_type=jnp.float32)
    up_part = jnp.dot(flat_rows, up_weight, preferred_element_type=jnp.float32)
    hidden = (jax.nn.silu(gate_part) * up_part).astype(jnp.bfloat16)
    partial_value = jnp.dot(hidden, down_weight, preferred_element_type=jnp.float32)
    return partial_value.astype(jnp.bfloat16).reshape(received.shape)


def moe_by_slots(moe_input, expert_ids, route_scores, gate_weight, up_weight, down_weight, attention):
    members = lax.axis_size("attn")
    shards = members // EXPERTS
    features = moe_input.shape[1]
    place, owner = slot_table(expert_ids)
    picked = moe_input[jnp.maximum(owner, 0)]
    slot_rows = jnp.where((owner >= 0)[:, None], picked, jnp.zeros_like(picked))
    outbound = jnp.broadcast_to(
        slot_rows.reshape(EXPERTS, 1, CAP, features), (EXPERTS, shards, CAP, features)
    )
    outbound = outbound.reshape(members, CAP, features)
    partial_value = expert_rows(
        lax.all_to_all(outbound, "attn", split_axis=0, concat_axis=0, tiled=True),
        gate_weight,
        up_weight,
        down_weight,
    )
    returned = lax.all_to_all(partial_value, "attn", split_axis=0, concat_axis=0, tiled=True)
    grouped = returned.reshape((EXPERTS, shards) + returned.shape[1:]).astype(jnp.float32)
    expert_out = jnp.sum(grouped, axis=1).astype(jnp.bfloat16)
    combine_weight = route_factor * route_scores / jnp.sum(route_scores, axis=1, keepdims=True)
    token_count, picks = expert_ids.shape
    values = expert_out.reshape(EXPERTS * CAP, features)[place].astype(jnp.float32)
    values = values.reshape(token_count, picks, features)
    moe_output = jnp.sum(values * combine_weight[:, :, None], axis=1).astype(jnp.bfloat16)
    probs, finish = attention
    return moe_output, finish(probs)


def attend(q_latent, q_rope, latent_cache, rope_cache, cache_lengths):
    seq_count, step_count, _ = q_latent.shape
    cache_len = latent_cache.shape[1]
    latent_width = latent_cache.shape[2]
    rope_width = rope_cache.shape[2]
    head_count = q_latent.shape[2] // latent_width
    query_lat = q_latent.reshape(seq_count, step_count, head_count, latent_width)
    query_rot = q_rope.reshape(seq_count, step_count, head_count, rope_width)
    scores = jnp.einsum(
        "bthc,bpc->bthp", query_lat, latent_cache, preferred_element_type=jnp.float32
    )
    scores = scores + jnp.einsum(
        "bthc,bpc->bthp", query_rot, rope_cache, preferred_element_type=jnp.float32
    )
    scores = scores * score_factor
    position = jnp.arange(cache_len, dtype=jnp.int32)
    limit = cache_lengths[:, None] - step_count + jnp.arange(step_count, dtype=jnp.int32)[None, :]
    allowed = position[None, None, None, :] <= limit[:, :, None, None]
    scores = jnp.where(allowed, scores, -jnp.inf)
    largest = jnp.max(scores, axis=-1, keepdims=True)
    weights = jnp.exp(scores - largest)
    probs = (weights / jnp.sum(weights, axis=-1, keepdims=True)).astype(jnp.bfloat16)

    def finish(probs):
        attn = jnp.einsum("bthp,bpc->bthc", probs, latent_cache, preferred_element_type=jnp.float32)
        return attn.astype(jnp.bfloat16).reshape(seq_count, step_count, head_count * latent_width)

    return probs, finish


def body(
    moe_input,
    expert_ids,
    route_scores,
    gate_weight,
    up_weight,
    down_weight,
    q_latent,
    q_rope,
    latent_cache,
    rope_cache,
    cache_lengths,
):
    moe = moe_by_chips if lax.axis_size("attn") == 2 * EXPERTS else moe_by_slots
    attention = attend(q_latent, q_rope, latent_cache, rope_cache, cache_lengths)
    return moe(moe_input, expert_ids, route_scores, gate_weight, up_weight, down_weight, attention)


def solution(mesh):
    placed = (
        P(("rep", "attn"), None),
        P(("rep", "attn"), None),
        P(("rep", "attn"), None),
        P(None, "attn"),
        P(None, "attn"),
        P("attn", None),
        P(("rep", "attn"), None, None),
        P(("rep", "attn"), None, None),
        P(("rep", "attn"), None, None),
        P(("rep", "attn"), None, None),
        P(("rep", "attn")),
    )
    return jax.shard_map(
        body,
        mesh=mesh,
        in_specs=placed,
        out_specs=(P(("rep", "attn"), None), P(("rep", "attn"), None, None)),
        check_vma=False,
    )
```

time: 98 us -> 77.7 us (0.79)
  local copies, waits for them, and re-layouts: 19.4 us -> 10.8 us
  waiting for transfers between devices: 14 us -> 8.56 us
  Pallas kernels: 14.6 us -> 11 us
  starting transfers between devices: 38.9 us -> 37 us
    ppermute x14, waiting for transfers between devices: 13.5 us -> 3.93 us  [exchange(): lax.ppermute(sent[m], 'attn', [(i, i ^ 2 * m) for i in range(members)])]
    unnamed x44 -> x17, local copies, waits for them, and re-layouts: 9.62 us -> 1.83 us
    dot_general x2 -> x1, matrix products: 6.56 us -> 1.75 us  [finish(): jnp.einsum('bthp,bpc->bthc', probs, latent_cache, preferred_element_type=...]
    ppermute x16 -> x3, waiting for transfers between devices: 0.52 us -> 4.62 us  [sibling(): return lax.ppermute(value, 'attn', [(i, i ^ 1) for i in range(members)])]
    div x0 -> x1, matrix products: none -> 3.66 us  [attend(): weights / jnp.sum(weights, axis=-1, keepdims=True)]
    pallas_call x2 -> x3, Pallas kernels: 13 us -> 9.44 us  [the longest x1 8.46 us: experts(): pl.pallas_call(functools.partial(expert_kernel, len(groups)), out_shape=[...]
    ppermute x16 -> x3, starting transfers between devices: 3.78 us -> 0.77 us  [sibling(): return lax.ppermute(value, 'attn', [(i, i ^ 1) for i in range(members)])]
    convert_element_type x8 -> x0, other arithmetic: 1.17 us -> none  [moe_by_chips(): (a.astype(f32) + b.astype(f32)).astype(bf16)]
  transfers between devices with their start and end apart: 30 -> 17, of which waited for: 9 -> 7; matrix products, arithmetic and copies ran while one was open for 20% -> 23% of each run, Pallas kernels for 0% -> 0%
where the time goes in v2:
time: 77.7 us; the launch traced here: 77.3 us
  starting transfers between devices  37 us (48%)
  Pallas kernels  11 us (14%)
  local copies, waits for them, and re-layouts  10.8 us (14%)
  waiting for transfers between devices  8.56 us (11%)
  matrix products  7.82 us (10%)
  other arithmetic  1.28 us (2%)
    ppermute x14, starting transfers between devices, exchange(): lax.ppermute(sent[m], 'attn', [(i, i ^ 2 * m) for i in range(members)])  36.3 us
    pallas_call x1, Pallas kernels, experts(): pl.pallas_call(functools.partial(expert_kernel, len(groups)), out_shape=[...  8.46 us
    ppermute x3, waiting for transfers between devices, sibling(): return lax.ppermute(value, 'attn', [(i, i ^ 1) for i in range(members)])  4.62 us
    ppermute x14, waiting for transfers between devices, exchange(): lax.ppermute(sent[m], 'attn', [(i, i ^ 2 * m) for i in range(members)])  3.93 us
    reshape x1, local copies, waits for them, and re-layouts, finish(): attn.astype(jnp.bfloat16)  3.87 us
    reshape x1, local copies, waits for them, and re-layouts, attend(): q_latent.reshape(seq_count, step_count, head_count, latent_width)  3.83 us
    div x1, matrix products, attend(): weights / jnp.sum(weights, axis=-1, keepdims=True)  3.66 us
    dot_general x1, matrix products, attend(): jnp.einsum('bthc,bpc->bthp', query_rot, rope_cache, preferred_element_typ...  2.42 us
  transfers between devices with their start and end apart: 17, of which 7 were waited for; matrix products, arithmetic and copies ran while one was open for 23% of the time, Pallas kernels for 0%

profile of v2, /device:TPU:0, one launch (start us, length us, event | category | flops | bytes accessed | tf_op | source)
XLA Modules:
  0.0 77.3 jit_solution(11666847325227450545)
XLA Ops:
  3.2 4.0 %collective-permute-start = (bf16[8,8064]{1,0:T(8,128)(2,1)S(1)}, bf16[8,8064]{1,0:T(8,128)(2,1)S(1)}, u32[]{:S(2)}, u32[]{:S(2)}) collective-permute-start(bf16[8,8064]{1,0:T(8,128)(2,1)S(1)} %get-tuple-element.23), channel_id=1, source_target_pairs={{0,6},{1,7},{2,4},{3,5},{4,2},{5,3},{6,0},{7,1},{8,14},{9,15},{10,... | collective-permute-start | bytes 387080 | tf_op jit(solution)/shard_map/ppermute | solution.py:233
  7.2 2.6 %collective-permute-start.6 = (bf16[8,8064]{1,0:T(8,128)(2,1)S(1)}, bf16[8,8064]{1,0:T(8,128)(2,1)}, u32[]{:S(2)}, u32[]{:S(2)}) collective-permute-start(bf16[8,8064]{1,0:T(8,128)(2,1)S(1)} %get-tuple-element.29), channel_id=1, source_target_pairs={{0,8},{1,9},{2,10},{3,11},{4,12},{5,13},{6,14},{7,15},{8,0},{9,1},... | collective-permute-start | bytes 387080 | tf_op jit(solution)/shard_map/ppermute | solution.py:233
  10.1 2.5 %collective-permute-start.4 = (bf16[8,8064]{1,0:T(8,128)(2,1)S(1)}, bf16[8,8064]{1,0:T(8,128)(2,1)}, u32[]{:S(2)}, u32[]{:S(2)}) collective-permute-start(bf16[8,8064]{1,0:T(8,128)(2,1)S(1)} %get-tuple-element.27), channel_id=1, source_target_pairs={{0,12},{1,13},{2,14},{3,15},{4,8},{5,9},{6,10},{7,11},{8,4},{9,5},... | collective-permute-start | bytes 387080 | tf_op jit(solution)/shard_map/ppermute | solution.py:233
  12.6 2.3 %collective-permute-start.3 = (bf16[8,8064]{1,0:T(8,128)(2,1)S(1)}, bf16[8,8064]{1,0:T(8,128)(2,1)}, u32[]{:S(2)}, u32[]{:S(2)}) collective-permute-start(bf16[8,8064]{1,0:T(8,128)(2,1)S(1)} %get-tuple-element.26), channel_id=1, source_target_pairs={{0,14},{1,15},{2,12},{3,13},{4,10},{5,11},{6,8},{7,9},{8,6},{9,7},... | collective-permute-start | bytes 387080 | tf_op jit(solution)/shard_map/ppermute | solution.py:233
  14.9 1.3 %reshape.49 = bf16[6,4,64,64]{3,2,1,0:T(8,128)(2,1)S(1)} reshape(bf16[6,4,4096]{2,1,0:T(4,128)(2,1)} %param.18) | data formatting | bytes 393216 | tf_op jit(solution)/shard_map/reshape | solution.py:309
  16.2 3.8 %reshape.48 = bf16[6,4,64,512]{3,2,1,0:T(8,128)(2,1)} reshape(bf16[6,4,32768]{2,1,0:T(4,128)(2,1)} %param.17) | data formatting | bytes 3145728 | tf_op jit(solution)/shard_map/reshape | solution.py:308
  20.2 2.4 %fusion.11 = f32[6,4,64,256]{3,2,1,0:T(8,128)} fusion(bf16[6,4,64,64]{3,2,1,0:T(8,128)(2,1)S(1)} %reshape.49, bf16[6,256,64]{1,2,0:T(8,128)(2,1)} %param.20), kind=kOutput, calls=%fused_computation.12 | convolution fusion | flops 50331648 | bytes 1966080 | tf_op jit(solution)/shard_map/bthc,bpc->bthp/dot_general | solution.py:313
  22.6 3.7 %fusion.10 = bf16[6,4,64,256]{3,2,1,0:T(8,128)(2,1)} fusion(f32[6,4,64,256]{3,2,1,0:T(8,128)} %fusion.11, bf16[6,4,64,512]{3,2,1,0:T(8,128)(2,1)} %reshape.48, bf16[6,256,512]{2,1,0:T(8,128)(2,1)S(1)} %copy-done, pred[6,4,256]{2,1,0:T(4,128)(4,1)S(1)} %iota_compare_fusion), kind=kOutput, calls=%fused_computation.10 | convolution fusion | flops 405016064 | bytes 5511168 | tf_op jit(solution)/shard_map/div | solution.py:323
  27.4 2.1 %collective-permute-start.2 = (bf16[8,8064]{1,0:T(8,128)(2,1)S(1)}, bf16[8,8064]{1,0:T(8,128)(2,1)S(1)}, u32[]{:S(2)}, u32[]{:S(2)}) collective-permute-start(bf16[8,8064]{1,0:T(8,128)(2,1)S(1)} %get-tuple-element.25), channel_id=1, source_target_pairs={{0,2},{1,3},{2,0},{3,1},{4,6},{5,7},{6,4},{7,5},{8,10},{9,11},{10,... | collective-permute-start | bytes 387080 | tf_op jit(solution)/shard_map/ppermute | solution.py:233
  29.5 1.1 %pad_maximum_fusion.refs_1_ = bf16[32,8064]{1,0:T(8,128)(2,1)S(1)} fusion(bf16[8,8064]{1,0:T(8,128)(2,1)} %collective-permute-done.6, bf16[8,8064]{1,0:T(8,128)(2,1)} %collective-permute-done.5, bf16[8,8064]{1,0:T(8,128)(2,1)} %collective-permute-done.4, bf16[8,8064]{1,0:T(8,128)(2,1)} %collective-permute-done.3), kind=kLoop, calls=%fused_computation.11 | loop fusion | flops 2064384 | bytes 1032192 | tf_op jit(solution)/shard_map/concatenate | solution.py:239
  31.2 1.2 %collective-permute-done.2 = bf16[8,8064]{1,0:T(8,128)(2,1)S(1)} collective-permute-done((bf16[8,8064]{1,0:T(8,128)(2,1)S(1)}, bf16[8,8064]{1,0:T(8,128)(2,1)S(1)}, u32[]{:S(2)}, u32[]{:S(2)}) %collective-permute-start.2) | collective-permute-done | bytes 129056 | tf_op jit(solution)/shard_map/ppermute | solution.py:233
  33.0 1.4 %collective-permute-done.7.refs_2_ = bf16[32,8064]{1,0:T(8,128)(2,1)S(1)} collective-permute-done((bf16[32,8064]{1,0:T(8,128)(2,1)S(1)}, bf16[32,8064]{1,0:T(8,128)(2,1)S(1)}, u32[]{:S(2)}, u32[]{:S(2)}) %collective-permute-start.7) | collective-permute-done | bytes 516128 | tf_op jit(solution)/shard_map/ppermute | solution.py:228
  35.1 8.5 %experts.1 = (bf16[64,8064]{1,0:T(8,128)(2,1)S(1)}, bf16[64,8064]{1,0:T(8,128)(2,1)S(1)}) custom-call(bf16[32,8064]{1,0:T(8,128)(2,1)S(1)} %constant_dynamic-update-slice_fusion.refs_0_, bf16[32,8064]{1,0:T(8,128)(2,1)S(1)} %pad_maximum_fusion.refs_1_, bf16[32,8064]{1,0:T(8,128)(2,1)S(1)} %collective-permute-done.7.refs_2_, ...), custom_call_target="tpu_custom_call" | custom-call | flops 3170893824 | bytes 22020096 | tf_op jit(solution)/shard_map/experts/pallas_call | solution.py:137
  43.8 2.5 %collective-permute-done.9.b_ref = bf16[64,8064]{1,0:T(8,128)(2,1)S(1)} collective-permute-done((bf16[64,8064]{1,0:T(8,128)(2,1)S(1)}, bf16[64,8064]{1,0:T(8,128)(2,1)S(1)}, u32[]{:S(2)}, u32[]{:S(2)}) %collective-permute-start.9) | collective-permute-done | bytes 1032224 | tf_op jit(solution)/shard_map/ppermute | solution.py:228
  46.5 4.3 %collective-permute-start.10 = (bf16[8,8064]{1,0:T(8,128)(2,1)S(1)}, bf16[8,8064]{1,0:T(8,128)(2,1)S(1)}, u32[]{:S(2)}, u32[]{:S(2)}) collective-permute-start(bf16[8,8064]{1,0:T(8,128)(2,1)S(1)} %get-tuple-element.33), channel_id=1, source_target_pairs={{0,14},{1,15},{2,12},{3,13},{4,10},{5,11},{6,8},{7,9},{8,6},{9,7},... | collective-permute-start | bytes 387080 | tf_op jit(solution)/shard_map/ppermute | solution.py:233
  50.8 1.1 %collective-permute-start.11 = (bf16[8,8064]{1,0:T(8,128)(2,1)S(1)}, bf16[8,8064]{1,0:T(8,128)(2,1)S(1)}, u32[]{:S(2)}, u32[]{:S(2)}) collective-permute-start(bf16[8,8064]{1,0:T(8,128)(2,1)S(1)} %get-tuple-element.34), channel_id=1, source_target_pairs={{0,12},{1,13},{2,14},{3,15},{4,8},{5,9},{6,10},{7,11},{8,4},{9,5},... | collective-permute-start | bytes 387080 | tf_op jit(solution)/shard_map/ppermute | solution.py:233
  52.7 1.6 %collective-permute-start.13 = (bf16[8,8064]{1,0:T(8,128)(2,1)S(1)}, bf16[8,8064]{1,0:T(8,128)(2,1)S(1)}, u32[]{:S(2)}, u32[]{:S(2)}) collective-permute-start(bf16[8,8064]{1,0:T(8,128)(2,1)S(1)} %get-tuple-element.36), channel_id=1, source_target_pairs={{0,8},{1,9},{2,10},{3,11},{4,12},{5,13},{6,14},{7,15},{8,0},{9,1},... | collective-permute-start | bytes 387080 | tf_op jit(solution)/shard_map/ppermute | solution.py:233
  54.2 1.8 %collective-permute-start.14 = (bf16[8,8064]{1,0:T(8,128)(2,1)S(1)}, bf16[8,8064]{1,0:T(8,128)(2,1)S(1)}, u32[]{:S(2)}, u32[]{:S(2)}) collective-permute-start(bf16[8,8064]{1,0:T(8,128)(2,1)S(1)} %get-tuple-element.37), channel_id=1, source_target_pairs={{0,6},{1,7},{2,4},{3,5},{4,2},{5,3},{6,0},{7,1},{8,14},{9,15},{10,... | collective-permute-start | bytes 387080 | tf_op jit(solution)/shard_map/ppermute | solution.py:233
  56.1 11.3 %collective-permute-start.15 = (bf16[8,8064]{1,0:T(8,128)(2,1)S(1)}, bf16[8,8064]{1,0:T(8,128)(2,1)S(1)}, u32[]{:S(2)}, u32[]{:S(2)}) collective-permute-start(bf16[8,8064]{1,0:T(8,128)(2,1)S(1)} %get-tuple-element.38), channel_id=1, source_target_pairs={{0,4},{1,5},{2,6},{3,7},{4,0},{5,1},{6,2},{7,3},{8,12},{9,13},{10,... | collective-permute-start | bytes 387080 | tf_op jit(solution)/shard_map/ppermute | solution.py:233
  67.4 1.6 %collective-permute-start.16 = (bf16[8,8064]{1,0:T(8,128)(2,1)S(1)}, bf16[8,8064]{1,0:T(8,128)(2,1)S(1)}, u32[]{:S(2)}, u32[]{:S(2)}) collective-permute-start(bf16[8,8064]{1,0:T(8,128)(2,1)S(1)} %get-tuple-element.39), channel_id=1, source_target_pairs={{0,2},{1,3},{2,0},{3,1},{4,6},{5,7},{6,4},{7,5},{8,10},{9,11},{10,... | collective-permute-start | bytes 387080 | tf_op jit(solution)/shard_map/ppermute | solution.py:233
  69.0 1.7 %convolution_convert_fusion = bf16[6,4,64,512]{3,2,1,0:T(8,128)(2,1)} fusion(bf16[6,4,64,256]{3,2,1,0:T(8,128)(2,1)S(1)} %copy-done.5, bf16[6,256,512]{2,1,0:T(8,128)(2,1)S(1)} %copy-done), kind=kOutput, calls=%fused_computation.4 | convolution fusion | flops 403439616 | bytes 3932160 | tf_op jit(solution)/shard_map/bthp,bpc->bthc/dot_general | solution.py:326
  70.7 3.9 %reshape.50 = bf16[6,4,32768]{2,1,0:T(4,128)(2,1)} reshape(bf16[6,4,64,512]{3,2,1,0:T(8,128)(2,1)} %convolution_convert_fusion) | data formatting | bytes 3145728 | tf_op jit(solution)/shard_map/reshape | solution.py:327
  74.6 1.1 %collective-permute-done.15.refs_5_ = bf16[8,8064]{1,0:T(8,128)(2,1)S(1)} collective-permute-done((bf16[8,8064]{1,0:T(8,128)(2,1)S(1)}, bf16[8,8064]{1,0:T(8,128)(2,1)S(1)}, u32[]{:S(2)}, u32[]{:S(2)}) %collective-permute-start.15) | collective-permute-done | bytes 129056 | tf_op jit(solution)/shard_map/ppermute | solution.py:233
  75.7 1.6 %combine.1 = bf16[24,7168]{1,0:T(8,128)(2,1)} custom-call(s32[1]{0:T(128)} %bitcast.chip_ref, s32[2,24]{1,0:T(2,128)S(1)} %bitcast.27, f32[2,24]{1,0:T(2,128)S(1)} %bitcast.28, bf16[8,8064]{1,0:T(8,128)(2,1)S(1)} %collective-permute-done.10.refs_0_, bf16[8,8064]{1,0:T(8,128)(2,1)S(1)} %collective-permute-done.11.refs_1_, ...), custom_call_target="tpu_custom_call" | custom-call | tf_op jit(solution)/shard_map/combine/pallas_call | solution.py:202
  (42 shorter events, 7.2 us)
Async XLA Ops:
  0.6 22.0 %copy-start = (bf16[6,256,512]{2,1,0:T(8,128)(2,1)S(1)}, bf16[6,256,512]{2,1,0:T(8,128)(2,1)}, u32[]{:S(2)}) copy-start(bf16[6,256,512]{2,1,0:T(8,128)(2,1)} %param.19) | copy-start | bytes 4718596
  0.7 1.1 %copy-start.1 = (bf16[24,7168]{1,0:T(8,128)(2,1)S(1)}, bf16[24,7168]{1,0:T(8,128)(2,1)}, u32[]{:S(2)}) copy-start(bf16[24,7168]{1,0:T(8,128)(2,1)} %x_ref.1) | copy-start | bytes 1032196
  1.8 0.7 copy-start.2
  3.2 27.4 %collective-permute-start = (bf16[8,8064]{1,0:T(8,128)(2,1)S(1)}, bf16[8,8064]{1,0:T(8,128)(2,1)S(1)}, u32[]{:S(2)}, u32[]{:S(2)}) collective-permute-start(bf16[8,8064]{1,0:T(8,128)(2,1)S(1)} %get-tuple-element.23), channel_id=1, source_target_pairs={{0,6},{1,7},{2,4},{3,5},{4,2},{5,3},{6,0},{7,1},{8,14},{9,15},{10,... | collective-permute-start | bytes 387080 | tf_op jit(solution)/shard_map/ppermute | solution.py:233
  7.2 19.0 %collective-permute-start.6 = (bf16[8,8064]{1,0:T(8,128)(2,1)S(1)}, bf16[8,8064]{1,0:T(8,128)(2,1)}, u32[]{:S(2)}, u32[]{:S(2)}) collective-permute-start(bf16[8,8064]{1,0:T(8,128)(2,1)S(1)} %get-tuple-element.29), channel_id=1, source_target_pairs={{0,8},{1,9},{2,10},{3,11},{4,12},{5,13},{6,14},{7,15},{8,0},{9,1},... | collective-permute-start | bytes 387080 | tf_op jit(solution)/shard_map/ppermute | solution.py:233
  9.8 17.5 %collective-permute-start.5 = (bf16[8,8064]{1,0:T(8,128)(2,1)S(1)}, bf16[8,8064]{1,0:T(8,128)(2,1)}, u32[]{:S(2)}, u32[]{:S(2)}) collective-permute-start(bf16[8,8064]{1,0:T(8,128)(2,1)S(1)} %get-tuple-element.28), channel_id=1, source_target_pairs={{0,10},{1,11},{2,8},{3,9},{4,14},{5,15},{6,12},{7,13},{8,2},{9,3},... | collective-permute-start | bytes 387080 | tf_op jit(solution)/shard_map/ppermute | solution.py:233
  10.1 19.4 %collective-permute-start.4 = (bf16[8,8064]{1,0:T(8,128)(2,1)S(1)}, bf16[8,8064]{1,0:T(8,128)(2,1)}, u32[]{:S(2)}, u32[]{:S(2)}) collective-permute-start(bf16[8,8064]{1,0:T(8,128)(2,1)S(1)} %get-tuple-element.27), channel_id=1, source_target_pairs={{0,12},{1,13},{2,14},{3,15},{4,8},{5,9},{6,10},{7,11},{8,4},{9,5},... | collective-permute-start | bytes 387080 | tf_op jit(solution)/shard_map/ppermute | solution.py:233
  12.6 16.9 %collective-permute-start.3 = (bf16[8,8064]{1,0:T(8,128)(2,1)S(1)}, bf16[8,8064]{1,0:T(8,128)(2,1)}, u32[]{:S(2)}, u32[]{:S(2)}) collective-permute-start(bf16[8,8064]{1,0:T(8,128)(2,1)S(1)} %get-tuple-element.26), channel_id=1, source_target_pairs={{0,14},{1,15},{2,12},{3,13},{4,10},{5,11},{6,8},{7,9},{8,6},{9,7},... | collective-permute-start | bytes 387080 | tf_op jit(solution)/shard_map/ppermute | solution.py:233
  16.2 3.8 %copy-start.6 = (s32[6]{0:T(128)S(1)}, s32[6]{0:T(128)}, u32[]{:S(2)}) copy-start(s32[6]{0:T(128)} %param.21) | copy-start | bytes 76
  26.3 4.9 %collective-permute-start.1 = (bf16[8,8064]{1,0:T(8,128)(2,1)S(1)}, bf16[8,8064]{1,0:T(8,128)(2,1)S(1)}, u32[]{:S(2)}, u32[]{:S(2)}) collective-permute-start(bf16[8,8064]{1,0:T(8,128)(2,1)S(1)} %get-tuple-element.24), channel_id=1, source_target_pairs={{0,4},{1,5},{2,6},{3,7},{4,0},{5,1},{6,2},{7,3},{8,12},{9,13},{10,... | collective-permute-start | bytes 387080 | tf_op jit(solution)/shard_map/ppermute | solution.py:233
  27.4 5.0 %collective-permute-start.2 = (bf16[8,8064]{1,0:T(8,128)(2,1)S(1)}, bf16[8,8064]{1,0:T(8,128)(2,1)S(1)}, u32[]{:S(2)}, u32[]{:S(2)}) collective-permute-start(bf16[8,8064]{1,0:T(8,128)(2,1)S(1)} %get-tuple-element.25), channel_id=1, source_target_pairs={{0,2},{1,3},{2,0},{3,1},{4,6},{5,7},{6,4},{7,5},{8,10},{9,11},{10,... | collective-permute-start | bytes 387080 | tf_op jit(solution)/shard_map/ppermute | solution.py:233
  32.4 2.0 %collective-permute-start.7 = (bf16[32,8064]{1,0:T(8,128)(2,1)S(1)}, bf16[32,8064]{1,0:T(8,128)(2,1)S(1)}, u32[]{:S(2)}, u32[]{:S(2)}) collective-permute-start(bf16[32,8064]{1,0:T(8,128)(2,1)S(1)} %constant_dynamic-update-slice_fusion.refs_0_), channel_id=1, source_target_pairs={{0,1},{1,0},{2,3},{3,2},{4,5},{5,4},{6,7},{7,6},{8,9},{9,8},{10,11... | collective-permute-start | bytes 1548296 | tf_op jit(solution)/shard_map/ppermute | solution.py:228
  32.5 2.6 %collective-permute-start.8 = (bf16[32,8064]{1,0:T(8,128)(2,1)S(1)}, bf16[32,8064]{1,0:T(8,128)(2,1)S(1)}, u32[]{:S(2)}, u32[]{:S(2)}) collective-permute-start(bf16[32,8064]{1,0:T(8,128)(2,1)S(1)} %pad_maximum_fusion.refs_1_), channel_id=1, source_target_pairs={{0,1},{1,0},{2,3},{3,2},{4,5},{5,4},{6,7},{7,6},{8,9},{9,8},{10,11... | collective-permute-start | bytes 1548296 | tf_op jit(solution)/shard_map/ppermute | solution.py:228
  43.6 25.4 %copy-start.5 = (bf16[6,4,64,256]{3,2,1,0:T(8,128)(2,1)S(1)}, bf16[6,4,64,256]{3,2,1,0:T(8,128)(2,1)}, u32[]{:S(2)}) copy-start(bf16[6,4,64,256]{3,2,1,0:T(8,128)(2,1)} %fusion.10) | copy-start | bytes 2359300
  43.6 2.7 %collective-permute-start.9 = (bf16[64,8064]{1,0:T(8,128)(2,1)S(1)}, bf16[64,8064]{1,0:T(8,128)(2,1)S(1)}, u32[]{:S(2)}, u32[]{:S(2)}) collective-permute-start(bf16[64,8064]{1,0:T(8,128)(2,1)S(1)} %get-tuple-element.32), channel_id=1, source_target_pairs={{0,1},{1,0},{2,3},{3,2},{4,5},{5,4},{6,7},{7,6},{8,9},{9,8},{10,11... | collective-permute-start | bytes 3096584 | tf_op jit(solution)/shard_map/ppermute | solution.py:228
  46.5 9.5 %collective-permute-start.10 = (bf16[8,8064]{1,0:T(8,128)(2,1)S(1)}, bf16[8,8064]{1,0:T(8,128)(2,1)S(1)}, u32[]{:S(2)}, u32[]{:S(2)}) collective-permute-start(bf16[8,8064]{1,0:T(8,128)(2,1)S(1)} %get-tuple-element.33), channel_id=1, source_target_pairs={{0,14},{1,15},{2,12},{3,13},{4,10},{5,11},{6,8},{7,9},{8,6},{9,7},... | collective-permute-start | bytes 387080 | tf_op jit(solution)/shard_map/ppermute | solution.py:233
  50.8 16.6 %collective-permute-start.11 = (bf16[8,8064]{1,0:T(8,128)(2,1)S(1)}, bf16[8,8064]{1,0:T(8,128)(2,1)S(1)}, u32[]{:S(2)}, u32[]{:S(2)}) collective-permute-start(bf16[8,8064]{1,0:T(8,128)(2,1)S(1)} %get-tuple-element.34), channel_id=1, source_target_pairs={{0,12},{1,13},{2,14},{3,15},{4,8},{5,9},{6,10},{7,11},{8,4},{9,5},... | collective-permute-start | bytes 387080 | tf_op jit(solution)/shard_map/ppermute | solution.py:233
  51.9 22.7 %collective-permute-start.12 = (bf16[8,8064]{1,0:T(8,128)(2,1)S(1)}, bf16[8,8064]{1,0:T(8,128)(2,1)S(1)}, u32[]{:S(2)}, u32[]{:S(2)}) collective-permute-start(bf16[8,8064]{1,0:T(8,128)(2,1)S(1)} %get-tuple-element.35), channel_id=1, source_target_pairs={{0,10},{1,11},{2,8},{3,9},{4,14},{5,15},{6,12},{7,13},{8,2},{9,3},... | collective-permute-start | bytes 387080 | tf_op jit(solution)/shard_map/ppermute | solution.py:233
  52.7 22.0 %collective-permute-start.13 = (bf16[8,8064]{1,0:T(8,128)(2,1)S(1)}, bf16[8,8064]{1,0:T(8,128)(2,1)S(1)}, u32[]{:S(2)}, u32[]{:S(2)}) collective-permute-start(bf16[8,8064]{1,0:T(8,128)(2,1)S(1)} %get-tuple-element.36), channel_id=1, source_target_pairs={{0,8},{1,9},{2,10},{3,11},{4,12},{5,13},{6,14},{7,15},{8,0},{9,1},... | collective-permute-start | bytes 387080 | tf_op jit(solution)/shard_map/ppermute | solution.py:233
  54.2 20.4 %collective-permute-start.14 = (bf16[8,8064]{1,0:T(8,128)(2,1)S(1)}, bf16[8,8064]{1,0:T(8,128)(2,1)S(1)}, u32[]{:S(2)}, u32[]{:S(2)}) collective-permute-start(bf16[8,8064]{1,0:T(8,128)(2,1)S(1)} %get-tuple-element.37), channel_id=1, source_target_pairs={{0,6},{1,7},{2,4},{3,5},{4,2},{5,3},{6,0},{7,1},{8,14},{9,15},{10,... | collective-permute-start | bytes 387080 | tf_op jit(solution)/shard_map/ppermute | solution.py:233
  56.1 19.6 %collective-permute-start.15 = (bf16[8,8064]{1,0:T(8,128)(2,1)S(1)}, bf16[8,8064]{1,0:T(8,128)(2,1)S(1)}, u32[]{:S(2)}, u32[]{:S(2)}) collective-permute-start(bf16[8,8064]{1,0:T(8,128)(2,1)S(1)} %get-tuple-element.38), channel_id=1, source_target_pairs={{0,4},{1,5},{2,6},{3,7},{4,0},{5,1},{6,2},{7,3},{8,12},{9,13},{10,... | collective-permute-start | bytes 387080 | tf_op jit(solution)/shard_map/ppermute | solution.py:233
  67.4 8.3 %collective-permute-start.16 = (bf16[8,8064]{1,0:T(8,128)(2,1)S(1)}, bf16[8,8064]{1,0:T(8,128)(2,1)S(1)}, u32[]{:S(2)}, u32[]{:S(2)}) collective-permute-start(bf16[8,8064]{1,0:T(8,128)(2,1)S(1)} %get-tuple-element.39), channel_id=1, source_target_pairs={{0,2},{1,3},{2,0},{3,1},{4,6},{5,7},{6,4},{7,5},{8,10},{9,11},{10,... | collective-permute-start | bytes 387080 | tf_op jit(solution)/shard_map/ppermute | solution.py:233
  70.7 5.0 %copy-start.3 = (s32[24,2]{0,1:T(2,128)S(1)}, s32[24,2]{0,1:T(2,128)}, u32[]{:S(2)}) copy-start(s32[24,2]{0,1:T(2,128)} %param.12) | copy-start | bytes 580
  70.7 5.0 %copy-start.4 = (f32[24,2]{0,1:T(2,128)S(1)}, f32[24,2]{0,1:T(2,128)}, u32[]{:S(2)}) copy-start(f32[24,2]{0,1:T(2,128)} %param.13) | copy-start | bytes 580

commit v3 on v2

--- a/solution.py
+++ b/solution.py
@@ -12,7 +12,10 @@
 SUB = 8
 FOLD = SUB // 2
 MIB = 1 << 20
-ORDER = (7, 6, 5, 4, 3, 2, 1)
+ORDER = (7, 6, 5, 1, 2, 4, 3)
+GROUPED = (7, 6, 5, 4, 0, 1, 2, 3)
+BACK = (7, 6, 5, 4, 3, 2, 1, 0)
+HBM = pl.BlockSpec(memory_space=pltpu.HBM)
 VMEM = pl.BlockSpec(memory_space=pltpu.VMEM)
 
 score_factor = 192.0 ** (-0.5)
@@ -47,7 +50,18 @@
     return jnp.where(mask, 1.0, jnp.zeros(mask.shape, f32)).astype(bf16)
 
 
-def pack_kernel(chip_ref, ids_ref, x_ref, *outs):
+def in_hbm(value):
+    return pltpu.with_memory_space_constraint(value, pltpu.HBM)
+
+
+def pack_kernel(chip_ref, ids_hbm, x_hbm, *refs):
+    outs, (ids_ref, x_ref, sems) = refs[:EXPERTS], refs[EXPERTS:]
+    ids_copy = pltpu.make_async_copy(ids_hbm, ids_ref, sems.at[0])
+    x_copy = pltpu.make_async_copy(x_hbm, x_ref, sems.at[1])
+    ids_copy.start()
+    x_copy.start()
+    ids_copy.wait()
+    x_copy.wait()
     features = x_ref.shape[1]
     tail = features // SUB
     hit, slot, _, q = routing(ids_ref[...], chip_ref[0])
@@ -66,11 +80,16 @@
     return pl.pallas_call(
         pack_kernel,
         out_shape=[jax.ShapeDtypeStruct((SUB, features + features // SUB), bf16)] * EXPERTS,
-        in_specs=[pl.BlockSpec(memory_space=pltpu.SMEM)] + [VMEM] * 2,
+        in_specs=[pl.BlockSpec(memory_space=pltpu.SMEM)] + [HBM] * 2,
         out_specs=[VMEM] * EXPERTS,
+        scratch_shapes=[
+            pltpu.VMEM(ids.shape, ids.dtype),
+            pltpu.VMEM(x.shape, x.dtype),
+            pltpu.SemaphoreType.DMA((2,)),
+        ],
         compiler_params=pltpu.CompilerParams(vmem_limit_bytes=12 * MIB),
         name="pack",
-    )(chip, ids, x)
+    )(chip, in_hbm(ids), in_hbm(x))
 
 
 def spread(i, count):
@@ -137,7 +156,7 @@
     return pl.pallas_call(
         functools.partial(expert_kernel, len(groups)),
         out_shape=[jax.ShapeDtypeStruct((top // 2, wide), bf16)] * 2,
-        in_specs=[VMEM] * len(groups) + [pl.BlockSpec(memory_space=pltpu.HBM)] * 3,
+        in_specs=[VMEM] * len(groups) + [HBM] * 3,
         out_specs=[VMEM] * 2,
         scratch_shapes=[
             pltpu.VMEM(gate_weight.shape, bf16),
@@ -181,7 +200,7 @@
     scores = scores_ref[...]
     weight = route_factor * scores / (scores[0:1, :] + scores[1:2, :])
     weight = jnp.where(first, weight[0:1, :], weight[1:2, :])
-    for m, ref in zip(ORDER + (0,), ins):
+    for m, ref in zip(BACK, ins):
         rows_ref[m * SUB:(m + 1) * SUB, :] = ref[...]
 
     def weighted(mask, values):
@@ -219,30 +238,30 @@
     members = lax.axis_size("attn")
     chip = (lax.axis_index("attn") // 2).astype(jnp.int32).reshape(1)
     ids, scores = expert_ids.T, route_scores.T
-    weights = [
-        pltpu.with_memory_space_constraint(w, pltpu.HBM) for w in (gate_weight, up_weight, down_weight)
-    ]
-    probs, finish = attention
+    weights = [in_hbm(w) for w in (gate_weight, up_weight, down_weight)]
+    scores_of, soften, finish = attention
 
     def sibling(value):
         return lax.ppermute(value, "attn", [(i, i ^ 1) for i in range(members)])
 
-    def exchange(sent):
+    def exchange(sent, *first):
         got = {0: sent[0]}
         for m in ORDER:
-            got[m] = lax.ppermute(sent[m], "attn", [(i, i ^ (2 * m)) for i in range(members)])
+            value = after(sent[m], got[5 - m], *first) if m in (4, 3) else sent[m]
+            got[m] = lax.ppermute(value, "attn", [(i, i ^ (2 * m)) for i in range(members)])
         return got
 
     got = exchange(pack(chip, ids, moe_input))
-    order = (0,) + ORDER[FOLD:] + ORDER[:FOLD]
+    order = GROUPED
     first = jnp.concatenate([got[m] for m in order[:FOLD]], axis=0)
     second = jnp.concatenate([got[m] for m in order[FOLD:]], axis=0)
+    probs = soften(after(scores_of, got[1]))
     second = after(second, probs)
     mine, theirs = experts([first, second, sibling(first), sibling(second)], *weights)
     total = add(mine, sibling(theirs))
     attn_output = finish(after(probs, *total))
-    back = exchange({m: total[place] for place, m in enumerate(order)})
-    moe_output = combine(chip, ids, scores, [back[m] for m in ORDER + (0,)], features)
+    back = exchange({m: total[place] for place, m in enumerate(order)}, attn_output)
+    moe_output = combine(chip, ids, scores, [back[m] for m in BACK], features)
     return moe_output, attn_output
 
 
@@ -295,8 +314,8 @@
     values = expert_out.reshape(EXPERTS * CAP, features)[place].astype(jnp.float32)
     values = values.reshape(token_count, picks, features)
     moe_output = jnp.sum(values * combine_weight[:, :, None], axis=1).astype(jnp.bfloat16)
-    probs, finish = attention
-    return moe_output, finish(probs)
+    scores_of, soften, finish = attention
+    return moe_output, finish(soften(scores_of))
 
 
 def attend(q_latent, q_rope, latent_cache, rope_cache, cache_lengths):
@@ -313,20 +332,22 @@
     scores = scores + jnp.einsum(
         "bthc,bpc->bthp", query_rot, rope_cache, preferred_element_type=jnp.float32
     )
-    scores = scores * score_factor
-    position = jnp.arange(cache_len, dtype=jnp.int32)
-    limit = cache_lengths[:, None] - step_count + jnp.arange(step_count, dtype=jnp.int32)[None, :]
-    allowed = position[None, None, None, :] <= limit[:, :, None, None]
-    scores = jnp.where(allowed, scores, -jnp.inf)
-    largest = jnp.max(scores, axis=-1, keepdims=True)
-    weights = jnp.exp(scores - largest)
-    probs = (weights / jnp.sum(weights, axis=-1, keepdims=True)).astype(jnp.bfloat16)
+
+    def soften(scores):
+        scores = scores * score_factor
+        position = jnp.arange(cache_len, dtype=jnp.int32)
+        limit = cache_lengths[:, None] - step_count + jnp.arange(step_count, dtype=jnp.int32)[None, :]
+        allowed = position[None, None, None, :] <= limit[:, :, None, None]
+        scores = jnp.where(allowed, scores, -jnp.inf)
+        largest = jnp.max(scores, axis=-1, keepdims=True)
+        weights = jnp.exp(scores - largest)
+        return (weights / jnp.sum(weights, axis=-1, keepdims=True)).astype(jnp.bfloat16)
 
     def finish(probs):
         attn = jnp.einsum("bthp,bpc->bthc", probs, latent_cache, preferred_element_type=jnp.float32)
         return attn.astype(jnp.bfloat16).reshape(seq_count, step_count, head_count * latent_width)
 
-    return probs, finish
+    return scores, soften, finish
 
 
 def body(

time: 77.7 us -> 72.8 us (0.937)
  starting transfers between devices: 37 us -> 26 us
  waiting for transfers between devices: 8.56 us -> 13.8 us
  matrix products: 7.82 us -> 3.84 us
  other arithmetic: 1.28 us -> 4.73 us
  Pallas kernels: 11 us -> 12.2 us
    ppermute x14, starting transfers between devices: 36.3 us -> 25.3 us  [exchange(): lax.ppermute(value, 'attn', [(i, i ^ 2 * m) for i in range(members)])]
    ppermute x14, waiting for transfers between devices: 3.93 us -> 9.73 us  [exchange(): lax.ppermute(value, 'attn', [(i, i ^ 2 * m) for i in range(members)])]
    div x1 -> x0, matrix products: 3.66 us -> none  [attend(): weights / jnp.sum(weights, axis=-1, keepdims=True)]
    div x0 -> x1, other arithmetic: none -> 2.92 us  [soften(): weights / jnp.sum(weights, axis=-1, keepdims=True)]
    dot_general x1, matrix products: 2.42 us -> 0.34 us  [attend(): jnp.einsum('bthc,bpc->bthp', query_rot, rope_cache, preferred_element_typ...]
    dot_general x0 -> x1, matrix products: none -> 1.75 us  [attend(): jnp.einsum('bthc,bpc->bthp', query_lat, latent_cache, preferred_element_t...]
    pallas_call x1, Pallas kernels: 0.74 us -> 1.88 us  [pack(): pl.pallas_call(pack_kernel, out_shape=[jax.ShapeDtypeStruct((SUB, feature...]
    unnamed x17 -> x15, local copies, waits for them, and re-layouts: 1.83 us -> 2.03 us
  transfers between devices with their start and end apart: 17 -> 17, of which waited for: 7 -> 9; matrix products, arithmetic and copies ran while one was open for 23% -> 26% of each run, Pallas kernels for 0% -> 0%
where the time goes in v3:
time: 72.8 us; the launch traced here: 72.4 us
  starting transfers between devices  26 us (36%)
  waiting for transfers between devices  13.8 us (19%)
  Pallas kernels  12.2 us (17%)
  local copies, waits for them, and re-layouts  11.1 us (15%)
  other arithmetic  4.73 us (6%)
  matrix products  3.84 us (5%)
  between operations  0.79 us (1%)
    ppermute x14, starting transfers between devices, exchange(): lax.ppermute(value, 'attn', [(i, i ^ 2 * m) for i in range(members)])  25.3 us
    ppermute x14, waiting for transfers between devices, exchange(): lax.ppermute(value, 'attn', [(i, i ^ 2 * m) for i in range(members)])  9.73 us
    pallas_call x1, Pallas kernels, experts(): pl.pallas_call(functools.partial(expert_kernel, len(groups)), out_shape=[...  8.46 us
    ppermute x3, waiting for transfers between devices, sibling(): return lax.ppermute(value, 'attn', [(i, i ^ 1) for i in range(members)])  4.11 us
    reshape x1, local copies, waits for them, and re-layouts, finish(): attn.astype(jnp.bfloat16)  3.87 us
    reshape x1, local copies, waits for them, and re-layouts, attend(): q_latent.reshape(seq_count, step_count, head_count, latent_width)  3.86 us
    div x1, other arithmetic, soften(): weights / jnp.sum(weights, axis=-1, keepdims=True)  2.92 us
    unnamed x15, local copies, waits for them, and re-layouts  2.03 us
  transfers between devices with their start and end apart: 17, of which 9 were waited for; matrix products, arithmetic and copies ran while one was open for 26% of the time, Pallas kernels for 0%

profile of v3, /device:TPU:0, one launch (start us, length us, event | category | flops | bytes accessed | tf_op | source)
XLA Modules:
  0.0 72.4 jit_solution(6109695977423406791)
XLA Ops:
  0.7 1.9 %pack.1 = (bf16[8,8064]{1,0:T(8,128)(2,1)S(1)}, bf16[8,8064]{1,0:T(8,128)(2,1)S(1)}, bf16[8,8064]{1,0:T(8,128)(2,1)S(1)}, bf16[8,8064]{1,0:T(8,128)(2,1)S(1)}, b...) custom-call(s32[1]{0:T(128)} %bitcast.chip_ref, ...), custom_call_target="tpu_custom_call" | custom-call | tf_op jit(solution)/shard_map/pack/pallas_call | solution.py:80
  2.5 6.1 %collective-permute-start = (bf16[8,8064]{1,0:T(8,128)(2,1)S(1)}, bf16[8,8064]{1,0:T(8,128)(2,1)}, u32[]{:S(2)}, u32[]{:S(2)}) collective-permute-start(bf16[8,8064]{1,0:T(8,128)(2,1)S(1)} %get-tuple-element.27), channel_id=1, source_target_pairs={{0,14},{1,15},{2,12},{3,13},{4,10},{5,11},{6,8},{7,9},{8,6},{9,7},... | collective-permute-start | bytes 387080 | tf_op jit(solution)/shard_map/ppermute | solution.py:251
  9.6 1.5 %collective-permute-start.3 = (bf16[8,8064]{1,0:T(8,128)(2,1)S(1)}, bf16[8,8064]{1,0:T(8,128)(2,1)}, u32[]{:S(2)}, u32[]{:S(2)}) collective-permute-start(bf16[8,8064]{1,0:T(8,128)(2,1)S(1)} %get-tuple-element.31), channel_id=1, source_target_pairs={{0,2},{1,3},{2,0},{3,1},{4,6},{5,7},{6,4},{7,5},{8,10},{9,11},{10,... | collective-permute-start | bytes 387080 | tf_op jit(solution)/shard_map/ppermute | solution.py:251
  11.1 3.4 %collective-permute-start.5 = (bf16[8,8064]{1,0:T(8,128)(2,1)S(1)}, bf16[8,8064]{1,0:T(8,128)(2,1)}, u32[]{:S(2)}, u32[]{:S(2)}) collective-permute-start(bf16[8,8064]{1,0:T(8,128)(2,1)S(1)} %get-tuple-element.34), channel_id=1, source_target_pairs={{0,4},{1,5},{2,6},{3,7},{4,0},{5,1},{6,2},{7,3},{8,12},{9,13},{10,... | collective-permute-start | bytes 387080 | tf_op jit(solution)/shard_map/ppermute | solution.py:251
  15.2 1.3 %reshape.49 = bf16[6,4,64,64]{3,2,1,0:T(8,128)(2,1)S(1)} reshape(bf16[6,4,4096]{2,1,0:T(4,128)(2,1)} %param.18) | data formatting | bytes 393216 | tf_op jit(solution)/shard_map/reshape | solution.py:328
  16.5 3.9 %reshape.48 = bf16[6,4,64,512]{3,2,1,0:T(8,128)(2,1)} reshape(bf16[6,4,32768]{2,1,0:T(4,128)(2,1)} %param.17) | data formatting | bytes 3145728 | tf_op jit(solution)/shard_map/reshape | solution.py:327
  20.7 1.1 %copy-done.3 = bf16[6,4,64,512]{3,2,1,0:T(8,128)(2,1)S(1)} copy-done((bf16[6,4,64,512]{3,2,1,0:T(8,128)(2,1)S(1)}, bf16[6,4,64,512]{3,2,1,0:T(8,128)(2,1)}, u32[]{:S(2)}) %copy-start.3) | copy-done | bytes 1572888
  21.8 1.7 %fusion.8 = f32[6,4,64,256]{3,2,1,0:T(8,128)} fusion(f32[6,4,64,256]{3,2,1,0:T(8,128)S(1)} %fusion.16, bf16[6,4,64,512]{3,2,1,0:T(8,128)(2,1)S(1)} %copy-done.3, bf16[6,256,512]{2,1,0:T(8,128)(2,1)S(1)} %copy-done), kind=kOutput, calls=%fused_computation.10 | convolution fusion | flops 403046400 | bytes 6291456 | tf_op jit(solution)/shard_map/bthc,bpc->bthp/dot_general | solution.py:329
  24.3 0.9 %constant_dynamic-update-slice_fusion.3 = bf16[32,8064]{1,0:T(8,128)(2,1)S(1)} fusion(bf16[8,8064]{1,0:T(8,128)(2,1)} %collective-permute-done), kind=kLoop, calls=%fused_computation.23 | loop fusion | bytes 258048
  25.3 2.9 %fusion.11 = bf16[6,4,64,256]{3,2,1,0:T(8,128)(2,1)} fusion(f32[6,4,64,256]{3,2,1,0:T(8,128)} %fusion.8, pred[6,4,256]{2,1,0:T(4,128)(4,1)S(1)} %iota_compare_fusion), kind=kOutput, calls=%fused_computation.11 | output fusion | flops 1969662 | bytes 2365440 | tf_op jit(solution)/shard_map/div | solution.py:344
  28.2 2.6 %collective-permute-done.4 = bf16[8,8064]{1,0:T(8,128)(2,1)S(1)} collective-permute-done((bf16[8,8064]{1,0:T(8,128)(2,1)S(1)}, bf16[8,8064]{1,0:T(8,128)(2,1)S(1)}, u32[]{:S(2)}, u32[]{:S(2)}) %collective-permute-start.4) | collective-permute-done | bytes 129056 | tf_op jit(solution)/shard_map/ppermute | solution.py:251
  31.2 1.0 %pad_maximum_fusion.refs_1_ = bf16[32,8064]{1,0:T(8,128)(2,1)S(1)} fusion(bf16[8,8064]{1,0:T(8,128)(2,1)S(1)} %collective-permute-done.6, bf16[8,8064]{1,0:T(8,128)(2,1)} %collective-permute-done.5, bf16[8,8064]{1,0:T(8,128)(2,1)} %collective-permute-done.3, bf16[8,8064]{1,0:T(8,128)(2,1)S(1)} %get-tuple-element.33), kind=kLoop, calls=%fused_computation.16 | loop fusion | flops 2064384 | bytes 1032192 | tf_op jit(solution)/shard_map/concatenate | solution.py:257
  32.8 1.4 %collective-permute-done.8.refs_3_ = bf16[32,8064]{1,0:T(8,128)(2,1)S(1)} collective-permute-done((bf16[32,8064]{1,0:T(8,128)(2,1)S(1)}, bf16[32,8064]{1,0:T(8,128)(2,1)S(1)}, u32[]{:S(2)}, u32[]{:S(2)}) %collective-permute-start.8) | collective-permute-done | bytes 516128 | tf_op jit(solution)/shard_map/ppermute | solution.py:245
  34.2 8.5 %experts.1 = (bf16[64,8064]{1,0:T(8,128)(2,1)S(1)}, bf16[64,8064]{1,0:T(8,128)(2,1)S(1)}) custom-call(bf16[32,8064]{1,0:T(8,128)(2,1)S(1)} %constant_dynamic-update-slice_fusion.refs_0_, bf16[32,8064]{1,0:T(8,128)(2,1)S(1)} %pad_maximum_fusion.refs_1_, bf16[32,8064]{1,0:T(8,128)(2,1)S(1)} %collective-permute-done.7.refs_2_, ...), custom_call_target="tpu_custom_call" | custom-call | flops 3170893824 | bytes 22020096 | tf_op jit(solution)/shard_map/experts/pallas_call | solution.py:156
  43.0 2.4 %collective-permute-done.9.b_ref = bf16[64,8064]{1,0:T(8,128)(2,1)S(1)} collective-permute-done((bf16[64,8064]{1,0:T(8,128)(2,1)S(1)}, bf16[64,8064]{1,0:T(8,128)(2,1)S(1)}, u32[]{:S(2)}, u32[]{:S(2)}) %collective-permute-start.9) | collective-permute-done | bytes 1032224 | tf_op jit(solution)/shard_map/ppermute | solution.py:245
  45.6 4.4 %collective-permute-start.10 = (bf16[8,8064]{1,0:T(8,128)(2,1)S(1)}, bf16[8,8064]{1,0:T(8,128)(2,1)S(1)}, u32[]{:S(2)}, u32[]{:S(2)}) collective-permute-start(bf16[8,8064]{1,0:T(8,128)(2,1)S(1)} %get-tuple-element.41), channel_id=1, source_target_pairs={{0,14},{1,15},{2,12},{3,13},{4,10},{5,11},{6,8},{7,9},{8,6},{9,7},... | collective-permute-start | bytes 387080 | tf_op jit(solution)/shard_map/ppermute | solution.py:251
  51.0 4.9 %collective-permute-start.15 = (bf16[8,8064]{1,0:T(8,128)(2,1)S(1)}, bf16[8,8064]{1,0:T(8,128)(2,1)S(1)}, u32[]{:S(2)}, u32[]{:S(2)}) collective-permute-start(bf16[8,8064]{1,0:T(8,128)(2,1)S(1)} %get-tuple-element.47), channel_id=1, source_target_pairs={{0,4},{1,5},{2,6},{3,7},{4,0},{5,1},{6,2},{7,3},{8,12},{9,13},{10,... | collective-permute-start | bytes 387080 | tf_op jit(solution)/shard_map/ppermute | solution.py:251
  55.9 1.8 %convolution_convert_fusion = bf16[6,4,64,512]{3,2,1,0:T(8,128)(2,1)} fusion(bf16[6,4,64,256]{3,2,1,0:T(8,128)(2,1)S(1)} %copy-done.4, bf16[6,256,512]{2,1,0:T(8,128)(2,1)S(1)} %copy-done), kind=kOutput, calls=%fused_computation.4 | convolution fusion | flops 403439616 | bytes 3932160 | tf_op jit(solution)/shard_map/bthp,bpc->bthc/dot_general | solution.py:347
  57.7 3.9 %reshape.50 = bf16[6,4,32768]{2,1,0:T(4,128)(2,1)} reshape(bf16[6,4,64,512]{3,2,1,0:T(8,128)(2,1)} %convolution_convert_fusion) | data formatting | bytes 3145728 | tf_op jit(solution)/shard_map/reshape | solution.py:348
  61.7 1.8 %collective-permute-start.14 = (bf16[8,8064]{1,0:T(8,128)(2,1)S(1)}, bf16[8,8064]{1,0:T(8,128)(2,1)S(1)}, u32[]{:S(2)}, u32[]{:S(2)}) collective-permute-start(bf16[8,8064]{1,0:T(8,128)(2,1)S(1)} %get-tuple-element.50), channel_id=1, source_target_pairs={{0,8},{1,9},{2,10},{3,11},{4,12},{5,13},{6,14},{7,15},{8,0},{9,1},... | collective-permute-start | bytes 387080 | tf_op jit(solution)/shard_map/ppermute | solution.py:251
  64.1 2.5 %collective-permute-done.12.refs_2_ = bf16[8,8064]{1,0:T(8,128)(2,1)S(1)} collective-permute-done((bf16[8,8064]{1,0:T(8,128)(2,1)S(1)}, bf16[8,8064]{1,0:T(8,128)(2,1)S(1)}, u32[]{:S(2)}, u32[]{:S(2)}) %collective-permute-start.12) | collective-permute-done | bytes 129056 | tf_op jit(solution)/shard_map/ppermute | solution.py:251
  66.7 3.0 %collective-permute-done.14.refs_3_ = bf16[8,8064]{1,0:T(8,128)(2,1)S(1)} collective-permute-done((bf16[8,8064]{1,0:T(8,128)(2,1)S(1)}, bf16[8,8064]{1,0:T(8,128)(2,1)S(1)}, u32[]{:S(2)}, u32[]{:S(2)}) %collective-permute-start.14) | collective-permute-done | bytes 129056 | tf_op jit(solution)/shard_map/ppermute | solution.py:251
  69.7 1.1 %collective-permute-done.16.refs_4_ = bf16[8,8064]{1,0:T(8,128)(2,1)S(1)} collective-permute-done((bf16[8,8064]{1,0:T(8,128)(2,1)S(1)}, bf16[8,8064]{1,0:T(8,128)(2,1)S(1)}, u32[]{:S(2)}, u32[]{:S(2)}) %collective-permute-start.16) | collective-permute-done | bytes 129056 | tf_op jit(solution)/shard_map/ppermute | solution.py:251
  70.8 1.6 %combine.1 = bf16[24,7168]{1,0:T(8,128)(2,1)} custom-call(s32[1]{0:T(128)} %bitcast.chip_ref, s32[2,24]{1,0:T(2,128)S(1)} %bitcast.23, f32[2,24]{1,0:T(2,128)S(1)} %bitcast.24, bf16[8,8064]{1,0:T(8,128)(2,1)S(1)} %collective-permute-done.10.refs_0_, bf16[8,8064]{1,0:T(8,128)(2,1)S(1)} %collective-permute-done.11.refs_1_, ...), custom_call_target="tpu_custom_call" | custom-call | tf_op jit(solution)/shard_map/combine/pallas_call | solution.py:221
  (41 shorter events, 6.1 us)
Async XLA Ops:
  0.6 20.1 %copy-start = (bf16[6,256,512]{2,1,0:T(8,128)(2,1)S(1)}, bf16[6,256,512]{2,1,0:T(8,128)(2,1)}, u32[]{:S(2)}) copy-start(bf16[6,256,512]{2,1,0:T(8,128)(2,1)} %param.19) | copy-start | bytes 4718596
  2.5 21.8 %collective-permute-start = (bf16[8,8064]{1,0:T(8,128)(2,1)S(1)}, bf16[8,8064]{1,0:T(8,128)(2,1)}, u32[]{:S(2)}, u32[]{:S(2)}) collective-permute-start(bf16[8,8064]{1,0:T(8,128)(2,1)S(1)} %get-tuple-element.27), channel_id=1, source_target_pairs={{0,14},{1,15},{2,12},{3,13},{4,10},{5,11},{6,8},{7,9},{8,6},{9,7},... | collective-permute-start | bytes 387080 | tf_op jit(solution)/shard_map/ppermute | solution.py:251
  8.6 16.6 %collective-permute-start.1 = (bf16[8,8064]{1,0:T(8,128)(2,1)S(1)}, bf16[8,8064]{1,0:T(8,128)(2,1)S(1)}, u32[]{:S(2)}, u32[]{:S(2)}) collective-permute-start(bf16[8,8064]{1,0:T(8,128)(2,1)S(1)} %get-tuple-element.28), channel_id=1, source_target_pairs={{0,12},{1,13},{2,14},{3,15},{4,8},{5,9},{6,10},{7,11},{8,4},{9,5},... | collective-permute-start | bytes 387080 | tf_op jit(solution)/shard_map/ppermute | solution.py:251
  8.8 16.4 %collective-permute-start.2 = (bf16[8,8064]{1,0:T(8,128)(2,1)S(1)}, bf16[8,8064]{1,0:T(8,128)(2,1)S(1)}, u32[]{:S(2)}, u32[]{:S(2)}) collective-permute-start(bf16[8,8064]{1,0:T(8,128)(2,1)S(1)} %get-tuple-element.29), channel_id=1, source_target_pairs={{0,10},{1,11},{2,8},{3,9},{4,14},{5,15},{6,12},{7,13},{8,2},{9,3},... | collective-permute-start | bytes 387080 | tf_op jit(solution)/shard_map/ppermute | solution.py:251
  9.6 14.0 %collective-permute-start.3 = (bf16[8,8064]{1,0:T(8,128)(2,1)S(1)}, bf16[8,8064]{1,0:T(8,128)(2,1)}, u32[]{:S(2)}, u32[]{:S(2)}) collective-permute-start(bf16[8,8064]{1,0:T(8,128)(2,1)S(1)} %get-tuple-element.31), channel_id=1, source_target_pairs={{0,2},{1,3},{2,0},{3,1},{4,6},{5,7},{6,4},{7,5},{8,10},{9,11},{10,... | collective-permute-start | bytes 387080 | tf_op jit(solution)/shard_map/ppermute | solution.py:251
  11.1 12.6 %collective-permute-start.5 = (bf16[8,8064]{1,0:T(8,128)(2,1)S(1)}, bf16[8,8064]{1,0:T(8,128)(2,1)}, u32[]{:S(2)}, u32[]{:S(2)}) collective-permute-start(bf16[8,8064]{1,0:T(8,128)(2,1)S(1)} %get-tuple-element.34), channel_id=1, source_target_pairs={{0,4},{1,5},{2,6},{3,7},{4,0},{5,1},{6,2},{7,3},{8,12},{9,13},{10,... | collective-permute-start | bytes 387080 | tf_op jit(solution)/shard_map/ppermute | solution.py:251
  16.5 3.9 %copy-start.5 = (bf16[6,256,64]{1,2,0:T(8,128)(2,1)S(1)}, bf16[6,256,64]{1,2,0:T(8,128)(2,1)}, u32[]{:S(2)}) copy-start(bf16[6,256,64]{1,2,0:T(8,128)(2,1)} %param.20) | copy-start | bytes 589828
  20.4 1.4 %copy-start.3 = (bf16[6,4,64,512]{3,2,1,0:T(8,128)(2,1)S(1)}, bf16[6,4,64,512]{3,2,1,0:T(8,128)(2,1)}, u32[]{:S(2)}) copy-start(bf16[6,4,64,512]{3,2,1,0:T(8,128)(2,1)} %reshape.48) | copy-start | bytes 4718596
  23.6 7.2 %collective-permute-start.4 = (bf16[8,8064]{1,0:T(8,128)(2,1)S(1)}, bf16[8,8064]{1,0:T(8,128)(2,1)S(1)}, u32[]{:S(2)}, u32[]{:S(2)}) collective-permute-start(bf16[8,8064]{1,0:T(8,128)(2,1)S(1)} %get-tuple-element.32), channel_id=1, source_target_pairs={{0,8},{1,9},{2,10},{3,11},{4,12},{5,13},{6,14},{7,15},{8,0},{9,1},... | collective-permute-start | bytes 387080 | tf_op jit(solution)/shard_map/ppermute | solution.py:251
  23.7 7.5 %collective-permute-start.6 = (bf16[8,8064]{1,0:T(8,128)(2,1)S(1)}, bf16[8,8064]{1,0:T(8,128)(2,1)S(1)}, u32[]{:S(2)}, u32[]{:S(2)}) collective-permute-start(bf16[8,8064]{1,0:T(8,128)(2,1)S(1)} %get-tuple-element.36), channel_id=1, source_target_pairs={{0,6},{1,7},{2,4},{3,5},{4,2},{5,3},{6,0},{7,1},{8,14},{9,15},{10,... | collective-permute-start | bytes 387080 | tf_op jit(solution)/shard_map/ppermute | solution.py:251
  30.9 2.0 %collective-permute-start.7 = (bf16[32,8064]{1,0:T(8,128)(2,1)S(1)}, bf16[32,8064]{1,0:T(8,128)(2,1)S(1)}, u32[]{:S(2)}, u32[]{:S(2)}) collective-permute-start(bf16[32,8064]{1,0:T(8,128)(2,1)S(1)} %constant_dynamic-update-slice_fusion.refs_0_), channel_id=1, source_target_pairs={{0,1},{1,0},{2,3},{3,2},{4,5},{5,4},{6,7},{7,6},{8,9},{9,8},{10,11... | collective-permute-start | bytes 1548296 | tf_op jit(solution)/shard_map/ppermute | solution.py:245
  32.2 2.0 %collective-permute-start.8 = (bf16[32,8064]{1,0:T(8,128)(2,1)S(1)}, bf16[32,8064]{1,0:T(8,128)(2,1)S(1)}, u32[]{:S(2)}, u32[]{:S(2)}) collective-permute-start(bf16[32,8064]{1,0:T(8,128)(2,1)S(1)} %pad_maximum_fusion.refs_1_), channel_id=1, source_target_pairs={{0,1},{1,0},{2,3},{3,2},{4,5},{5,4},{6,7},{7,6},{8,9},{9,8},{10,11... | collective-permute-start | bytes 1548296 | tf_op jit(solution)/shard_map/ppermute | solution.py:245
  42.7 13.3 %copy-start.4 = (bf16[6,4,64,256]{3,2,1,0:T(8,128)(2,1)S(1)}, bf16[6,4,64,256]{3,2,1,0:T(8,128)(2,1)}, u32[]{:S(2)}) copy-start(bf16[6,4,64,256]{3,2,1,0:T(8,128)(2,1)} %fusion.11) | copy-start | bytes 2359300
  42.7 2.7 %collective-permute-start.9 = (bf16[64,8064]{1,0:T(8,128)(2,1)S(1)}, bf16[64,8064]{1,0:T(8,128)(2,1)S(1)}, u32[]{:S(2)}, u32[]{:S(2)}) collective-permute-start(bf16[64,8064]{1,0:T(8,128)(2,1)S(1)} %get-tuple-element.40), channel_id=1, source_target_pairs={{0,1},{1,0},{2,3},{3,2},{4,5},{5,4},{6,7},{7,6},{8,9},{9,8},{10,11... | collective-permute-start | bytes 3096584 | tf_op jit(solution)/shard_map/ppermute | solution.py:245
  45.6 18.5 %collective-permute-start.10 = (bf16[8,8064]{1,0:T(8,128)(2,1)S(1)}, bf16[8,8064]{1,0:T(8,128)(2,1)S(1)}, u32[]{:S(2)}, u32[]{:S(2)}) collective-permute-start(bf16[8,8064]{1,0:T(8,128)(2,1)S(1)} %get-tuple-element.41), channel_id=1, source_target_pairs={{0,14},{1,15},{2,12},{3,13},{4,10},{5,11},{6,8},{7,9},{8,6},{9,7},... | collective-permute-start | bytes 387080 | tf_op jit(solution)/shard_map/ppermute | solution.py:251
  50.1 14.1 %collective-permute-start.11 = (bf16[8,8064]{1,0:T(8,128)(2,1)S(1)}, bf16[8,8064]{1,0:T(8,128)(2,1)S(1)}, u32[]{:S(2)}, u32[]{:S(2)}) collective-permute-start(bf16[8,8064]{1,0:T(8,128)(2,1)S(1)} %get-tuple-element.42), channel_id=1, source_target_pairs={{0,12},{1,13},{2,14},{3,15},{4,8},{5,9},{6,10},{7,11},{8,4},{9,5},... | collective-permute-start | bytes 387080 | tf_op jit(solution)/shard_map/ppermute | solution.py:251
  50.1 16.6 %collective-permute-start.12 = (bf16[8,8064]{1,0:T(8,128)(2,1)S(1)}, bf16[8,8064]{1,0:T(8,128)(2,1)S(1)}, u32[]{:S(2)}, u32[]{:S(2)}) collective-permute-start(bf16[8,8064]{1,0:T(8,128)(2,1)S(1)} %get-tuple-element.43), channel_id=1, source_target_pairs={{0,10},{1,11},{2,8},{3,9},{4,14},{5,15},{6,12},{7,13},{8,2},{9,3},... | collective-permute-start | bytes 387080 | tf_op jit(solution)/shard_map/ppermute | solution.py:251
  50.1 11.6 %collective-permute-start.13 = (bf16[8,8064]{1,0:T(8,128)(2,1)S(1)}, bf16[8,8064]{1,0:T(8,128)(2,1)S(1)}, u32[]{:S(2)}, u32[]{:S(2)}) collective-permute-start(bf16[8,8064]{1,0:T(8,128)(2,1)S(1)} %get-tuple-element.45), channel_id=1, source_target_pairs={{0,2},{1,3},{2,0},{3,1},{4,6},{5,7},{6,4},{7,5},{8,10},{9,11},{10,... | collective-permute-start | bytes 387080 | tf_op jit(solution)/shard_map/ppermute | solution.py:251
  51.0 10.7 %collective-permute-start.15 = (bf16[8,8064]{1,0:T(8,128)(2,1)S(1)}, bf16[8,8064]{1,0:T(8,128)(2,1)S(1)}, u32[]{:S(2)}, u32[]{:S(2)}) collective-permute-start(bf16[8,8064]{1,0:T(8,128)(2,1)S(1)} %get-tuple-element.47), channel_id=1, source_target_pairs={{0,4},{1,5},{2,6},{3,7},{4,0},{5,1},{6,2},{7,3},{8,12},{9,13},{10,... | collective-permute-start | bytes 387080 | tf_op jit(solution)/shard_map/ppermute | solution.py:251
  57.7 13.1 %copy-start.1 = (s32[24,2]{0,1:T(2,128)S(1)}, s32[24,2]{0,1:T(2,128)}, u32[]{:S(2)}) copy-start(s32[24,2]{0,1:T(2,128)} %param.12) | copy-start | bytes 580
  57.7 13.1 %copy-start.2 = (f32[24,2]{0,1:T(2,128)S(1)}, f32[24,2]{0,1:T(2,128)}, u32[]{:S(2)}) copy-start(f32[24,2]{0,1:T(2,128)} %param.13) | copy-start | bytes 580
  61.7 8.0 %collective-permute-start.14 = (bf16[8,8064]{1,0:T(8,128)(2,1)S(1)}, bf16[8,8064]{1,0:T(8,128)(2,1)S(1)}, u32[]{:S(2)}, u32[]{:S(2)}) collective-permute-start(bf16[8,8064]{1,0:T(8,128)(2,1)S(1)} %get-tuple-element.50), channel_id=1, source_target_pairs={{0,8},{1,9},{2,10},{3,11},{4,12},{5,13},{6,14},{7,15},{8,0},{9,1},... | collective-permute-start | bytes 387080 | tf_op jit(solution)/shard_map/ppermute | solution.py:251
  63.4 7.3 %collective-permute-start.16 = (bf16[8,8064]{1,0:T(8,128)(2,1)S(1)}, bf16[8,8064]{1,0:T(8,128)(2,1)S(1)}, u32[]{:S(2)}, u32[]{:S(2)}) collective-permute-start(bf16[8,8064]{1,0:T(8,128)(2,1)S(1)} %get-tuple-element.51), channel_id=1, source_target_pairs={{0,6},{1,7},{2,4},{3,5},{4,2},{5,3},{6,0},{7,1},{8,14},{9,15},{10,... | collective-permute-start | bytes 387080 | tf_op jit(solution)/shard_map/ppermute | solution.py:251

commit v4 on v3

--- a/solution.py
+++ b/solution.py
@@ -12,9 +12,10 @@
 SUB = 8
 FOLD = SUB // 2
 MIB = 1 << 20
-ORDER = (7, 6, 5, 1, 2, 4, 3)
-GROUPED = (7, 6, 5, 4, 0, 1, 2, 3)
-BACK = (7, 6, 5, 4, 3, 2, 1, 0)
+FAR = (7, 6, 5, 4)
+BACK = (7, 6, 5, 1, 2, 3, 4, 0)
+PLACED = (0, 1, 2, 3) + FAR
+TAKEN = (SUB, SUB, 2 * SUB) + (SUB,) * 4
 HBM = pl.BlockSpec(memory_space=pltpu.HBM)
 VMEM = pl.BlockSpec(memory_space=pltpu.VMEM)
 
@@ -54,14 +55,34 @@
     return pltpu.with_memory_space_constraint(value, pltpu.HBM)
 
 
-def pack_kernel(chip_ref, ids_hbm, x_hbm, *refs):
-    outs, (ids_ref, x_ref, sems) = refs[:EXPERTS], refs[EXPERTS:]
-    ids_copy = pltpu.make_async_copy(ids_hbm, ids_ref, sems.at[0])
-    x_copy = pltpu.make_async_copy(x_hbm, x_ref, sems.at[1])
-    ids_copy.start()
-    x_copy.start()
-    ids_copy.wait()
-    x_copy.wait()
+def in_vmem(value):
+    return pltpu.with_memory_space_constraint(value, pltpu.VMEM)
+
+
+def load_kernel(*refs):
+    token_ref, sems = refs[-2:]
+    token_ref[...] = jnp.zeros_like(token_ref)
+    count = len(refs) // 2 - 1
+    copies = [pltpu.make_async_copy(refs[i], refs[count + i], sems.at[i]) for i in range(count)]
+    for copy in copies:
+        copy.start()
+    for copy in copies:
+        copy.wait()
+
+
+def load(*weights):
+    return pl.pallas_call(
+        load_kernel,
+        out_shape=[pltpu.VMEM(w.shape, w.dtype) for w in weights] + [jax.ShapeDtypeStruct((8, 128), f32)],
+        in_specs=[HBM] * len(weights),
+        out_specs=[VMEM] * (len(weights) + 1),
+        scratch_shapes=[pltpu.SemaphoreType.DMA((len(weights),))],
+        compiler_params=pltpu.CompilerParams(vmem_limit_bytes=MIB),
+        name="load",
+    )(*[in_hbm(w) for w in weights])
+
+
+def pack_kernel(chip_ref, ids_ref, x_ref, *outs):
     features = x_ref.shape[1]
     tail = features // SUB
     hit, slot, _, q = routing(ids_ref[...], chip_ref[0])
@@ -70,26 +91,48 @@
     for i in range(SUB):
         last = last + dot(ones(hit & (slot == SUB) & (q == i)), x_ref[:, i * tail:(i + 1) * tail])
     last = last.astype(bf16)
-    for m, out in enumerate(outs):
-        out[:, :features] = main[m * SUB:(m + 1) * SUB]
-        out[:, features:] = last[m * SUB:(m + 1) * SUB]
+    for m, out in destinations(outs):
+        rows = slice(m * SUB, (m + 1) * SUB)
+        out[:, :features] = main[rows]
+        out[:, features:] = last[rows]
+
+
+def sent_shapes(wide):
+    return [jax.ShapeDtypeStruct((rows, wide), bf16) for rows in (SUB, 2 * SUB) + (SUB,) * 5]
+
+
+def destinations(outs):
+    own, along_y, along_z, *far = outs
+    near = [(0, own), (1, along_y.at[:SUB]), (3, along_y.at[SUB:]), (2, along_z)]
+    return near + list(zip(FAR, far))
 
 
 def pack(chip, ids, x):
     features = x.shape[1]
     return pl.pallas_call(
         pack_kernel,
-        out_shape=[jax.ShapeDtypeStruct((SUB, features + features // SUB), bf16)] * EXPERTS,
-        in_specs=[pl.BlockSpec(memory_space=pltpu.SMEM)] + [HBM] * 2,
-        out_specs=[VMEM] * EXPERTS,
-        scratch_shapes=[
-            pltpu.VMEM(ids.shape, ids.dtype),
-            pltpu.VMEM(x.shape, x.dtype),
-            pltpu.SemaphoreType.DMA((2,)),
-        ],
+        out_shape=sent_shapes(features + features // SUB),
+        in_specs=[pl.BlockSpec(memory_space=pltpu.SMEM)] + [VMEM] * 2,
+        out_specs=[VMEM] * len(TAKEN),
         compiler_params=pltpu.CompilerParams(vmem_limit_bytes=12 * MIB),
         name="pack",
     )(chip, in_hbm(ids), in_hbm(x))
+
+
+def stack_kernel(first_ref, second_ref, out_ref):
+    out_ref[:SUB, :] = first_ref[...]
+    out_ref[SUB:, :] = second_ref[SUB:, :]
+
+
+def stack(first, second):
+    return pl.pallas_call(
+        stack_kernel,
+        out_shape=jax.ShapeDtypeStruct(second.shape, bf16),
+        in_specs=[VMEM] * 2,
+        out_specs=VMEM,
+        compiler_params=pltpu.CompilerParams(vmem_limit_bytes=4 * MIB),
+        name="stack",
+    )(first, second)
 
 
 def spread(i, count):
@@ -99,44 +142,32 @@
 
 
 def expert_kernel(groups, *refs):
-    ins, (gate_hbm, up_hbm, down_hbm) = refs[:groups], refs[groups:groups + 3]
+    ins, (gate_ref, up_ref, down_ref) = refs[:groups], refs[groups:groups + 3]
     mine_ref, theirs_ref = refs[groups + 3:groups + 5]
-    gate_ref, up_ref, down_ref, rows_ref, tail_ref, acc_ref, sems = refs[groups + 5:]
+    rows_ref, tail_ref, acc_ref = refs[groups + 5:]
     features, units = gate_ref.shape
     tail = features // SUB
     top = tail_ref.shape[0]
     count = top // SUB
     wide = 2 * tail
-    copies = []
-    for k in range(FOLD):
-        rows = pl.ds(k * wide, wide)
-        for ref, to in ((gate_hbm, gate_ref), (up_hbm, up_ref)):
-            copies.append(pltpu.make_async_copy(ref.at[rows], to.at[rows], sems.at[len(copies)]))
-    for k in range(FOLD):
-        columns = pl.ds(k * wide, wide)
-        copies.append(pltpu.make_async_copy(down_hbm.at[:, columns], down_ref.at[:, columns], sems.at[len(copies)]))
-    for copy in copies:
-        copy.start()
     start = 0
-    for ref in ins:
-        rows = slice(start, start + ref.shape[0])
-        rows_ref[rows, :] = ref[:, :features]
-        tail_ref[rows, :] = ref[:, features:]
-        start += ref.shape[0]
+    for ref, taken in zip(ins, 2 * TAKEN):
+        rows = slice(start, start + taken)
+        rows_ref[rows, :] = ref[:taken, :features]
+        tail_ref[rows, :] = ref[:taken, features:]
+        start += taken
     folded = tail_ref[...]
     for i in range(SUB):
         rows_ref[top:, i * tail:(i + 1) * tail] = dot(spread(i, count), folded).astype(bf16)
     for k in range(FOLD):
         at = slice(k * wide, (k + 1) * wide)
         for n, ref in enumerate((gate_ref, up_ref)):
-            copies[2 * k + n].wait()
             columns = slice(n * units, (n + 1) * units)
             product = dot(rows_ref[:, at], ref[at, :])
             acc_ref[:, columns] = product if k == 0 else acc_ref[:, columns] + product
     hidden = (jax.nn.silu(acc_ref[:, :units]) * acc_ref[:, units:]).astype(bf16)
     folded = jnp.zeros((top, tail), f32)
     for k in range(FOLD):
-        copies[2 * FOLD + k].wait()
         at = slice(k * wide, (k + 1) * wide)
         part = dot(hidden, down_ref[:, at]).astype(bf16)
         mine_ref[:, at] = part[:top // 2]
@@ -150,24 +181,20 @@
 
 def experts(groups, gate_weight, up_weight, down_weight):
     features, units = gate_weight.shape
-    top = sum(group.shape[0] for group in groups)
+    top = 2 * sum(TAKEN)
     rows = top + top // SUB
     wide = groups[0].shape[1]
     return pl.pallas_call(
         functools.partial(expert_kernel, len(groups)),
         out_shape=[jax.ShapeDtypeStruct((top // 2, wide), bf16)] * 2,
-        in_specs=[VMEM] * len(groups) + [HBM] * 3,
+        in_specs=[VMEM] * (len(groups) + 3),
         out_specs=[VMEM] * 2,
         scratch_shapes=[
-            pltpu.VMEM(gate_weight.shape, bf16),
-            pltpu.VMEM(up_weight.shape, bf16),
-            pltpu.VMEM(down_weight.shape, bf16),
             pltpu.VMEM((rows, features), bf16),
             pltpu.VMEM((top, features // SUB), bf16),
             pltpu.VMEM((rows, 2 * units), f32),
-            pltpu.SemaphoreType.DMA((3 * FOLD,)),
         ],
-        compiler_params=pltpu.CompilerParams(vmem_limit_bytes=36 * MIB),
+        compiler_params=pltpu.CompilerParams(vmem_limit_bytes=14 * MIB),
         cost_estimate=pl.CostEstimate(
             flops=6 * rows * features * units, bytes_accessed=6 * features * units, transcendentals=0
         ),
@@ -177,7 +204,8 @@
 
 def add_kernel(a_ref, b_ref, *outs):
     for m, out in enumerate(outs):
-        rows = slice(m * SUB, (m + 1) * SUB)
+        start = PLACED.index(m) * SUB
+        rows = slice(start, start + SUB)
         out[...] = (a_ref[rows, :].astype(f32) + b_ref[rows, :].astype(f32)).astype(bf16)
 
 
@@ -193,7 +221,7 @@
 
 
 def combine_kernel(chip_ref, ids_ref, scores_ref, *refs):
-    ins, out_ref, rows_ref = refs[:EXPERTS], refs[EXPERTS], refs[EXPERTS + 1]
+    *ins, out_ref, rows_ref = refs
     features = out_ref.shape[1]
     tail = features // SUB
     hit, slot, first, q = routing(ids_ref[...], chip_ref[0])
@@ -221,7 +249,7 @@
     return pl.pallas_call(
         combine_kernel,
         out_shape=jax.ShapeDtypeStruct((ids.shape[1], features), bf16),
-        in_specs=[pl.BlockSpec(memory_space=pltpu.SMEM)] + [VMEM] * (2 + EXPERTS),
+        in_specs=[pl.BlockSpec(memory_space=pltpu.SMEM)] + [VMEM] * (2 + len(buffers)),
         out_specs=VMEM,
         scratch_shapes=[pltpu.VMEM((EXPERTS * SUB, features + features // SUB), bf16)],
         compiler_params=pltpu.CompilerParams(vmem_limit_bytes=12 * MIB),
@@ -238,29 +266,30 @@
     members = lax.axis_size("attn")
     chip = (lax.axis_index("attn") // 2).astype(jnp.int32).reshape(1)
     ids, scores = expert_ids.T, route_scores.T
-    weights = [in_hbm(w) for w in (gate_weight, up_weight, down_weight)]
-    scores_of, soften, finish = attention
+    raw_scores, soften, finish = attention
 
     def sibling(value):
         return lax.ppermute(value, "attn", [(i, i ^ 1) for i in range(members)])
 
-    def exchange(sent, *first):
-        got = {0: sent[0]}
-        for m in ORDER:
-            value = after(sent[m], got[5 - m], *first) if m in (4, 3) else sent[m]
-            got[m] = lax.ppermute(value, "attn", [(i, i ^ (2 * m)) for i in range(members)])
-        return got
-
-    got = exchange(pack(chip, ids, moe_input))
-    order = GROUPED
-    first = jnp.concatenate([got[m] for m in order[:FOLD]], axis=0)
-    second = jnp.concatenate([got[m] for m in order[FOLD:]], axis=0)
-    probs = soften(after(scores_of, got[1]))
-    second = after(second, probs)
-    mine, theirs = experts([first, second, sibling(first), sibling(second)], *weights)
+    def across(value, m):
+        return lax.ppermute(value, "attn", [(i, i ^ (2 * m)) for i in range(members)])
+
+    own, along_y, along_z, *far = pack(chip, ids, moe_input)
+    far = [across(value, m) for value, m in zip(far, FAR)]
+    along_y = across(along_y, 1)
+    got = [own, along_y, across(stack(along_z, along_y), 2)] + far
+    raw = raw_scores(got[1:2])
+    weights, _ = lax.optimization_barrier(((gate_weight, up_weight, down_weight), raw))
+    *weights, token = load(*weights)
+    mine = got[:3] + [after(value, token) for value in got[3:]]
+    theirs = [sibling(value) for value in mine]
+    mine, theirs = experts(mine + theirs, *[in_vmem(w) for w in weights])
     total = add(mine, sibling(theirs))
-    attn_output = finish(after(probs, *total))
-    back = exchange({m: total[place] for place, m in enumerate(order)}, attn_output)
+    attn_output = finish(soften(after(raw, *total)))
+    back = {0: total[0]}
+    for m in (7, 6, 5, 1, 2, 4, 3):
+        value = after(total[m], back[5 - m], attn_output) if m in (4, 3) else total[m]
+        back[m] = across(value, m)
     moe_output = combine(chip, ids, scores, [back[m] for m in BACK], features)
     return moe_output, attn_output
 
@@ -314,8 +343,8 @@
     values = expert_out.reshape(EXPERTS * CAP, features)[place].astype(jnp.float32)
     values = values.reshape(token_count, picks, features)
     moe_output = jnp.sum(values * combine_weight[:, :, None], axis=1).astype(jnp.bfloat16)
-    scores_of, soften, finish = attention
-    return moe_output, finish(soften(scores_of))
+    raw_scores, soften, finish = attention
+    return moe_output, finish(soften(raw_scores()))
 
 
 def attend(q_latent, q_rope, latent_cache, rope_cache, cache_lengths):
@@ -324,14 +353,17 @@
     latent_width = latent_cache.shape[2]
     rope_width = rope_cache.shape[2]
     head_count = q_latent.shape[2] // latent_width
-    query_lat = q_latent.reshape(seq_count, step_count, head_count, latent_width)
-    query_rot = q_rope.reshape(seq_count, step_count, head_count, rope_width)
-    scores = jnp.einsum(
-        "bthc,bpc->bthp", query_lat, latent_cache, preferred_element_type=jnp.float32
-    )
-    scores = scores + jnp.einsum(
-        "bthc,bpc->bthp", query_rot, rope_cache, preferred_element_type=jnp.float32
-    )
+
+    def raw_scores(before=()):
+        query_rot = q_rope.reshape(seq_count, step_count, head_count, rope_width)
+        query_lat = after(q_latent, *before)
+        query_lat = query_lat.reshape(seq_count, step_count, head_count, latent_width)
+        scores = jnp.einsum(
+            "bthc,bpc->bthp", query_lat, latent_cache, preferred_element_type=jnp.float32
+        )
+        return scores + jnp.einsum(
+            "bthc,bpc->bthp", query_rot, rope_cache, preferred_element_type=jnp.float32
+        )
 
     def soften(scores):
         scores = scores * score_factor
@@ -347,7 +379,7 @@
         attn = jnp.einsum("bthp,bpc->bthc", probs, latent_cache, preferred_element_type=jnp.float32)
         return attn.astype(jnp.bfloat16).reshape(seq_count, step_count, head_count * latent_width)
 
-    return scores, soften, finish
+    return raw_scores, soften, finish
 
 
 def body(

time: 72.8 us -> 74 us (1.016)
  matrix products: 3.84 us -> 10.4 us
  Pallas kernels: 12.2 us -> 17.2 us
  waiting for transfers between devices: 13.8 us -> 9.53 us
  other arithmetic: 4.73 us -> 0.71 us
  local copies, waits for them, and re-layouts: 11.1 us -> 9.77 us
  starting transfers between devices: 26 us -> 25.2 us
    pallas_call x1 -> x3, Pallas kernels: 1.88 us -> 10.3 us  [the longest x1 8.45 us: load(): pl.pallas_call(load_kernel, out_shape=[pltpu.VMEM(w.shape, w.dtype) for w...]
    ppermute x14 -> x13, waiting for transfers between devices: 9.73 us -> 5.98 us  [across(): return lax.ppermute(value, 'attn', [(i, i ^ 2 * m) for i in range(members)])]
    dot_general x1, matrix products: 1.75 us -> 5.41 us  [finish(): jnp.einsum('bthp,bpc->bthc', probs, latent_cache, preferred_element_type=...]
    pallas_call x1, Pallas kernels: 8.46 us -> 5.05 us  [experts(): pl.pallas_call(functools.partial(expert_kernel, len(groups)), out_shape=[...]
    dot_general x2, matrix products: 2.09 us -> 5.02 us  [the longest x1 2.53 us: raw_scores(): jnp.einsum('bthc,bpc->bthp', query_rot, rope_cache, preferred_element_typ...]
    div x1 -> x0, other arithmetic: 2.92 us -> none  [soften(): weights / jnp.sum(weights, axis=-1, keepdims=True)]
    ppermute x14 -> x13, starting transfers between devices: 25.3 us -> 23.2 us  [across(): return lax.ppermute(value, 'attn', [(i, i ^ 2 * m) for i in range(members)])]
    unnamed x15 -> x10, local copies, waits for them, and re-layouts: 2.03 us -> 0.03 us
  transfers between devices with their start and end apart: 17 -> 21, of which waited for: 9 -> 8; matrix products, arithmetic and copies ran while one was open for 26% -> 28% of each run, Pallas kernels for 0% -> 12%
where the time goes in v4:
time: 74 us; the launch traced here: 73.6 us
  starting transfers between devices  25.2 us (34%)
  Pallas kernels  17.2 us (23%)
  matrix products  10.4 us (14%)
  local copies, waits for them, and re-layouts  9.77 us (13%)
  waiting for transfers between devices  9.53 us (13%)
  between operations  0.77 us (1%)
    ppermute x13, starting transfers between devices, across(): return lax.ppermute(value, 'attn', [(i, i ^ 2 * m) for i in range(members)])  23.2 us
    pallas_call x1, Pallas kernels, load(): pl.pallas_call(load_kernel, out_shape=[pltpu.VMEM(w.shape, w.dtype) for w...  8.45 us
    ppermute x13, waiting for transfers between devices, across(): return lax.ppermute(value, 'attn', [(i, i ^ 2 * m) for i in range(members)])  5.98 us
    dot_general x1, matrix products, finish(): jnp.einsum('bthp,bpc->bthc', probs, latent_cache, preferred_element_type=...  5.41 us
    pallas_call x1, Pallas kernels, experts(): pl.pallas_call(functools.partial(expert_kernel, len(groups)), out_shape=[...  5.05 us
    reshape x1, local copies, waits for them, and re-layouts, finish(): attn.astype(jnp.bfloat16)  3.87 us
    reshape x1, local copies, waits for them, and re-layouts, raw_scores(): query_lat.reshape(seq_count, step_count, head_count, latent_width)  3.82 us
    ppermute x8, waiting for transfers between devices, sibling(): return lax.ppermute(value, 'attn', [(i, i ^ 1) for i in range(members)])  3.55 us
  transfers between devices with their start and end apart: 21, of which 8 were waited for; matrix products, arithmetic and copies ran while one was open for 28% of the time, Pallas kernels for 12%

profile of v4, /device:TPU:0, one launch (start us, length us, event | category | flops | bytes accessed | tf_op | source)
XLA Modules:
  0.0 73.6 jit_solution(4019169173538327897)
XLA Ops:
  0.7 1.9 %pack.1 = (bf16[8,8064]{1,0:T(8,128)(2,1)S(1)}, bf16[16,8064]{1,0:T(8,128)(2,1)S(1)}, bf16[8,8064]{1,0:T(8,128)(2,1)S(1)}, bf16[8,8064]{1,0:T(8,128)(2,1)S(1)}, ...) custom-call(s32[1]{0:T(128)} %bitcast.chip_ref, s32[2,24]{1,0:T(2,128)} %bitcast.21, ...), custom_call_target="tpu_custom_call" | custom-call | tf_op jit(solution)/shard_map/pack/pallas_call | solution.py:112
  2.5 3.0 %collective-permute-start = (bf16[16,8064]{1,0:T(8,128)(2,1)S(1)}, bf16[16,8064]{1,0:T(8,128)(2,1)S(1)}, u32[]{:S(2)}, u32[]{:S(2)}) collective-permute-start(bf16[16,8064]{1,0:T(8,128)(2,1)S(1)} %get-tuple-element.35), channel_id=1, source_target_pairs={{0,2},{1,3},{2,0},{3,1},{4,6},{5,7},{6,4},{7,5},{8,10},{9,11},{10,... | collective-permute-start | bytes 774152 | tf_op jit(solution)/shard_map/ppermute | solution.py:275
  5.6 2.6 %collective-permute-start.5 = (bf16[8,8064]{1,0:T(8,128)(2,1)S(1)}, bf16[8,8064]{1,0:T(8,128)(2,1)S(1)}, u32[]{:S(2)}, u32[]{:S(2)}) collective-permute-start(bf16[8,8064]{1,0:T(8,128)(2,1)S(1)} %get-tuple-element.48), channel_id=1, source_target_pairs={{0,8},{1,9},{2,10},{3,11},{4,12},{5,13},{6,14},{7,15},{8,0},{9,1},... | collective-permute-start | bytes 387080 | tf_op jit(solution)/shard_map/ppermute | solution.py:275
  8.1 3.9 %collective-permute-start.3 = (bf16[8,8064]{1,0:T(8,128)(2,1)S(1)}, bf16[8,8064]{1,0:T(8,128)(2,1)S(1)}, u32[]{:S(2)}, u32[]{:S(2)}) collective-permute-start(bf16[8,8064]{1,0:T(8,128)(2,1)S(1)} %get-tuple-element.44), channel_id=1, source_target_pairs={{0,12},{1,13},{2,14},{3,15},{4,8},{5,9},{6,10},{7,11},{8,4},{9,5},... | collective-permute-start | bytes 387080 | tf_op jit(solution)/shard_map/ppermute | solution.py:275
  12.0 1.2 %collective-permute-start.2 = (bf16[8,8064]{1,0:T(8,128)(2,1)S(1)}, bf16[8,8064]{1,0:T(8,128)(2,1)S(1)}, u32[]{:S(2)}, u32[]{:S(2)}) collective-permute-start(bf16[8,8064]{1,0:T(8,128)(2,1)S(1)} %get-tuple-element.37), channel_id=1, source_target_pairs={{0,14},{1,15},{2,12},{3,13},{4,10},{5,11},{6,8},{7,9},{8,6},{9,7},... | collective-permute-start | bytes 387080 | tf_op jit(solution)/shard_map/ppermute | solution.py:275
  13.2 2.0 %reshape.49 = bf16[6,4,64,64]{3,2,1,0:T(8,128)(2,1)} reshape(bf16[6,4,4096]{2,1,0:T(4,128)(2,1)} %param.18) | data formatting | bytes 393216 | tf_op jit(solution)/shard_map/reshape | solution.py:358
  15.2 2.5 %fusion.14 = f32[6,4,64,256]{3,2,1,0:T(8,128)} fusion(bf16[6,4,64,64]{3,2,1,0:T(8,128)(2,1)} %reshape.49, bf16[6,256,64]{1,2,0:T(8,128)(2,1)} %param.20), kind=kOutput, calls=%fused_computation.15 | convolution fusion | flops 50331648 | bytes 1966080 | tf_op jit(solution)/shard_map/bthc,bpc->bthp/dot_general | solution.py:364
  17.8 3.8 %reshape.48 = bf16[6,4,64,512]{3,2,1,0:T(8,128)(2,1)} reshape(bf16[6,4,32768]{2,1,0:T(4,128)(2,1)} %param.17) | data formatting | bytes 3145728 | tf_op jit(solution)/shard_map/reshape | solution.py:360
  21.7 2.5 %fusion.6 = f32[6,4,64,256]{3,2,1,0:T(8,128)S(1)} fusion(f32[6,4,64,256]{3,2,1,0:T(8,128)} %fusion.14, bf16[6,4,64,512]{3,2,1,0:T(8,128)(2,1)} %reshape.48, bf16[6,256,512]{2,1,0:T(8,128)(2,1)S(1)} %copy-done), kind=kOutput, calls=%fused_computation.9 | convolution fusion | flops 403046400 | bytes 6291456 | tf_op jit(solution)/shard_map/bthc,bpc->bthp/dot_general | solution.py:361
  24.2 8.4 %load.1 = (bf16[7168,512]{1,0:T(8,128)(2,1)S(1)}, bf16[7168,512]{1,0:T(8,128)(2,1)S(1)}, bf16[512,7168]{1,0:T(8,128)(2,1)S(1)}, f32[8,128]{1,0:T(8,128)}) custom-call(bf16[7168,512]{1,0:T(8,128)(2,1)} %refs_0_, bf16[7168,512]{1,0:T(8,128)(2,1)} %refs_1_, bf16[512,7168]{1,0:T(8,128)(2,1)} %refs_2_), custom_call_target="tpu_custom_call" | custom-call | tf_op jit(solution)/shard_map/load/pallas_call | solution.py:74
  34.6 0.7 %collective-permute-done.11.refs_12_ = bf16[8,8064]{1,0:T(8,128)(2,1)S(1)} collective-permute-done((bf16[8,8064]{1,0:T(8,128)(2,1)S(1)}, bf16[8,8064]{1,0:T(8,128)(2,1)S(1)}, u32[]{:S(2)}, u32[]{:S(2)}) %collective-permute-start.11) | collective-permute-done | bytes 129056 | tf_op jit(solution)/shard_map/ppermute | solution.py:272
  35.7 5.0 %experts.1 = (bf16[64,8064]{1,0:T(8,128)(2,1)S(1)}, bf16[64,8064]{1,0:T(8,128)(2,1)S(1)}) custom-call(bf16[8,8064]{1,0:T(8,128)(2,1)S(1)} %get-tuple-element.34.refs_0_, bf16[16,8064]{1,0:T(8,128)(2,1)S(1)} %collective-permute-done.second_ref.refs_1_, bf16[16,8064]{1,0:T(8,128)(2,1)S(1)} %collective-permute-done.1.refs_2_, ...), custom_call_target="tpu_custom_call" | custom-call | flops 3170893824 | bytes 22020096 | tf_op jit(solution)/shard_map/experts/pallas_call | solution.py:187
  41.3 2.2 %collective-permute-done.13.b_ref = bf16[64,8064]{1,0:T(8,128)(2,1)S(1)} collective-permute-done((bf16[64,8064]{1,0:T(8,128)(2,1)S(1)}, bf16[64,8064]{1,0:T(8,128)(2,1)S(1)}, u32[]{:S(2)}, u32[]{:S(2)}) %collective-permute-start.13) | collective-permute-done | bytes 1032224 | tf_op jit(solution)/shard_map/ppermute | solution.py:272
  44.1 2.0 %collective-permute-start.18 = (bf16[8,8064]{1,0:T(8,128)(2,1)S(1)}, bf16[8,8064]{1,0:T(8,128)(2,1)S(1)}, u32[]{:S(2)}, u32[]{:S(2)}) collective-permute-start(bf16[8,8064]{1,0:T(8,128)(2,1)S(1)} %get-tuple-element.59), channel_id=1, source_target_pairs={{0,4},{1,5},{2,6},{3,7},{4,0},{5,1},{6,2},{7,3},{8,12},{9,13},{10,... | collective-permute-start | bytes 387080 | tf_op jit(solution)/shard_map/ppermute | solution.py:275
  46.1 4.7 %collective-permute-start.14 = (bf16[8,8064]{1,0:T(8,128)(2,1)S(1)}, bf16[8,8064]{1,0:T(8,128)(2,1)S(1)}, u32[]{:S(2)}, u32[]{:S(2)}) collective-permute-start(bf16[8,8064]{1,0:T(8,128)(2,1)S(1)} %get-tuple-element.55), channel_id=1, source_target_pairs={{0,14},{1,15},{2,12},{3,13},{4,10},{5,11},{6,8},{7,9},{8,6},{9,7},... | collective-permute-start | bytes 387080 | tf_op jit(solution)/shard_map/ppermute | solution.py:275
  51.4 0.6 fusion.22
  52.0 5.4 %convolution_convert_fusion = bf16[6,4,64,512]{3,2,1,0:T(8,128)(2,1)} fusion(bf16[6,256,512]{2,1,0:T(8,128)(2,1)S(1)} %copy-done, f32[6,4,64]{2,1,0:T(4,128)S(1)} %fusion.22, f32[6,4,64,256]{3,2,1,0:T(8,128)} %copy-done.3, pred[6,4,256]{2,1,0:T(4,128)(4,1)S(1)} %iota_compare_fusion), kind=kOutput, calls=%fused_computation.2 | convolution fusion | flops 405407488 | bytes 4730880 | tf_op jit(solution)/shard_map/bthp,bpc->bthc/dot_general | solution.py:379
  57.4 3.9 %reshape.50 = bf16[6,4,32768]{2,1,0:T(4,128)(2,1)} reshape(bf16[6,4,64,512]{3,2,1,0:T(8,128)(2,1)} %convolution_convert_fusion) | data formatting | bytes 3145728 | tf_op jit(solution)/shard_map/reshape | solution.py:380
  61.2 2.4 %collective-permute-start.20 = (bf16[8,8064]{1,0:T(8,128)(2,1)S(1)}, bf16[8,8064]{1,0:T(8,128)(2,1)S(1)}, u32[]{:S(2)}, u32[]{:S(2)}) collective-permute-start(bf16[8,8064]{1,0:T(8,128)(2,1)S(1)} %get-tuple-element.65), channel_id=1, source_target_pairs={{0,8},{1,9},{2,10},{3,11},{4,12},{5,13},{6,14},{7,15},{8,0},{9,1},... | collective-permute-start | bytes 387080 | tf_op jit(solution)/shard_map/ppermute | solution.py:275
  63.6 2.4 %collective-permute-start.19 = (bf16[8,8064]{1,0:T(8,128)(2,1)S(1)}, bf16[8,8064]{1,0:T(8,128)(2,1)S(1)}, u32[]{:S(2)}, u32[]{:S(2)}) collective-permute-start(bf16[8,8064]{1,0:T(8,128)(2,1)S(1)} %get-tuple-element.64), channel_id=1, source_target_pairs={{0,6},{1,7},{2,4},{3,5},{4,2},{5,3},{6,0},{7,1},{8,14},{9,15},{10,... | collective-permute-start | bytes 387080 | tf_op jit(solution)/shard_map/ppermute | solution.py:275
  66.1 1.6 %collective-permute-done.16.refs_2_ = bf16[8,8064]{1,0:T(8,128)(2,1)S(1)} collective-permute-done((bf16[8,8064]{1,0:T(8,128)(2,1)S(1)}, bf16[8,8064]{1,0:T(8,128)(2,1)S(1)}, u32[]{:S(2)}, u32[]{:S(2)}) %collective-permute-start.16) | collective-permute-done | bytes 129056 | tf_op jit(solution)/shard_map/ppermute | solution.py:275
  67.7 3.8 %collective-permute-done.20.refs_6_ = bf16[8,8064]{1,0:T(8,128)(2,1)S(1)} collective-permute-done((bf16[8,8064]{1,0:T(8,128)(2,1)S(1)}, bf16[8,8064]{1,0:T(8,128)(2,1)S(1)}, u32[]{:S(2)}, u32[]{:S(2)}) %collective-permute-start.20) | collective-permute-done | bytes 129056 | tf_op jit(solution)/shard_map/ppermute | solution.py:275
  71.4 0.6 collective-permute-done.19.refs_5_
  72.0 1.6 %combine.1 = bf16[24,7168]{1,0:T(8,128)(2,1)} custom-call(s32[1]{0:T(128)} %bitcast.chip_ref, s32[2,24]{1,0:T(2,128)S(1)} %bitcast.22, f32[2,24]{1,0:T(2,128)S(1)} %bitcast.23, bf16[8,8064]{1,0:T(8,128)(2,1)S(1)} %collective-permute-done.14.refs_0_, bf16[8,8064]{1,0:T(8,128)(2,1)S(1)} %collective-permute-done.15.refs_1_, ...), custom_call_target="tpu_custom_call" | custom-call | tf_op jit(solution)/shard_map/combine/pallas_call | solution.py:249
  (44 shorter events, 4.1 us)
Async XLA Ops:
  0.6 21.1 %copy-start = (bf16[6,256,512]{2,1,0:T(8,128)(2,1)S(1)}, bf16[6,256,512]{2,1,0:T(8,128)(2,1)}, u32[]{:S(2)}) copy-start(bf16[6,256,512]{2,1,0:T(8,128)(2,1)} %param.19) | copy-start | bytes 4718596
  2.5 15.3 %collective-permute-start = (bf16[16,8064]{1,0:T(8,128)(2,1)S(1)}, bf16[16,8064]{1,0:T(8,128)(2,1)S(1)}, u32[]{:S(2)}, u32[]{:S(2)}) collective-permute-start(bf16[16,8064]{1,0:T(8,128)(2,1)S(1)} %get-tuple-element.35), channel_id=1, source_target_pairs={{0,2},{1,3},{2,0},{3,1},{4,6},{5,7},{6,4},{7,5},{8,10},{9,11},{10,... | collective-permute-start | bytes 774152 | tf_op jit(solution)/shard_map/ppermute | solution.py:275
  5.6 27.1 %collective-permute-start.5 = (bf16[8,8064]{1,0:T(8,128)(2,1)S(1)}, bf16[8,8064]{1,0:T(8,128)(2,1)S(1)}, u32[]{:S(2)}, u32[]{:S(2)}) collective-permute-start(bf16[8,8064]{1,0:T(8,128)(2,1)S(1)} %get-tuple-element.48), channel_id=1, source_target_pairs={{0,8},{1,9},{2,10},{3,11},{4,12},{5,13},{6,14},{7,15},{8,0},{9,1},... | collective-permute-start | bytes 387080 | tf_op jit(solution)/shard_map/ppermute | solution.py:275
  8.1 24.6 %collective-permute-start.4 = (bf16[8,8064]{1,0:T(8,128)(2,1)S(1)}, bf16[8,8064]{1,0:T(8,128)(2,1)S(1)}, u32[]{:S(2)}, u32[]{:S(2)}) collective-permute-start(bf16[8,8064]{1,0:T(8,128)(2,1)S(1)} %get-tuple-element.46), channel_id=1, source_target_pairs={{0,10},{1,11},{2,8},{3,9},{4,14},{5,15},{6,12},{7,13},{8,2},{9,3},... | collective-permute-start | bytes 387080 | tf_op jit(solution)/shard_map/ppermute | solution.py:275
  8.1 25.1 %collective-permute-start.3 = (bf16[8,8064]{1,0:T(8,128)(2,1)S(1)}, bf16[8,8064]{1,0:T(8,128)(2,1)S(1)}, u32[]{:S(2)}, u32[]{:S(2)}) collective-permute-start(bf16[8,8064]{1,0:T(8,128)(2,1)S(1)} %get-tuple-element.44), channel_id=1, source_target_pairs={{0,12},{1,13},{2,14},{3,15},{4,8},{5,9},{6,10},{7,11},{8,4},{9,5},... | collective-permute-start | bytes 387080 | tf_op jit(solution)/shard_map/ppermute | solution.py:275
  12.0 21.8 %collective-permute-start.2 = (bf16[8,8064]{1,0:T(8,128)(2,1)S(1)}, bf16[8,8064]{1,0:T(8,128)(2,1)S(1)}, u32[]{:S(2)}, u32[]{:S(2)}) collective-permute-start(bf16[8,8064]{1,0:T(8,128)(2,1)S(1)} %get-tuple-element.37), channel_id=1, source_target_pairs={{0,14},{1,15},{2,12},{3,13},{4,10},{5,11},{6,8},{7,9},{8,6},{9,7},... | collective-permute-start | bytes 387080 | tf_op jit(solution)/shard_map/ppermute | solution.py:275
  21.6 11.7 %collective-permute-start.1 = (bf16[16,8064]{1,0:T(8,128)(2,1)S(1)}, bf16[16,8064]{1,0:T(8,128)(2,1)S(1)}, u32[]{:S(2)}, u32[]{:S(2)}) collective-permute-start(bf16[16,8064]{1,0:T(8,128)(2,1)S(1)} %stack.1), channel_id=1, source_target_pairs={{0,4},{1,5},{2,6},{3,7},{4,0},{5,1},{6,2},{7,3},{8,12},{9,13},{10,... | collective-permute-start | bytes 774152 | tf_op jit(solution)/shard_map/ppermute | solution.py:275
  24.2 27.2 %copy-start.3 = (f32[6,4,64,256]{3,2,1,0:T(8,128)}, f32[6,4,64,256]{3,2,1,0:T(8,128)S(1)}, u32[]{:S(2)}) copy-start(f32[6,4,64,256]{3,2,1,0:T(8,128)S(1)} %fusion.6) | copy-start | bytes 4718596
  32.7 1.4 %collective-permute-start.6 = (bf16[8,8064]{1,0:T(8,128)(2,1)S(1)}, bf16[8,8064]{1,0:T(8,128)(2,1)S(1)}, u32[]{:S(2)}, u32[]{:S(2)}) collective-permute-start(bf16[8,8064]{1,0:T(8,128)(2,1)S(1)} %get-tuple-element.34.refs_0_), channel_id=1, source_target_pairs={{0,1},{1,0},{2,3},{3,2},{4,5},{5,4},{6,7},{7,6},{8,9},{9,8},{10,11... | collective-permute-start | bytes 387080 | tf_op jit(solution)/shard_map/ppermute | solution.py:272
  32.8 1.5 %collective-permute-start.12 = (bf16[8,8064]{1,0:T(8,128)(2,1)S(1)}, bf16[8,8064]{1,0:T(8,128)(2,1)S(1)}, u32[]{:S(2)}, u32[]{:S(2)}) collective-permute-start(bf16[8,8064]{1,0:T(8,128)(2,1)S(1)} %collective-permute-done.5.refs_6_), channel_id=1, source_target_pairs={{0,1},{1,0},{2,3},{3,2},{4,5},{5,4},{6,7},{7,6},{8,9},{9,8},{10,11... | collective-permute-start | bytes 387080 | tf_op jit(solution)/shard_map/ppermute | solution.py:272
  33.3 2.5 %collective-permute-start.7 = (bf16[16,8064]{1,0:T(8,128)(2,1)S(1)}, bf16[16,8064]{1,0:T(8,128)(2,1)S(1)}, u32[]{:S(2)}, u32[]{:S(2)}) collective-permute-start(bf16[16,8064]{1,0:T(8,128)(2,1)S(1)} %collective-permute-done.second_ref.refs_1_), channel_id=1, source_target_pairs={{0,1},{1,0},{2,3},{3,2},{4,5},{5,4},{6,7},{7,6},{8,9},{9,8},{10,11... | collective-permute-start | bytes 774152 | tf_op jit(solution)/shard_map/ppermute | solution.py:272
  33.4 2.4 %collective-permute-start.8 = (bf16[16,8064]{1,0:T(8,128)(2,1)S(1)}, bf16[16,8064]{1,0:T(8,128)(2,1)S(1)}, u32[]{:S(2)}, u32[]{:S(2)}) collective-permute-start(bf16[16,8064]{1,0:T(8,128)(2,1)S(1)} %collective-permute-done.1.refs_2_), channel_id=1, source_target_pairs={{0,1},{1,0},{2,3},{3,2},{4,5},{5,4},{6,7},{7,6},{8,9},{9,8},{10,11... | collective-permute-start | bytes 774152 | tf_op jit(solution)/shard_map/ppermute | solution.py:272
  33.8 1.6 %collective-permute-start.11 = (bf16[8,8064]{1,0:T(8,128)(2,1)S(1)}, bf16[8,8064]{1,0:T(8,128)(2,1)S(1)}, u32[]{:S(2)}, u32[]{:S(2)}) collective-permute-start(bf16[8,8064]{1,0:T(8,128)(2,1)S(1)} %collective-permute-done.4.refs_5_), channel_id=1, source_target_pairs={{0,1},{1,0},{2,3},{3,2},{4,5},{5,4},{6,7},{7,6},{8,9},{9,8},{10,11... | collective-permute-start | bytes 387080 | tf_op jit(solution)/shard_map/ppermute | solution.py:272
  34.1 1.4 %collective-permute-start.10 = (bf16[8,8064]{1,0:T(8,128)(2,1)S(1)}, bf16[8,8064]{1,0:T(8,128)(2,1)S(1)}, u32[]{:S(2)}, u32[]{:S(2)}) collective-permute-start(bf16[8,8064]{1,0:T(8,128)(2,1)S(1)} %collective-permute-done.3.refs_4_), channel_id=1, source_target_pairs={{0,1},{1,0},{2,3},{3,2},{4,5},{5,4},{6,7},{7,6},{8,9},{9,8},{10,11... | collective-permute-start | bytes 387080 | tf_op jit(solution)/shard_map/ppermute | solution.py:272
  34.3 1.4 %collective-permute-start.9 = (bf16[8,8064]{1,0:T(8,128)(2,1)S(1)}, bf16[8,8064]{1,0:T(8,128)(2,1)S(1)}, u32[]{:S(2)}, u32[]{:S(2)}) collective-permute-start(bf16[8,8064]{1,0:T(8,128)(2,1)S(1)} %collective-permute-done.2.refs_3_), channel_id=1, source_target_pairs={{0,1},{1,0},{2,3},{3,2},{4,5},{5,4},{6,7},{7,6},{8,9},{9,8},{10,11... | collective-permute-start | bytes 387080 | tf_op jit(solution)/shard_map/ppermute | solution.py:272
  40.8 2.7 %collective-permute-start.13 = (bf16[64,8064]{1,0:T(8,128)(2,1)S(1)}, bf16[64,8064]{1,0:T(8,128)(2,1)S(1)}, u32[]{:S(2)}, u32[]{:S(2)}) collective-permute-start(bf16[64,8064]{1,0:T(8,128)(2,1)S(1)} %get-tuple-element.54), channel_id=1, source_target_pairs={{0,1},{1,0},{2,3},{3,2},{4,5},{5,4},{6,7},{7,6},{8,9},{9,8},{10,11... | collective-permute-start | bytes 3096584 | tf_op jit(solution)/shard_map/ppermute | solution.py:272
  43.7 17.5 %collective-permute-start.17 = (bf16[8,8064]{1,0:T(8,128)(2,1)S(1)}, bf16[8,8064]{1,0:T(8,128)(2,1)S(1)}, u32[]{:S(2)}, u32[]{:S(2)}) collective-permute-start(bf16[8,8064]{1,0:T(8,128)(2,1)S(1)} %get-tuple-element.58), channel_id=1, source_target_pairs={{0,2},{1,3},{2,0},{3,1},{4,6},{5,7},{6,4},{7,5},{8,10},{9,11},{10,... | collective-permute-start | bytes 387080 | tf_op jit(solution)/shard_map/ppermute | solution.py:275
  44.1 19.5 %collective-permute-start.18 = (bf16[8,8064]{1,0:T(8,128)(2,1)S(1)}, bf16[8,8064]{1,0:T(8,128)(2,1)S(1)}, u32[]{:S(2)}, u32[]{:S(2)}) collective-permute-start(bf16[8,8064]{1,0:T(8,128)(2,1)S(1)} %get-tuple-element.59), channel_id=1, source_target_pairs={{0,4},{1,5},{2,6},{3,7},{4,0},{5,1},{6,2},{7,3},{8,12},{9,13},{10,... | collective-permute-start | bytes 387080 | tf_op jit(solution)/shard_map/ppermute | solution.py:275
  46.1 19.9 %collective-permute-start.14 = (bf16[8,8064]{1,0:T(8,128)(2,1)S(1)}, bf16[8,8064]{1,0:T(8,128)(2,1)S(1)}, u32[]{:S(2)}, u32[]{:S(2)}) collective-permute-start(bf16[8,8064]{1,0:T(8,128)(2,1)S(1)} %get-tuple-element.55), channel_id=1, source_target_pairs={{0,14},{1,15},{2,12},{3,13},{4,10},{5,11},{6,8},{7,9},{8,6},{9,7},... | collective-permute-start | bytes 387080 | tf_op jit(solution)/shard_map/ppermute | solution.py:275
  50.9 15.2 %collective-permute-start.15 = (bf16[8,8064]{1,0:T(8,128)(2,1)S(1)}, bf16[8,8064]{1,0:T(8,128)(2,1)S(1)}, u32[]{:S(2)}, u32[]{:S(2)}) collective-permute-start(bf16[8,8064]{1,0:T(8,128)(2,1)S(1)} %get-tuple-element.56), channel_id=1, source_target_pairs={{0,12},{1,13},{2,14},{3,15},{4,8},{5,9},{6,10},{7,11},{8,4},{9,5},... | collective-permute-start | bytes 387080 | tf_op jit(solution)/shard_map/ppermute | solution.py:275
  51.1 16.6 %collective-permute-start.16 = (bf16[8,8064]{1,0:T(8,128)(2,1)S(1)}, bf16[8,8064]{1,0:T(8,128)(2,1)S(1)}, u32[]{:S(2)}, u32[]{:S(2)}) collective-permute-start(bf16[8,8064]{1,0:T(8,128)(2,1)S(1)} %get-tuple-element.57), channel_id=1, source_target_pairs={{0,10},{1,11},{2,8},{3,9},{4,14},{5,15},{6,12},{7,13},{8,2},{9,3},... | collective-permute-start | bytes 387080 | tf_op jit(solution)/shard_map/ppermute | solution.py:275
  57.4 14.7 %copy-start.2 = (f32[24,2]{0,1:T(2,128)S(1)}, f32[24,2]{0,1:T(2,128)}, u32[]{:S(2)}) copy-start(f32[24,2]{0,1:T(2,128)} %param.13) | copy-start | bytes 580
  61.2 10.2 %collective-permute-start.20 = (bf16[8,8064]{1,0:T(8,128)(2,1)S(1)}, bf16[8,8064]{1,0:T(8,128)(2,1)S(1)}, u32[]{:S(2)}, u32[]{:S(2)}) collective-permute-start(bf16[8,8064]{1,0:T(8,128)(2,1)S(1)} %get-tuple-element.65), channel_id=1, source_target_pairs={{0,8},{1,9},{2,10},{3,11},{4,12},{5,13},{6,14},{7,15},{8,0},{9,1},... | collective-permute-start | bytes 387080 | tf_op jit(solution)/shard_map/ppermute | solution.py:275
  63.6 8.4 %collective-permute-start.19 = (bf16[8,8064]{1,0:T(8,128)(2,1)S(1)}, bf16[8,8064]{1,0:T(8,128)(2,1)S(1)}, u32[]{:S(2)}, u32[]{:S(2)}) collective-permute-start(bf16[8,8064]{1,0:T(8,128)(2,1)S(1)} %get-tuple-element.64), channel_id=1, source_target_pairs={{0,6},{1,7},{2,4},{3,5},{4,2},{5,3},{6,0},{7,1},{8,14},{9,15},{10,... | collective-permute-start | bytes 387080 | tf_op jit(solution)/shard_map/ppermute | solution.py:275
  (2 other events, 20.1 us)

commit v5 on v2

--- a/solution.py
+++ b/solution.py
@@ -12,7 +12,9 @@
 SUB = 8
 FOLD = SUB // 2
 MIB = 1 << 20
-ORDER = (7, 6, 5, 4, 3, 2, 1)
+BACK = (7, 6, 5, 4, 3, 2, 1, 0)
+PLACED = (0, 1, 2, 3, 4, 5, 6, 7)
+HBM = pl.BlockSpec(memory_space=pltpu.HBM)
 VMEM = pl.BlockSpec(memory_space=pltpu.VMEM)
 
 score_factor = 192.0 ** (-0.5)
@@ -47,6 +49,90 @@
     return jnp.where(mask, 1.0, jnp.zeros(mask.shape, f32)).astype(bf16)
 
 
+def in_hbm(value):
+    return pltpu.with_memory_space_constraint(value, pltpu.HBM)
+
+
+def in_vmem(value):
+    return pltpu.with_memory_space_constraint(value, pltpu.VMEM)
+
+
+def dot_nt(a, b):
+    return lax.dot_general(a, b, (((1,), (1,)), ((), ())), preferred_element_type=f32)
+
+
+def attend_kernel(lengths_ref, q_ref, q_rope_ref, latent_ref, rope_ref, out_ref, lat_ref, rot_ref):
+    seqs, steps, _ = q_ref.shape
+    width, turned = latent_ref.shape[2], rope_ref.shape[1]
+    heads = q_ref.shape[2] // width
+
+    def one(n, carry):
+        for h in range(heads):
+            rows = slice(h * steps, (h + 1) * steps)
+            lat_ref[rows, :] = q_ref[n, :, h * width:(h + 1) * width]
+            rot_ref[rows, :] = q_rope_ref[n, :, h * turned:(h + 1) * turned]
+        latent = latent_ref[n]
+        scores = (dot_nt(lat_ref[...], latent) + dot(rot_ref[...], rope_ref[n])) * score_factor
+        row = lax.broadcasted_iota(jnp.int32, scores.shape, 0)
+        position = lax.broadcasted_iota(jnp.int32, scores.shape, 1)
+        allowed = position <= lengths_ref[n] - steps + row % steps
+        scores = jnp.where(allowed, scores, -jnp.inf)
+        weights = jnp.exp(scores - jnp.max(scores, axis=1, keepdims=True))
+        probs = (weights / jnp.sum(weights, axis=1, keepdims=True)).astype(bf16)
+        attn = dot(probs, latent).astype(bf16)
+        for h in range(heads):
+            out_ref[n, :, h * width:(h + 1) * width] = attn[h * steps:(h + 1) * steps]
+        return carry
+
+    lax.fori_loop(0, seqs, one, 0)
+
+
+def attend_by_sequence(q_latent, q_rope, latent_cache, rope_cache, lengths):
+    width, turned = latent_cache.shape[2], rope_cache.shape[2]
+    rows = q_latent.shape[2] // width * q_latent.shape[1]
+    arrays = q_latent, q_rope, latent_cache, rope_cache.transpose(0, 2, 1)
+    return pl.pallas_call(
+        attend_kernel,
+        out_shape=jax.ShapeDtypeStruct(q_latent.shape, bf16),
+        in_specs=[pl.BlockSpec(memory_space=pltpu.SMEM)] + [VMEM] * 4,
+        out_specs=VMEM,
+        scratch_shapes=[pltpu.VMEM((rows, width), bf16), pltpu.VMEM((rows, turned), bf16)],
+        compiler_params=pltpu.CompilerParams(vmem_limit_bytes=14 * MIB),
+        cost_estimate=pl.CostEstimate(
+            flops=32 * q_latent.size * latent_cache.shape[1],
+            bytes_accessed=2 * (2 * q_latent.size + latent_cache.size),
+            transcendentals=0,
+        ),
+        name="attend",
+    )(lengths, *[in_hbm(v) for v in arrays])
+
+
+def load_kernel(*refs):
+    token_ref, sems = refs[-2:]
+    token_ref[...] = jnp.zeros_like(token_ref)
+    count = len(refs) // 2 - 1
+    copies = [pltpu.make_async_copy(refs[i], refs[count + i], sems.at[i]) for i in range(count)]
+    for copy in copies:
+        copy.start()
+    for copy in copies:
+        copy.wait()
+
+
+def load(*weights):
+    return pl.pallas_call(
+        load_kernel,
+        out_shape=[pltpu.VMEM(w.shape, w.dtype) for w in weights] + [jax.ShapeDtypeStruct((8, 128), f32)],
+        in_specs=[HBM] * len(weights),
+        out_specs=[VMEM] * (len(weights) + 1),
+        scratch_shapes=[pltpu.SemaphoreType.DMA((len(weights),))],
+        compiler_params=pltpu.CompilerParams(vmem_limit_bytes=MIB),
+        cost_estimate=pl.CostEstimate(
+            flops=0, bytes_accessed=2 * sum(w.size for w in weights), transcendentals=0
+        ),
+        name="load",
+    )(*[in_hbm(w) for w in weights])
+
+
 def pack_kernel(chip_ref, ids_ref, x_ref, *outs):
     features = x_ref.shape[1]
     tail = features // SUB
@@ -57,8 +143,9 @@
         last = last + dot(ones(hit & (slot == SUB) & (q == i)), x_ref[:, i * tail:(i + 1) * tail])
     last = last.astype(bf16)
     for m, out in enumerate(outs):
-        out[:, :features] = main[m * SUB:(m + 1) * SUB]
-        out[:, features:] = last[m * SUB:(m + 1) * SUB]
+        rows = slice(m * SUB, (m + 1) * SUB)
+        out[:, :features] = main[rows]
+        out[:, features:] = last[rows]
 
 
 def pack(chip, ids, x):
@@ -70,7 +157,7 @@
         out_specs=[VMEM] * EXPERTS,
         compiler_params=pltpu.CompilerParams(vmem_limit_bytes=12 * MIB),
         name="pack",
-    )(chip, ids, x)
+    )(chip, in_hbm(ids), in_hbm(x))
 
 
 def spread(i, count):
@@ -80,44 +167,32 @@
 
 
 def expert_kernel(groups, *refs):
-    ins, (gate_hbm, up_hbm, down_hbm) = refs[:groups], refs[groups:groups + 3]
+    ins, (gate_ref, up_ref, down_ref) = refs[:groups], refs[groups:groups + 3]
     mine_ref, theirs_ref = refs[groups + 3:groups + 5]
-    gate_ref, up_ref, down_ref, rows_ref, tail_ref, acc_ref, sems = refs[groups + 5:]
+    rows_ref, tail_ref, acc_ref = refs[groups + 5:]
     features, units = gate_ref.shape
     tail = features // SUB
     top = tail_ref.shape[0]
     count = top // SUB
     wide = 2 * tail
-    copies = []
-    for k in range(FOLD):
-        rows = pl.ds(k * wide, wide)
-        for ref, to in ((gate_hbm, gate_ref), (up_hbm, up_ref)):
-            copies.append(pltpu.make_async_copy(ref.at[rows], to.at[rows], sems.at[len(copies)]))
-    for k in range(FOLD):
-        columns = pl.ds(k * wide, wide)
-        copies.append(pltpu.make_async_copy(down_hbm.at[:, columns], down_ref.at[:, columns], sems.at[len(copies)]))
-    for copy in copies:
-        copy.start()
     start = 0
     for ref in ins:
-        rows = slice(start, start + ref.shape[0])
+        rows = slice(start, start + SUB)
         rows_ref[rows, :] = ref[:, :features]
         tail_ref[rows, :] = ref[:, features:]
-        start += ref.shape[0]
+        start += SUB
     folded = tail_ref[...]
     for i in range(SUB):
         rows_ref[top:, i * tail:(i + 1) * tail] = dot(spread(i, count), folded).astype(bf16)
     for k in range(FOLD):
         at = slice(k * wide, (k + 1) * wide)
         for n, ref in enumerate((gate_ref, up_ref)):
-            copies[2 * k + n].wait()
             columns = slice(n * units, (n + 1) * units)
             product = dot(rows_ref[:, at], ref[at, :])
             acc_ref[:, columns] = product if k == 0 else acc_ref[:, columns] + product
     hidden = (jax.nn.silu(acc_ref[:, :units]) * acc_ref[:, units:]).astype(bf16)
     folded = jnp.zeros((top, tail), f32)
     for k in range(FOLD):
-        copies[2 * FOLD + k].wait()
         at = slice(k * wide, (k + 1) * wide)
         part = dot(hidden, down_ref[:, at]).astype(bf16)
         mine_ref[:, at] = part[:top // 2]
@@ -137,18 +212,14 @@
     return pl.pallas_call(
         functools.partial(expert_kernel, len(groups)),
         out_shape=[jax.ShapeDtypeStruct((top // 2, wide), bf16)] * 2,
-        in_specs=[VMEM] * len(groups) + [pl.BlockSpec(memory_space=pltpu.HBM)] * 3,
+        in_specs=[VMEM] * (len(groups) + 3),
         out_specs=[VMEM] * 2,
         scratch_shapes=[
-            pltpu.VMEM(gate_weight.shape, bf16),
-            pltpu.VMEM(up_weight.shape, bf16),
-            pltpu.VMEM(down_weight.shape, bf16),
             pltpu.VMEM((rows, features), bf16),
             pltpu.VMEM((top, features // SUB), bf16),
             pltpu.VMEM((rows, 2 * units), f32),
-            pltpu.SemaphoreType.DMA((3 * FOLD,)),
         ],
-        compiler_params=pltpu.CompilerParams(vmem_limit_bytes=36 * MIB),
+        compiler_params=pltpu.CompilerParams(vmem_limit_bytes=14 * MIB),
         cost_estimate=pl.CostEstimate(
             flops=6 * rows * features * units, bytes_accessed=6 * features * units, transcendentals=0
         ),
@@ -158,7 +229,8 @@
 
 def add_kernel(a_ref, b_ref, *outs):
     for m, out in enumerate(outs):
-        rows = slice(m * SUB, (m + 1) * SUB)
+        start = PLACED.index(m) * SUB
+        rows = slice(start, start + SUB)
         out[...] = (a_ref[rows, :].astype(f32) + b_ref[rows, :].astype(f32)).astype(bf16)
 
 
@@ -174,14 +246,14 @@
 
 
 def combine_kernel(chip_ref, ids_ref, scores_ref, *refs):
-    ins, out_ref, rows_ref = refs[:EXPERTS], refs[EXPERTS], refs[EXPERTS + 1]
+    *ins, out_ref, rows_ref = refs
     features = out_ref.shape[1]
     tail = features // SUB
     hit, slot, first, q = routing(ids_ref[...], chip_ref[0])
     scores = scores_ref[...]
     weight = route_factor * scores / (scores[0:1, :] + scores[1:2, :])
     weight = jnp.where(first, weight[0:1, :], weight[1:2, :])
-    for m, ref in zip(ORDER + (0,), ins):
+    for m, ref in zip(BACK, ins):
         rows_ref[m * SUB:(m + 1) * SUB, :] = ref[...]
 
     def weighted(mask, values):
@@ -202,7 +274,7 @@
     return pl.pallas_call(
         combine_kernel,
         out_shape=jax.ShapeDtypeStruct((ids.shape[1], features), bf16),
-        in_specs=[pl.BlockSpec(memory_space=pltpu.SMEM)] + [VMEM] * (2 + EXPERTS),
+        in_specs=[pl.BlockSpec(memory_space=pltpu.SMEM)] + [VMEM] * (2 + len(buffers)),
         out_specs=VMEM,
         scratch_shapes=[pltpu.VMEM((EXPERTS * SUB, features + features // SUB), bf16)],
         compiler_params=pltpu.CompilerParams(vmem_limit_bytes=12 * MIB),
@@ -219,30 +291,30 @@
     members = lax.axis_size("attn")
     chip = (lax.axis_index("attn") // 2).astype(jnp.int32).reshape(1)
     ids, scores = expert_ids.T, route_scores.T
-    weights = [
-        pltpu.with_memory_space_constraint(w, pltpu.HBM) for w in (gate_weight, up_weight, down_weight)
-    ]
-    probs, finish = attention
 
     def sibling(value):
         return lax.ppermute(value, "attn", [(i, i ^ 1) for i in range(members)])
 
-    def exchange(sent):
+    def across(value, m):
+        return lax.ppermute(value, "attn", [(i, i ^ (2 * m)) for i in range(members)])
+
+    def exchange(sent, *before):
         got = {0: sent[0]}
-        for m in ORDER:
-            got[m] = lax.ppermute(sent[m], "attn", [(i, i ^ (2 * m)) for i in range(members)])
+        for m in (7, 6, 5, 1, 2, 4, 3):
+            value = after(sent[m], got[5 - m], *before) if m in (4, 3) else sent[m]
+            got[m] = across(value, m)
         return got
 
     got = exchange(pack(chip, ids, moe_input))
-    order = (0,) + ORDER[FOLD:] + ORDER[:FOLD]
-    first = jnp.concatenate([got[m] for m in order[:FOLD]], axis=0)
-    second = jnp.concatenate([got[m] for m in order[FOLD:]], axis=0)
-    second = after(second, probs)
-    mine, theirs = experts([first, second, sibling(first), sibling(second)], *weights)
+    *weights, token = load(gate_weight, up_weight, down_weight)
+    weights = [in_vmem(w) for w in weights]
+    got = [after(got[m], token) if m in (3, 4, 5, 6, 7) else got[m] for m in PLACED]
+    theirs = [sibling(value) for value in got]
+    mine, theirs = experts(got + theirs, *weights)
     total = add(mine, sibling(theirs))
-    attn_output = finish(after(probs, *total))
-    back = exchange({m: total[place] for place, m in enumerate(order)})
-    moe_output = combine(chip, ids, scores, [back[m] for m in ORDER + (0,)], features)
+    attn_output = attend_by_sequence(*attention[:4], after(attention[4], *total))
+    back = exchange(total, attn_output)
+    moe_output = combine(chip, ids, scores, [back[m] for m in BACK], features)
     return moe_output, attn_output
 
 
@@ -295,8 +367,7 @@
     values = expert_out.reshape(EXPERTS * CAP, features)[place].astype(jnp.float32)
     values = values.reshape(token_count, picks, features)
     moe_output = jnp.sum(values * combine_weight[:, :, None], axis=1).astype(jnp.bfloat16)
-    probs, finish = attention
-    return moe_output, finish(probs)
+    return moe_output, attend(*attention)
 
 
 def attend(q_latent, q_rope, latent_cache, rope_cache, cache_lengths):
@@ -321,12 +392,8 @@
     largest = jnp.max(scores, axis=-1, keepdims=True)
     weights = jnp.exp(scores - largest)
     probs = (weights / jnp.sum(weights, axis=-1, keepdims=True)).astype(jnp.bfloat16)
-
-    def finish(probs):
-        attn = jnp.einsum("bthp,bpc->bthc", probs, latent_cache, preferred_element_type=jnp.float32)
-        return attn.astype(jnp.bfloat16).reshape(seq_count, step_count, head_count * latent_width)
-
-    return probs, finish
+    attn = jnp.einsum("bthp,bpc->bthc", probs, latent_cache, preferred_element_type=jnp.float32)
+    return attn.astype(jnp.bfloat16).reshape(seq_count, step_count, head_count * latent_width)
 
 
 def body(
@@ -343,7 +410,7 @@
     cache_lengths,
 ):
     moe = moe_by_chips if lax.axis_size("attn") == 2 * EXPERTS else moe_by_slots
-    attention = attend(q_latent, q_rope, latent_cache, rope_cache, cache_lengths)
+    attention = q_latent, q_rope, latent_cache, rope_cache, cache_lengths
     return moe(moe_input, expert_ids, route_scores, gate_weight, up_weight, down_weight, attention)
 
 

time: 77.7 us -> 73.5 us (0.946)
  Pallas kernels: 11 us -> 24.2 us
  local copies, waits for them, and re-layouts: 10.8 us -> 0.01 us
  waiting for transfers between devices: 8.56 us -> 19.3 us
  matrix products: 7.82 us -> 0 us
  starting transfers between devices: 37 us -> 29.2 us
  other arithmetic: 1.28 us -> 0 us
    pallas_call x0 -> x2, Pallas kernels: none -> 15.8 us  [the longest x1 7.94 us: attend_by_sequence(): pl.pallas_call(attend_kernel, out_shape=jax.ShapeDtypeStruct(q_latent.sha...]
    ppermute x14, waiting for transfers between devices: 3.93 us -> 16 us  [across(): return lax.ppermute(value, 'attn', [(i, i ^ 2 * m) for i in range(members)])]
    ppermute x14, starting transfers between devices: 36.3 us -> 26.6 us  [across(): return lax.ppermute(value, 'attn', [(i, i ^ 2 * m) for i in range(members)])]
    reshape x3 -> x0, local copies, waits for them, and re-layouts: 8.98 us -> none  [the longest x1 3.87 us: finish(): attn.astype(jnp.bfloat16)]
    dot_general x2 -> x0, matrix products: 4.16 us -> none  [the longest x1 2.42 us: attend(): jnp.einsum('bthc,bpc->bthp', query_rot, rope_cache, preferred_element_typ...]
    pallas_call x1, Pallas kernels: 8.46 us -> 4.78 us  [experts(): pl.pallas_call(functools.partial(expert_kernel, len(groups)), out_shape=[...]
    div x1 -> x0, matrix products: 3.66 us -> none  [attend(): weights / jnp.sum(weights, axis=-1, keepdims=True)]
    unnamed x17 -> x6, local copies, waits for them, and re-layouts: 1.83 us -> 0.01 us
  transfers between devices with their start and end apart: 17 -> 23, of which waited for: 7 -> 9; matrix products, arithmetic and copies ran while one was open for 23% -> 0% of each run, Pallas kernels for 0% -> 22%
where the time goes in v5:
time: 73.5 us; the launch traced here: 73.4 us
  starting transfers between devices  29.2 us (40%)
  Pallas kernels  24.2 us (33%)
  waiting for transfers between devices  19.3 us (26%)
    ppermute x14, starting transfers between devices, across(): return lax.ppermute(value, 'attn', [(i, i ^ 2 * m) for i in range(members)])  26.6 us
    ppermute x14, waiting for transfers between devices, across(): return lax.ppermute(value, 'attn', [(i, i ^ 2 * m) for i in range(members)])  16 us
    pallas_call x1, Pallas kernels, attend_by_sequence(): pl.pallas_call(attend_kernel, out_shape=jax.ShapeDtypeStruct(q_latent.sha...  7.94 us
    pallas_call x1, Pallas kernels, load(): pl.pallas_call(load_kernel, out_shape=[pltpu.VMEM(w.shape, w.dtype) for w...  7.88 us
    pallas_call x1, Pallas kernels, experts(): pl.pallas_call(functools.partial(expert_kernel, len(groups)), out_shape=[...  4.78 us
    ppermute x9, waiting for transfers between devices, sibling(): return lax.ppermute(value, 'attn', [(i, i ^ 1) for i in range(members)])  3.32 us
    ppermute x9, starting transfers between devices, sibling(): return lax.ppermute(value, 'attn', [(i, i ^ 1) for i in range(members)])  2.52 us
    pallas_call x1, Pallas kernels, pack(): pl.pallas_call(pack_kernel, out_shape=[jax.ShapeDtypeStruct((SUB, feature...  1.74 us
  transfers between devices with their start and end apart: 23, of which 9 were waited for; matrix products, arithmetic and copies ran while one was open for 0% of the time, Pallas kernels for 22%

profile of v5, /device:TPU:0, one launch (start us, length us, event | category | flops | bytes accessed | tf_op | source)
XLA Modules:
  0.0 73.4 jit_solution(467596010454093141)
XLA Ops:
  0.6 1.7 %pack.1 = (bf16[8,8064]{1,0:T(8,128)(2,1)S(1)}, bf16[8,8064]{1,0:T(8,128)(2,1)S(1)}, bf16[8,8064]{1,0:T(8,128)(2,1)S(1)}, bf16[8,8064]{1,0:T(8,128)(2,1)S(1)}, b...) custom-call(s32[1]{0:T(128)} %bitcast.chip_ref, ...), custom_call_target="tpu_custom_call" | custom-call | tf_op jit(solution)/shard_map/pack/pallas_call | solution.py:153
  2.4 3.0 %collective-permute-start = (bf16[8,8064]{1,0:T(8,128)(2,1)S(1)}, bf16[8,8064]{1,0:T(8,128)(2,1)S(1)}, u32[]{:S(2)}, u32[]{:S(2)}) collective-permute-start(bf16[8,8064]{1,0:T(8,128)(2,1)S(1)} %get-tuple-element.35), channel_id=1, source_target_pairs={{0,2},{1,3},{2,0},{3,1},{4,6},{5,7},{6,4},{7,5},{8,10},{9,11},{10,... | collective-permute-start | bytes 387080 | tf_op jit(solution)/shard_map/ppermute | solution.py:299
  5.4 1.6 %collective-permute-start.1 = (bf16[8,8064]{1,0:T(8,128)(2,1)S(1)}, bf16[8,8064]{1,0:T(8,128)(2,1)S(1)}, u32[]{:S(2)}, u32[]{:S(2)}) collective-permute-start(bf16[8,8064]{1,0:T(8,128)(2,1)S(1)} %get-tuple-element.36), channel_id=1, source_target_pairs={{0,4},{1,5},{2,6},{3,7},{4,0},{5,1},{6,2},{7,3},{8,12},{9,13},{10,... | collective-permute-start | bytes 387080 | tf_op jit(solution)/shard_map/ppermute | solution.py:299
  7.0 2.5 %collective-permute-start.4 = (bf16[8,8064]{1,0:T(8,128)(2,1)S(1)}, bf16[8,8064]{1,0:T(8,128)(2,1)S(1)}, u32[]{:S(2)}, u32[]{:S(2)}) collective-permute-start(bf16[8,8064]{1,0:T(8,128)(2,1)S(1)} %get-tuple-element.44), channel_id=1, source_target_pairs={{0,10},{1,11},{2,8},{3,9},{4,14},{5,15},{6,12},{7,13},{8,2},{9,3},... | collective-permute-start | bytes 387080 | tf_op jit(solution)/shard_map/ppermute | solution.py:299
  9.5 4.8 %collective-permute-start.6 = (bf16[8,8064]{1,0:T(8,128)(2,1)S(1)}, bf16[8,8064]{1,0:T(8,128)(2,1)S(1)}, u32[]{:S(2)}, u32[]{:S(2)}) collective-permute-start(bf16[8,8064]{1,0:T(8,128)(2,1)S(1)} %get-tuple-element.48), channel_id=1, source_target_pairs={{0,14},{1,15},{2,12},{3,13},{4,10},{5,11},{6,8},{7,9},{8,6},{9,7},... | collective-permute-start | bytes 387080 | tf_op jit(solution)/shard_map/ppermute | solution.py:299
  14.3 1.3 %collective-permute-start.2 = (bf16[8,8064]{1,0:T(8,128)(2,1)S(1)}, bf16[8,8064]{1,0:T(8,128)(2,1)S(1)}, u32[]{:S(2)}, u32[]{:S(2)}) collective-permute-start(bf16[8,8064]{1,0:T(8,128)(2,1)S(1)} %get-tuple-element.38), channel_id=1, source_target_pairs={{0,6},{1,7},{2,4},{3,5},{4,2},{5,3},{6,0},{7,1},{8,14},{9,15},{10,... | collective-permute-start | bytes 387080 | tf_op jit(solution)/shard_map/ppermute | solution.py:299
  15.7 9.9 %collective-permute-done.4.refs_5_ = bf16[8,8064]{1,0:T(8,128)(2,1)S(1)} collective-permute-done((bf16[8,8064]{1,0:T(8,128)(2,1)S(1)}, bf16[8,8064]{1,0:T(8,128)(2,1)S(1)}, u32[]{:S(2)}, u32[]{:S(2)}) %collective-permute-start.4) | collective-permute-done | bytes 129056 | tf_op jit(solution)/shard_map/ppermute | solution.py:299
  25.5 0.5 collective-permute-start.8
  26.1 7.9 %load.1 = (bf16[7168,512]{1,0:T(8,128)(2,1)S(1)}, bf16[7168,512]{1,0:T(8,128)(2,1)S(1)}, bf16[512,7168]{1,0:T(8,128)(2,1)S(1)}, f32[8,128]{1,0:T(8,128)}) custom-call(bf16[7168,512]{1,0:T(8,128)(2,1)} %refs_0_.1, bf16[7168,512]{1,0:T(8,128)(2,1)} %refs_1_.1, bf16[512,7168]{1,0:T(8,128)(2,1)} %refs_2_.1), custom_call_target="tpu_custom_call" | custom-call | bytes 22020096 | tf_op jit(solution)/shard_map/load/pallas_call | solution.py:122
  34.0 0.5 collective-permute-start.12
  34.6 0.4 collective-permute-start.14
  35.1 0.4 collective-permute-start.11
  36.6 4.8 %experts.1 = (bf16[64,8064]{1,0:T(8,128)(2,1)S(1)}, bf16[64,8064]{1,0:T(8,128)(2,1)S(1)}) custom-call(bf16[8,8064]{1,0:T(8,128)(2,1)S(1)} %get-tuple-element.34.refs_0_, bf16[8,8064]{1,0:T(8,128)(2,1)S(1)} %collective-permute-done.refs_1_, bf16[8,8064]{1,0:T(8,128)(2,1)S(1)} %collective-permute-done.1.refs_2_, ...), custom_call_target="tpu_custom_call" | custom-call | flops 3170893824 | bytes 22020096 | tf_op jit(solution)/shard_map/experts/pallas_call | solution.py:212
  41.8 2.3 %collective-permute-done.15.b_ref = bf16[64,8064]{1,0:T(8,128)(2,1)S(1)} collective-permute-done((bf16[64,8064]{1,0:T(8,128)(2,1)S(1)}, bf16[64,8064]{1,0:T(8,128)(2,1)S(1)}, u32[]{:S(2)}, u32[]{:S(2)}) %collective-permute-start.15) | collective-permute-done | bytes 1032224 | tf_op jit(solution)/shard_map/ppermute | solution.py:296
  44.3 2.9 %collective-permute-start.16 = (bf16[8,8064]{1,0:T(8,128)(2,1)S(1)}, bf16[8,8064]{1,0:T(8,128)(2,1)S(1)}, u32[]{:S(2)}, u32[]{:S(2)}) collective-permute-start(bf16[8,8064]{1,0:T(8,128)(2,1)S(1)} %get-tuple-element.55), channel_id=1, source_target_pairs={{0,14},{1,15},{2,12},{3,13},{4,10},{5,11},{6,8},{7,9},{8,6},{9,7},... | collective-permute-start | bytes 387080 | tf_op jit(solution)/shard_map/ppermute | solution.py:299
  47.2 1.4 %collective-permute-start.17 = (bf16[8,8064]{1,0:T(8,128)(2,1)S(1)}, bf16[8,8064]{1,0:T(8,128)(2,1)S(1)}, u32[]{:S(2)}, u32[]{:S(2)}) collective-permute-start(bf16[8,8064]{1,0:T(8,128)(2,1)S(1)} %get-tuple-element.56), channel_id=1, source_target_pairs={{0,12},{1,13},{2,14},{3,15},{4,8},{5,9},{6,10},{7,11},{8,4},{9,5},... | collective-permute-start | bytes 387080 | tf_op jit(solution)/shard_map/ppermute | solution.py:299
  48.6 5.5 %collective-permute-start.18 = (bf16[8,8064]{1,0:T(8,128)(2,1)S(1)}, bf16[8,8064]{1,0:T(8,128)(2,1)S(1)}, u32[]{:S(2)}, u32[]{:S(2)}) collective-permute-start(bf16[8,8064]{1,0:T(8,128)(2,1)S(1)} %get-tuple-element.57), channel_id=1, source_target_pairs={{0,10},{1,11},{2,8},{3,9},{4,14},{5,15},{6,12},{7,13},{8,2},{9,3},... | collective-permute-start | bytes 387080 | tf_op jit(solution)/shard_map/ppermute | solution.py:299
  54.1 0.7 collective-permute-start.19
  54.8 7.9 %attend.1 = bf16[6,4,32768]{2,1,0:T(4,128)(2,1)} custom-call(s32[6]{0:T(128)S(1)} %copy-done.2, bf16[6,4,32768]{2,1,0:T(4,128)(2,1)} %q_ref.1, bf16[6,4,4096]{2,1,0:T(4,128)(2,1)} %q_rope_ref.1, bf16[6,256,512]{2,1,0:T(8,128)(2,1)} %latent_ref.1, bf16[6,64,256]{2,1,0:T(8,128)(2,1)} %bitcast.7), custom_call_target="tpu_custom_call" | custom-call | flops 6442450944 | bytes 4718592 | tf_op jit(solution)/shard_map/attend/pallas_call | solution.py:94
  62.8 2.0 %collective-permute-start.20 = (bf16[8,8064]{1,0:T(8,128)(2,1)S(1)}, bf16[8,8064]{1,0:T(8,128)(2,1)S(1)}, u32[]{:S(2)}, u32[]{:S(2)}) collective-permute-start(bf16[8,8064]{1,0:T(8,128)(2,1)S(1)} %get-tuple-element.64), channel_id=1, source_target_pairs={{0,8},{1,9},{2,10},{3,11},{4,12},{5,13},{6,14},{7,15},{8,0},{9,1},... | collective-permute-start | bytes 387080 | tf_op jit(solution)/shard_map/ppermute | solution.py:299
  64.7 0.9 %collective-permute-start.22 = (bf16[8,8064]{1,0:T(8,128)(2,1)S(1)}, bf16[8,8064]{1,0:T(8,128)(2,1)S(1)}, u32[]{:S(2)}, u32[]{:S(2)}) collective-permute-start(bf16[8,8064]{1,0:T(8,128)(2,1)S(1)} %get-tuple-element.65), channel_id=1, source_target_pairs={{0,6},{1,7},{2,4},{3,5},{4,2},{5,3},{6,0},{7,1},{8,14},{9,15},{10,... | collective-permute-start | bytes 387080 | tf_op jit(solution)/shard_map/ppermute | solution.py:299
  65.7 1.0 %collective-permute-done.18.refs_2_ = bf16[8,8064]{1,0:T(8,128)(2,1)S(1)} collective-permute-done((bf16[8,8064]{1,0:T(8,128)(2,1)S(1)}, bf16[8,8064]{1,0:T(8,128)(2,1)S(1)}, u32[]{:S(2)}, u32[]{:S(2)}) %collective-permute-start.18) | collective-permute-done | bytes 129056 | tf_op jit(solution)/shard_map/ppermute | solution.py:299
  66.7 5.0 %collective-permute-done.20.refs_3_ = bf16[8,8064]{1,0:T(8,128)(2,1)S(1)} collective-permute-done((bf16[8,8064]{1,0:T(8,128)(2,1)S(1)}, bf16[8,8064]{1,0:T(8,128)(2,1)S(1)}, u32[]{:S(2)}, u32[]{:S(2)}) %collective-permute-start.20) | collective-permute-done | bytes 129056 | tf_op jit(solution)/shard_map/ppermute | solution.py:299
  71.7 1.6 %combine.1 = bf16[24,7168]{1,0:T(8,128)(2,1)} custom-call(s32[1]{0:T(128)} %bitcast.chip_ref, s32[2,24]{1,0:T(2,128)S(1)} %bitcast.5, f32[2,24]{1,0:T(2,128)S(1)} %bitcast.6, bf16[8,8064]{1,0:T(8,128)(2,1)S(1)} %collective-permute-done.16.refs_0_, bf16[8,8064]{1,0:T(8,128)(2,1)S(1)} %collective-permute-done.17.refs_1_, ...), custom_call_target="tpu_custom_call" | custom-call | tf_op jit(solution)/shard_map/combine/pallas_call | solution.py:274
  (34 shorter events, 2.0 us)
Async XLA Ops:
  2.4 11.9 %collective-permute-start = (bf16[8,8064]{1,0:T(8,128)(2,1)S(1)}, bf16[8,8064]{1,0:T(8,128)(2,1)S(1)}, u32[]{:S(2)}, u32[]{:S(2)}) collective-permute-start(bf16[8,8064]{1,0:T(8,128)(2,1)S(1)} %get-tuple-element.35), channel_id=1, source_target_pairs={{0,2},{1,3},{2,0},{3,1},{4,6},{5,7},{6,4},{7,5},{8,10},{9,11},{10,... | collective-permute-start | bytes 387080 | tf_op jit(solution)/shard_map/ppermute | solution.py:299
  5.4 8.9 %collective-permute-start.1 = (bf16[8,8064]{1,0:T(8,128)(2,1)S(1)}, bf16[8,8064]{1,0:T(8,128)(2,1)S(1)}, u32[]{:S(2)}, u32[]{:S(2)}) collective-permute-start(bf16[8,8064]{1,0:T(8,128)(2,1)S(1)} %get-tuple-element.36), channel_id=1, source_target_pairs={{0,4},{1,5},{2,6},{3,7},{4,0},{5,1},{6,2},{7,3},{8,12},{9,13},{10,... | collective-permute-start | bytes 387080 | tf_op jit(solution)/shard_map/ppermute | solution.py:299
  7.0 18.5 %collective-permute-start.4 = (bf16[8,8064]{1,0:T(8,128)(2,1)S(1)}, bf16[8,8064]{1,0:T(8,128)(2,1)S(1)}, u32[]{:S(2)}, u32[]{:S(2)}) collective-permute-start(bf16[8,8064]{1,0:T(8,128)(2,1)S(1)} %get-tuple-element.44), channel_id=1, source_target_pairs={{0,10},{1,11},{2,8},{3,9},{4,14},{5,15},{6,12},{7,13},{8,2},{9,3},... | collective-permute-start | bytes 387080 | tf_op jit(solution)/shard_map/ppermute | solution.py:299
  9.5 16.0 %collective-permute-start.5 = (bf16[8,8064]{1,0:T(8,128)(2,1)S(1)}, bf16[8,8064]{1,0:T(8,128)(2,1)S(1)}, u32[]{:S(2)}, u32[]{:S(2)}) collective-permute-start(bf16[8,8064]{1,0:T(8,128)(2,1)S(1)} %get-tuple-element.46), channel_id=1, source_target_pairs={{0,12},{1,13},{2,14},{3,15},{4,8},{5,9},{6,10},{7,11},{8,4},{9,5},... | collective-permute-start | bytes 387080 | tf_op jit(solution)/shard_map/ppermute | solution.py:299
  9.5 16.5 %collective-permute-start.6 = (bf16[8,8064]{1,0:T(8,128)(2,1)S(1)}, bf16[8,8064]{1,0:T(8,128)(2,1)S(1)}, u32[]{:S(2)}, u32[]{:S(2)}) collective-permute-start(bf16[8,8064]{1,0:T(8,128)(2,1)S(1)} %get-tuple-element.48), channel_id=1, source_target_pairs={{0,14},{1,15},{2,12},{3,13},{4,10},{5,11},{6,8},{7,9},{8,6},{9,7},... | collective-permute-start | bytes 387080 | tf_op jit(solution)/shard_map/ppermute | solution.py:299
  14.3 19.7 %collective-permute-start.3 = (bf16[8,8064]{1,0:T(8,128)(2,1)S(1)}, bf16[8,8064]{1,0:T(8,128)(2,1)S(1)}, u32[]{:S(2)}, u32[]{:S(2)}) collective-permute-start(bf16[8,8064]{1,0:T(8,128)(2,1)S(1)} %get-tuple-element.42), channel_id=1, source_target_pairs={{0,8},{1,9},{2,10},{3,11},{4,12},{5,13},{6,14},{7,15},{8,0},{9,1},... | collective-permute-start | bytes 387080 | tf_op jit(solution)/shard_map/ppermute | solution.py:299
  14.3 20.2 %collective-permute-start.2 = (bf16[8,8064]{1,0:T(8,128)(2,1)S(1)}, bf16[8,8064]{1,0:T(8,128)(2,1)S(1)}, u32[]{:S(2)}, u32[]{:S(2)}) collective-permute-start(bf16[8,8064]{1,0:T(8,128)(2,1)S(1)} %get-tuple-element.38), channel_id=1, source_target_pairs={{0,6},{1,7},{2,4},{3,5},{4,2},{5,3},{6,0},{7,1},{8,14},{9,15},{10,... | collective-permute-start | bytes 387080 | tf_op jit(solution)/shard_map/ppermute | solution.py:299
  25.5 9.1 %collective-permute-start.7 = (bf16[8,8064]{1,0:T(8,128)(2,1)S(1)}, bf16[8,8064]{1,0:T(8,128)(2,1)S(1)}, u32[]{:S(2)}, u32[]{:S(2)}) collective-permute-start(bf16[8,8064]{1,0:T(8,128)(2,1)S(1)} %get-tuple-element.34.refs_0_), channel_id=1, source_target_pairs={{0,1},{1,0},{2,3},{3,2},{4,5},{5,4},{6,7},{7,6},{8,9},{9,8},{10,11... | collective-permute-start | bytes 387080 | tf_op jit(solution)/shard_map/ppermute | solution.py:296
  25.5 9.5 %collective-permute-start.8 = (bf16[8,8064]{1,0:T(8,128)(2,1)S(1)}, bf16[8,8064]{1,0:T(8,128)(2,1)S(1)}, u32[]{:S(2)}, u32[]{:S(2)}) collective-permute-start(bf16[8,8064]{1,0:T(8,128)(2,1)S(1)} %collective-permute-done.refs_1_), channel_id=1, source_target_pairs={{0,1},{1,0},{2,3},{3,2},{4,5},{5,4},{6,7},{7,6},{8,9},{9,8},{10,11... | collective-permute-start | bytes 387080 | tf_op jit(solution)/shard_map/ppermute | solution.py:296
  26.1 9.1 %collective-permute-start.9 = (bf16[8,8064]{1,0:T(8,128)(2,1)S(1)}, bf16[8,8064]{1,0:T(8,128)(2,1)S(1)}, u32[]{:S(2)}, u32[]{:S(2)}) collective-permute-start(bf16[8,8064]{1,0:T(8,128)(2,1)S(1)} %collective-permute-done.1.refs_2_), channel_id=1, source_target_pairs={{0,1},{1,0},{2,3},{3,2},{4,5},{5,4},{6,7},{7,6},{8,9},{9,8},{10,11... | collective-permute-start | bytes 387080 | tf_op jit(solution)/shard_map/ppermute | solution.py:296
  34.0 1.5 %collective-permute-start.12 = (bf16[8,8064]{1,0:T(8,128)(2,1)S(1)}, bf16[8,8064]{1,0:T(8,128)(2,1)S(1)}, u32[]{:S(2)}, u32[]{:S(2)}) collective-permute-start(bf16[8,8064]{1,0:T(8,128)(2,1)S(1)} %collective-permute-done.4.refs_5_), channel_id=1, source_target_pairs={{0,1},{1,0},{2,3},{3,2},{4,5},{5,4},{6,7},{7,6},{8,9},{9,8},{10,11... | collective-permute-start | bytes 387080 | tf_op jit(solution)/shard_map/ppermute | solution.py:296
  34.5 1.3 %collective-permute-start.13 = (bf16[8,8064]{1,0:T(8,128)(2,1)S(1)}, bf16[8,8064]{1,0:T(8,128)(2,1)S(1)}, u32[]{:S(2)}, u32[]{:S(2)}) collective-permute-start(bf16[8,8064]{1,0:T(8,128)(2,1)S(1)} %collective-permute-done.5.refs_6_), channel_id=1, source_target_pairs={{0,1},{1,0},{2,3},{3,2},{4,5},{5,4},{6,7},{7,6},{8,9},{9,8},{10,11... | collective-permute-start | bytes 387080 | tf_op jit(solution)/shard_map/ppermute | solution.py:296
  34.6 1.4 %collective-permute-start.14 = (bf16[8,8064]{1,0:T(8,128)(2,1)S(1)}, bf16[8,8064]{1,0:T(8,128)(2,1)S(1)}, u32[]{:S(2)}, u32[]{:S(2)}) collective-permute-start(bf16[8,8064]{1,0:T(8,128)(2,1)S(1)} %collective-permute-done.6.refs_7_), channel_id=1, source_target_pairs={{0,1},{1,0},{2,3},{3,2},{4,5},{5,4},{6,7},{7,6},{8,9},{9,8},{10,11... | collective-permute-start | bytes 387080 | tf_op jit(solution)/shard_map/ppermute | solution.py:296
  35.0 1.3 %collective-permute-start.10 = (bf16[8,8064]{1,0:T(8,128)(2,1)S(1)}, bf16[8,8064]{1,0:T(8,128)(2,1)S(1)}, u32[]{:S(2)}, u32[]{:S(2)}) collective-permute-start(bf16[8,8064]{1,0:T(8,128)(2,1)S(1)} %collective-permute-done.2.refs_3_), channel_id=1, source_target_pairs={{0,1},{1,0},{2,3},{3,2},{4,5},{5,4},{6,7},{7,6},{8,9},{9,8},{10,11... | collective-permute-start | bytes 387080 | tf_op jit(solution)/shard_map/ppermute | solution.py:296
  35.1 1.4 %collective-permute-start.11 = (bf16[8,8064]{1,0:T(8,128)(2,1)S(1)}, bf16[8,8064]{1,0:T(8,128)(2,1)S(1)}, u32[]{:S(2)}, u32[]{:S(2)}) collective-permute-start(bf16[8,8064]{1,0:T(8,128)(2,1)S(1)} %collective-permute-done.3.refs_4_), channel_id=1, source_target_pairs={{0,1},{1,0},{2,3},{3,2},{4,5},{5,4},{6,7},{7,6},{8,9},{9,8},{10,11... | collective-permute-start | bytes 387080 | tf_op jit(solution)/shard_map/ppermute | solution.py:296
  36.6 18.2 %copy-start.2 = (s32[6]{0:T(128)S(1)}, s32[6]{0:T(128)}, u32[]{:S(2)}) copy-start(s32[6]{0:T(128)} %lengths_ref) | copy-start | bytes 76
  41.4 2.7 %collective-permute-start.15 = (bf16[64,8064]{1,0:T(8,128)(2,1)S(1)}, bf16[64,8064]{1,0:T(8,128)(2,1)S(1)}, u32[]{:S(2)}, u32[]{:S(2)}) collective-permute-start(bf16[64,8064]{1,0:T(8,128)(2,1)S(1)} %get-tuple-element.54), channel_id=1, source_target_pairs={{0,1},{1,0},{2,3},{3,2},{4,5},{5,4},{6,7},{7,6},{8,9},{9,8},{10,11... | collective-permute-start | bytes 3096584 | tf_op jit(solution)/shard_map/ppermute | solution.py:296
  44.3 21.4 %collective-permute-start.16 = (bf16[8,8064]{1,0:T(8,128)(2,1)S(1)}, bf16[8,8064]{1,0:T(8,128)(2,1)S(1)}, u32[]{:S(2)}, u32[]{:S(2)}) collective-permute-start(bf16[8,8064]{1,0:T(8,128)(2,1)S(1)} %get-tuple-element.55), channel_id=1, source_target_pairs={{0,14},{1,15},{2,12},{3,13},{4,10},{5,11},{6,8},{7,9},{8,6},{9,7},... | collective-permute-start | bytes 387080 | tf_op jit(solution)/shard_map/ppermute | solution.py:299
  47.2 18.5 %collective-permute-start.17 = (bf16[8,8064]{1,0:T(8,128)(2,1)S(1)}, bf16[8,8064]{1,0:T(8,128)(2,1)S(1)}, u32[]{:S(2)}, u32[]{:S(2)}) collective-permute-start(bf16[8,8064]{1,0:T(8,128)(2,1)S(1)} %get-tuple-element.56), channel_id=1, source_target_pairs={{0,12},{1,13},{2,14},{3,15},{4,8},{5,9},{6,10},{7,11},{8,4},{9,5},... | collective-permute-start | bytes 387080 | tf_op jit(solution)/shard_map/ppermute | solution.py:299
  48.6 18.1 %collective-permute-start.18 = (bf16[8,8064]{1,0:T(8,128)(2,1)S(1)}, bf16[8,8064]{1,0:T(8,128)(2,1)S(1)}, u32[]{:S(2)}, u32[]{:S(2)}) collective-permute-start(bf16[8,8064]{1,0:T(8,128)(2,1)S(1)} %get-tuple-element.57), channel_id=1, source_target_pairs={{0,10},{1,11},{2,8},{3,9},{4,14},{5,15},{6,12},{7,13},{8,2},{9,3},... | collective-permute-start | bytes 387080 | tf_op jit(solution)/shard_map/ppermute | solution.py:299
  54.1 8.7 %collective-permute-start.19 = (bf16[8,8064]{1,0:T(8,128)(2,1)S(1)}, bf16[8,8064]{1,0:T(8,128)(2,1)S(1)}, u32[]{:S(2)}, u32[]{:S(2)}) collective-permute-start(bf16[8,8064]{1,0:T(8,128)(2,1)S(1)} %get-tuple-element.59), channel_id=1, source_target_pairs={{0,2},{1,3},{2,0},{3,1},{4,6},{5,7},{6,4},{7,5},{8,10},{9,11},{10,... | collective-permute-start | bytes 387080 | tf_op jit(solution)/shard_map/ppermute | solution.py:299
  54.8 8.0 %collective-permute-start.21 = (bf16[8,8064]{1,0:T(8,128)(2,1)S(1)}, bf16[8,8064]{1,0:T(8,128)(2,1)S(1)}, u32[]{:S(2)}, u32[]{:S(2)}) collective-permute-start(bf16[8,8064]{1,0:T(8,128)(2,1)S(1)} %get-tuple-element.61), channel_id=1, source_target_pairs={{0,4},{1,5},{2,6},{3,7},{4,0},{5,1},{6,2},{7,3},{8,12},{9,13},{10,... | collective-permute-start | bytes 387080 | tf_op jit(solution)/shard_map/ppermute | solution.py:299
  62.8 8.9 %collective-permute-start.20 = (bf16[8,8064]{1,0:T(8,128)(2,1)S(1)}, bf16[8,8064]{1,0:T(8,128)(2,1)S(1)}, u32[]{:S(2)}, u32[]{:S(2)}) collective-permute-start(bf16[8,8064]{1,0:T(8,128)(2,1)S(1)} %get-tuple-element.64), channel_id=1, source_target_pairs={{0,8},{1,9},{2,10},{3,11},{4,12},{5,13},{6,14},{7,15},{8,0},{9,1},... | collective-permute-start | bytes 387080 | tf_op jit(solution)/shard_map/ppermute | solution.py:299
  64.7 7.0 %collective-permute-start.22 = (bf16[8,8064]{1,0:T(8,128)(2,1)S(1)}, bf16[8,8064]{1,0:T(8,128)(2,1)S(1)}, u32[]{:S(2)}, u32[]{:S(2)}) collective-permute-start(bf16[8,8064]{1,0:T(8,128)(2,1)S(1)} %get-tuple-element.65), channel_id=1, source_target_pairs={{0,6},{1,7},{2,4},{3,5},{4,2},{5,3},{6,0},{7,1},{8,14},{9,15},{10,... | collective-permute-start | bytes 387080 | tf_op jit(solution)/shard_map/ppermute | solution.py:299
  (2 other events, 33.9 us)

commit v6 on v2

--- a/solution.py
+++ b/solution.py
@@ -12,7 +12,10 @@
 SUB = 8
 FOLD = SUB // 2
 MIB = 1 << 20
-ORDER = (7, 6, 5, 4, 3, 2, 1)
+ORDER = (7, 6, 5, 1, 2, 4, 3)
+GROUPED = (7, 6, 5, 4, 0, 1, 2, 3)
+BACK = (7, 6, 5, 4, 3, 2, 1, 0)
+HBM = pl.BlockSpec(memory_space=pltpu.HBM)
 VMEM = pl.BlockSpec(memory_space=pltpu.VMEM)
 
 score_factor = 192.0 ** (-0.5)
@@ -45,6 +48,60 @@
 
 def ones(mask):
     return jnp.where(mask, 1.0, jnp.zeros(mask.shape, f32)).astype(bf16)
+
+
+def in_hbm(value):
+    return pltpu.with_memory_space_constraint(value, pltpu.HBM)
+
+
+def dot_nt(a, b):
+    return lax.dot_general(a, b, (((1,), (1,)), ((), ())), preferred_element_type=f32)
+
+
+def attend_kernel(lengths_ref, q_ref, q_rope_ref, latent_ref, rope_ref, out_ref, lat_ref, rot_ref):
+    seqs, steps, _ = q_ref.shape
+    width, turned = latent_ref.shape[2], rope_ref.shape[1]
+    heads = q_ref.shape[2] // width
+
+    def one(n, carry):
+        for h in range(heads):
+            rows = slice(h * steps, (h + 1) * steps)
+            lat_ref[rows, :] = q_ref[n, :, h * width:(h + 1) * width]
+            rot_ref[rows, :] = q_rope_ref[n, :, h * turned:(h + 1) * turned]
+        latent = latent_ref[n]
+        scores = (dot_nt(lat_ref[...], latent) + dot(rot_ref[...], rope_ref[n])) * score_factor
+        row = lax.broadcasted_iota(jnp.int32, scores.shape, 0)
+        position = lax.broadcasted_iota(jnp.int32, scores.shape, 1)
+        allowed = position <= lengths_ref[n] - steps + row % steps
+        scores = jnp.where(allowed, scores, -jnp.inf)
+        weights = jnp.exp(scores - jnp.max(scores, axis=1, keepdims=True))
+        probs = (weights / jnp.sum(weights, axis=1, keepdims=True)).astype(bf16)
+        attn = dot(probs, latent).astype(bf16)
+        for h in range(heads):
+            out_ref[n, :, h * width:(h + 1) * width] = attn[h * steps:(h + 1) * steps]
+        return carry
+
+    lax.fori_loop(0, seqs, one, 0)
+
+
+def attend_by_sequence(q_latent, q_rope, latent_cache, rope_cache, lengths):
+    width, turned = latent_cache.shape[2], rope_cache.shape[2]
+    rows = q_latent.shape[2] // width * q_latent.shape[1]
+    arrays = q_latent, q_rope, latent_cache, rope_cache.transpose(0, 2, 1)
+    return pl.pallas_call(
+        attend_kernel,
+        out_shape=jax.ShapeDtypeStruct(q_latent.shape, bf16),
+        in_specs=[pl.BlockSpec(memory_space=pltpu.SMEM)] + [VMEM] * 4,
+        out_specs=VMEM,
+        scratch_shapes=[pltpu.VMEM((rows, width), bf16), pltpu.VMEM((rows, turned), bf16)],
+        compiler_params=pltpu.CompilerParams(vmem_limit_bytes=14 * MIB),
+        cost_estimate=pl.CostEstimate(
+            flops=32 * q_latent.size * latent_cache.shape[1],
+            bytes_accessed=2 * (2 * q_latent.size + latent_cache.size),
+            transcendentals=0,
+        ),
+        name="attend",
+    )(lengths, *[in_hbm(v) for v in arrays])
 
 
 def pack_kernel(chip_ref, ids_ref, x_ref, *outs):
@@ -70,7 +127,7 @@
         out_specs=[VMEM] * EXPERTS,
         compiler_params=pltpu.CompilerParams(vmem_limit_bytes=12 * MIB),
         name="pack",
-    )(chip, ids, x)
+    )(chip, in_hbm(ids), in_hbm(x))
 
 
 def spread(i, count):
@@ -137,7 +194,7 @@
     return pl.pallas_call(
         functools.partial(expert_kernel, len(groups)),
         out_shape=[jax.ShapeDtypeStruct((top // 2, wide), bf16)] * 2,
-        in_specs=[VMEM] * len(groups) + [pl.BlockSpec(memory_space=pltpu.HBM)] * 3,
+        in_specs=[VMEM] * len(groups) + [HBM] * 3,
         out_specs=[VMEM] * 2,
         scratch_shapes=[
             pltpu.VMEM(gate_weight.shape, bf16),
@@ -181,7 +238,7 @@
     scores = scores_ref[...]
     weight = route_factor * scores / (scores[0:1, :] + scores[1:2, :])
     weight = jnp.where(first, weight[0:1, :], weight[1:2, :])
-    for m, ref in zip(ORDER + (0,), ins):
+    for m, ref in zip(BACK, ins):
         rows_ref[m * SUB:(m + 1) * SUB, :] = ref[...]
 
     def weighted(mask, values):
@@ -219,30 +276,27 @@
     members = lax.axis_size("attn")
     chip = (lax.axis_index("attn") // 2).astype(jnp.int32).reshape(1)
     ids, scores = expert_ids.T, route_scores.T
-    weights = [
-        pltpu.with_memory_space_constraint(w, pltpu.HBM) for w in (gate_weight, up_weight, down_weight)
-    ]
-    probs, finish = attention
+    weights = [in_hbm(w) for w in (gate_weight, up_weight, down_weight)]
 
     def sibling(value):
         return lax.ppermute(value, "attn", [(i, i ^ 1) for i in range(members)])
 
-    def exchange(sent):
+    def exchange(sent, *first):
         got = {0: sent[0]}
         for m in ORDER:
-            got[m] = lax.ppermute(sent[m], "attn", [(i, i ^ (2 * m)) for i in range(members)])
+            value = after(sent[m], got[5 - m], *first) if m in (4, 3) else sent[m]
+            got[m] = lax.ppermute(value, "attn", [(i, i ^ (2 * m)) for i in range(members)])
         return got
 
     got = exchange(pack(chip, ids, moe_input))
-    order = (0,) + ORDER[FOLD:] + ORDER[:FOLD]
+    order = GROUPED
     first = jnp.concatenate([got[m] for m in order[:FOLD]], axis=0)
     second = jnp.concatenate([got[m] for m in order[FOLD:]], axis=0)
-    second = after(second, probs)
     mine, theirs = experts([first, second, sibling(first), sibling(second)], *weights)
     total = add(mine, sibling(theirs))
-    attn_output = finish(after(probs, *total))
-    back = exchange({m: total[place] for place, m in enumerate(order)})
-    moe_output = combine(chip, ids, scores, [back[m] for m in ORDER + (0,)], features)
+    attn_output = attend_by_sequence(*attention[:4], after(attention[4], *total))
+    back = exchange({m: total[place] for place, m in enumerate(order)}, attn_output)
+    moe_output = combine(chip, ids, scores, [back[m] for m in BACK], features)
     return moe_output, attn_output
 
 
@@ -295,8 +349,7 @@
     values = expert_out.reshape(EXPERTS * CAP, features)[place].astype(jnp.float32)
     values = values.reshape(token_count, picks, features)
     moe_output = jnp.sum(values * combine_weight[:, :, None], axis=1).astype(jnp.bfloat16)
-    probs, finish = attention
-    return moe_output, finish(probs)
+    return moe_output, attend(*attention)
 
 
 def attend(q_latent, q_rope, latent_cache, rope_cache, cache_lengths):
@@ -321,12 +374,8 @@
     largest = jnp.max(scores, axis=-1, keepdims=True)
     weights = jnp.exp(scores - largest)
     probs = (weights / jnp.sum(weights, axis=-1, keepdims=True)).astype(jnp.bfloat16)
-
-    def finish(probs):
-        attn = jnp.einsum("bthp,bpc->bthc", probs, latent_cache, preferred_element_type=jnp.float32)
-        return attn.astype(jnp.bfloat16).reshape(seq_count, step_count, head_count * latent_width)
-
-    return probs, finish
+    attn = jnp.einsum("bthp,bpc->bthc", probs, latent_cache, preferred_element_type=jnp.float32)
+    return attn.astype(jnp.bfloat16).reshape(seq_count, step_count, head_count * latent_width)
 
 
 def body(
@@ -343,7 +392,7 @@
     cache_lengths,
 ):
     moe = moe_by_chips if lax.axis_size("attn") == 2 * EXPERTS else moe_by_slots
-    attention = attend(q_latent, q_rope, latent_cache, rope_cache, cache_lengths)
+    attention = q_latent, q_rope, latent_cache, rope_cache, cache_lengths
     return moe(moe_input, expert_ids, route_scores, gate_weight, up_weight, down_weight, attention)
 
 

time: 77.7 us -> 73.1 us (0.941)
  waiting for transfers between devices: 8.56 us -> 23.7 us
  local copies, waits for them, and re-layouts: 10.8 us -> 0.13 us
  Pallas kernels: 11 us -> 20 us
  starting transfers between devices: 37 us -> 28.4 us
  matrix products: 7.82 us -> 0 us
  other arithmetic: 1.28 us -> 0 us
    ppermute x14, waiting for transfers between devices: 3.93 us -> 19.3 us  [exchange(): lax.ppermute(value, 'attn', [(i, i ^ 2 * m) for i in range(members)])]
    reshape x3 -> x0, local copies, waits for them, and re-layouts: 8.98 us -> none  [the longest x1 3.87 us: finish(): attn.astype(jnp.bfloat16)]
    ppermute x14, starting transfers between devices: 36.3 us -> 28 us  [exchange(): lax.ppermute(value, 'attn', [(i, i ^ 2 * m) for i in range(members)])]
    pallas_call x0 -> x1, Pallas kernels: none -> 7.94 us  [attend_by_sequence(): pl.pallas_call(attend_kernel, out_shape=jax.ShapeDtypeStruct(q_latent.sha...]
    dot_general x2 -> x0, matrix products: 4.16 us -> none  [the longest x1 2.42 us: attend(): jnp.einsum('bthc,bpc->bthp', query_rot, rope_cache, preferred_element_typ...]
    div x1 -> x0, matrix products: 3.66 us -> none  [attend(): weights / jnp.sum(weights, axis=-1, keepdims=True)]
    unnamed x17 -> x12, local copies, waits for them, and re-layouts: 1.83 us -> 0.1 us
    concatenate x1 -> x0, other arithmetic: 1.13 us -> none  [moe_by_chips(): second = jnp.concatenate([got[m] for m in order[FOLD:]], axis=0)]
  transfers between devices with their start and end apart: 17 -> 17, of which waited for: 7 -> 10; matrix products, arithmetic and copies ran while one was open for 23% -> 0% of each run, Pallas kernels for 0% -> 11%
where the time goes in v6:
time: 73.1 us; the launch traced here: 72.9 us
  starting transfers between devices  28.4 us (39%)
  waiting for transfers between devices  23.7 us (32%)
  Pallas kernels  20 us (27%)
  between operations  0.75 us (1%)
    ppermute x14, starting transfers between devices, exchange(): lax.ppermute(value, 'attn', [(i, i ^ 2 * m) for i in range(members)])  28 us
    ppermute x14, waiting for transfers between devices, exchange(): lax.ppermute(value, 'attn', [(i, i ^ 2 * m) for i in range(members)])  19.3 us
    pallas_call x1, Pallas kernels, experts(): pl.pallas_call(functools.partial(expert_kernel, len(groups)), out_shape=[...  8.46 us
    pallas_call x1, Pallas kernels, attend_by_sequence(): pl.pallas_call(attend_kernel, out_shape=jax.ShapeDtypeStruct(q_latent.sha...  7.94 us
    ppermute x3, waiting for transfers between devices, sibling(): return lax.ppermute(value, 'attn', [(i, i ^ 1) for i in range(members)])  4.38 us
    pallas_call x1, Pallas kernels, pack(): pl.pallas_call(pack_kernel, out_shape=[jax.ShapeDtypeStruct((SUB, feature...  1.74 us
    pallas_call x1, Pallas kernels, combine(): pl.pallas_call(combine_kernel, out_shape=jax.ShapeDtypeStruct((ids.shape[...  1.61 us
  transfers between devices with their start and end apart: 17, of which 10 were waited for; matrix products, arithmetic and copies ran while one was open for 0% of the time, Pallas kernels for 11%

profile of v6, /device:TPU:0, one launch (start us, length us, event | category | flops | bytes accessed | tf_op | source)
XLA Modules:
  0.0 72.9 jit_solution(14162209807806501823)
XLA Ops:
  0.6 1.7 %pack.1 = (bf16[8,8064]{1,0:T(8,128)(2,1)S(1)}, bf16[8,8064]{1,0:T(8,128)(2,1)S(1)}, bf16[8,8064]{1,0:T(8,128)(2,1)S(1)}, bf16[8,8064]{1,0:T(8,128)(2,1)S(1)}, b...) custom-call(s32[1]{0:T(128)} %bitcast.chip_ref, ...), custom_call_target="tpu_custom_call" | custom-call | tf_op jit(solution)/shard_map/pack/pallas_call | solution.py:123
  2.4 6.1 %collective-permute-start = (bf16[8,8064]{1,0:T(8,128)(2,1)S(1)}, bf16[8,8064]{1,0:T(8,128)(2,1)S(1)}, u32[]{:S(2)}, u32[]{:S(2)}) collective-permute-start(bf16[8,8064]{1,0:T(8,128)(2,1)S(1)} %get-tuple-element.25), channel_id=1, source_target_pairs={{0,14},{1,15},{2,12},{3,13},{4,10},{5,11},{6,8},{7,9},{8,6},{9,7},... | collective-permute-start | bytes 387080 | tf_op jit(solution)/shard_map/ppermute | solution.py:288
  8.5 0.2 collective-permute-start.1
  8.7 0.7 %collective-permute-start.2 = (bf16[8,8064]{1,0:T(8,128)(2,1)S(1)}, bf16[8,8064]{1,0:T(8,128)(2,1)S(1)}, u32[]{:S(2)}, u32[]{:S(2)}) collective-permute-start(bf16[8,8064]{1,0:T(8,128)(2,1)S(1)} %get-tuple-element.27), channel_id=1, source_target_pairs={{0,10},{1,11},{2,8},{3,9},{4,14},{5,15},{6,12},{7,13},{8,2},{9,3},... | collective-permute-start | bytes 387080 | tf_op jit(solution)/shard_map/ppermute | solution.py:288
  9.4 1.5 %collective-permute-start.3 = (bf16[8,8064]{1,0:T(8,128)(2,1)S(1)}, bf16[8,8064]{1,0:T(8,128)(2,1)S(1)}, u32[]{:S(2)}, u32[]{:S(2)}) collective-permute-start(bf16[8,8064]{1,0:T(8,128)(2,1)S(1)} %get-tuple-element.29), channel_id=1, source_target_pairs={{0,2},{1,3},{2,0},{3,1},{4,6},{5,7},{6,4},{7,5},{8,10},{9,11},{10,... | collective-permute-start | bytes 387080 | tf_op jit(solution)/shard_map/ppermute | solution.py:288
  10.9 3.4 %collective-permute-start.5 = (bf16[8,8064]{1,0:T(8,128)(2,1)S(1)}, bf16[8,8064]{1,0:T(8,128)(2,1)S(1)}, u32[]{:S(2)}, u32[]{:S(2)}) collective-permute-start(bf16[8,8064]{1,0:T(8,128)(2,1)S(1)} %get-tuple-element.32), channel_id=1, source_target_pairs={{0,4},{1,5},{2,6},{3,7},{4,0},{5,1},{6,2},{7,3},{8,12},{9,13},{10,... | collective-permute-start | bytes 387080 | tf_op jit(solution)/shard_map/ppermute | solution.py:288
  14.3 0.5 collective-permute-done.3
  14.8 1.8 %collective-permute-start.4 = (bf16[8,8064]{1,0:T(8,128)(2,1)S(1)}, bf16[8,8064]{1,0:T(8,128)(2,1)S(1)}, u32[]{:S(2)}, u32[]{:S(2)}) collective-permute-start(bf16[8,8064]{1,0:T(8,128)(2,1)S(1)} %get-tuple-element.30), channel_id=1, source_target_pairs={{0,8},{1,9},{2,10},{3,11},{4,12},{5,13},{6,14},{7,15},{8,0},{9,1},... | collective-permute-start | bytes 387080 | tf_op jit(solution)/shard_map/ppermute | solution.py:288
  16.6 4.1 %collective-permute-done.5 = bf16[8,8064]{1,0:T(8,128)(2,1)S(1)} collective-permute-done((bf16[8,8064]{1,0:T(8,128)(2,1)S(1)}, bf16[8,8064]{1,0:T(8,128)(2,1)S(1)}, u32[]{:S(2)}, u32[]{:S(2)}) %collective-permute-start.5) | collective-permute-done | bytes 129056 | tf_op jit(solution)/shard_map/ppermute | solution.py:288
  20.7 2.4 %collective-permute-start.6 = (bf16[8,8064]{1,0:T(8,128)(2,1)S(1)}, bf16[8,8064]{1,0:T(8,128)(2,1)S(1)}, u32[]{:S(2)}, u32[]{:S(2)}) collective-permute-start(bf16[8,8064]{1,0:T(8,128)(2,1)S(1)} %get-tuple-element.34), channel_id=1, source_target_pairs={{0,6},{1,7},{2,4},{3,5},{4,2},{5,3},{6,0},{7,1},{8,14},{9,15},{10,... | collective-permute-start | bytes 387080 | tf_op jit(solution)/shard_map/ppermute | solution.py:288
  23.2 5.5 %collective-permute-done.2 = bf16[8,8064]{1,0:T(8,128)(2,1)S(1)} collective-permute-done((bf16[8,8064]{1,0:T(8,128)(2,1)S(1)}, bf16[8,8064]{1,0:T(8,128)(2,1)S(1)}, u32[]{:S(2)}, u32[]{:S(2)}) %collective-permute-start.2) | collective-permute-done | bytes 129056 | tf_op jit(solution)/shard_map/ppermute | solution.py:288
  28.7 1.7 %collective-permute-done.4 = bf16[8,8064]{1,0:T(8,128)(2,1)S(1)} collective-permute-done((bf16[8,8064]{1,0:T(8,128)(2,1)S(1)}, bf16[8,8064]{1,0:T(8,128)(2,1)S(1)}, u32[]{:S(2)}, u32[]{:S(2)}) %collective-permute-start.4) | collective-permute-done | bytes 129056 | tf_op jit(solution)/shard_map/ppermute | solution.py:288
  30.6 1.8 %collective-permute-done.7.refs_2_ = bf16[32,8064]{1,0:T(8,128)(2,1)S(1)} collective-permute-done((bf16[32,8064]{1,0:T(8,128)(2,1)S(1)}, bf16[32,8064]{1,0:T(8,128)(2,1)S(1)}, u32[]{:S(2)}, u32[]{:S(2)}) %collective-permute-start.7) | collective-permute-done | bytes 516128 | tf_op jit(solution)/shard_map/ppermute | solution.py:282
  32.4 8.5 %experts.1 = (bf16[64,8064]{1,0:T(8,128)(2,1)S(1)}, bf16[64,8064]{1,0:T(8,128)(2,1)S(1)}) custom-call(bf16[32,8064]{1,0:T(8,128)(2,1)S(1)} %constant_dynamic-update-slice_fusion.refs_0_, bf16[32,8064]{1,0:T(8,128)(2,1)S(1)} %constant_dynamic-update-slice_fusion.4.refs_1_, bf16[32,8064]{1,0:T(8,128)(2,1)S(1)} %collective-permute-done.7.refs_2_, ...), custom_call_target="tpu_custom_call" | custom-call | flops 3170893824 | bytes 22020096 | tf_op jit(solution)/shard_map/experts/pallas_call | solution.py:194
  41.1 2.5 %collective-permute-done.9.b_ref = bf16[64,8064]{1,0:T(8,128)(2,1)S(1)} collective-permute-done((bf16[64,8064]{1,0:T(8,128)(2,1)S(1)}, bf16[64,8064]{1,0:T(8,128)(2,1)S(1)}, u32[]{:S(2)}, u32[]{:S(2)}) %collective-permute-start.9) | collective-permute-done | bytes 1032224 | tf_op jit(solution)/shard_map/ppermute | solution.py:282
  43.6 0.2 add.2
  43.8 5.3 %collective-permute-start.10 = (bf16[8,8064]{1,0:T(8,128)(2,1)S(1)}, bf16[8,8064]{1,0:T(8,128)(2,1)S(1)}, u32[]{:S(2)}, u32[]{:S(2)}) collective-permute-start(bf16[8,8064]{1,0:T(8,128)(2,1)S(1)} %get-tuple-element.37), channel_id=1, source_target_pairs={{0,14},{1,15},{2,12},{3,13},{4,10},{5,11},{6,8},{7,9},{8,6},{9,7},... | collective-permute-start | bytes 387080 | tf_op jit(solution)/shard_map/ppermute | solution.py:288
  49.3 0.5 collective-permute-start.13
  49.8 5.2 %collective-permute-start.15 = (bf16[8,8064]{1,0:T(8,128)(2,1)S(1)}, bf16[8,8064]{1,0:T(8,128)(2,1)S(1)}, u32[]{:S(2)}, u32[]{:S(2)}) collective-permute-start(bf16[8,8064]{1,0:T(8,128)(2,1)S(1)} %get-tuple-element.43), channel_id=1, source_target_pairs={{0,4},{1,5},{2,6},{3,7},{4,0},{5,1},{6,2},{7,3},{8,12},{9,13},{10,... | collective-permute-start | bytes 387080 | tf_op jit(solution)/shard_map/ppermute | solution.py:288
  55.0 7.9 %attend.1 = bf16[6,4,32768]{2,1,0:T(4,128)(2,1)} custom-call(s32[6]{0:T(128)S(1)} %copy-done.2, bf16[6,4,32768]{2,1,0:T(4,128)(2,1)} %q_ref.1, bf16[6,4,4096]{2,1,0:T(4,128)(2,1)} %q_rope_ref.1, bf16[6,256,512]{2,1,0:T(8,128)(2,1)} %latent_ref.1, bf16[6,64,256]{2,1,0:T(8,128)(2,1)} %bitcast.7), custom_call_target="tpu_custom_call" | custom-call | flops 6442450944 | bytes 4718592 | tf_op jit(solution)/shard_map/attend/pallas_call | solution.py:91
  63.1 0.6 collective-permute-start.16
  63.9 6.9 %collective-permute-done.14.refs_3_ = bf16[8,8064]{1,0:T(8,128)(2,1)S(1)} collective-permute-done((bf16[8,8064]{1,0:T(8,128)(2,1)S(1)}, bf16[8,8064]{1,0:T(8,128)(2,1)S(1)}, u32[]{:S(2)}, u32[]{:S(2)}) %collective-permute-start.14) | collective-permute-done | bytes 129056 | tf_op jit(solution)/shard_map/ppermute | solution.py:288
  70.8 0.5 collective-permute-done.16.refs_4_
  71.3 1.6 %combine.1 = bf16[24,7168]{1,0:T(8,128)(2,1)} custom-call(s32[1]{0:T(128)} %bitcast.chip_ref, s32[2,24]{1,0:T(2,128)S(1)} %bitcast.5, f32[2,24]{1,0:T(2,128)S(1)} %bitcast.6, bf16[8,8064]{1,0:T(8,128)(2,1)S(1)} %collective-permute-done.10.refs_0_, bf16[8,8064]{1,0:T(8,128)(2,1)S(1)} %collective-permute-done.11.refs_1_, ...), custom_call_target="tpu_custom_call" | custom-call | tf_op jit(solution)/shard_map/combine/pallas_call | solution.py:259
  (29 shorter events, 1.0 us)
Async XLA Ops:
  2.4 20.7 %collective-permute-start = (bf16[8,8064]{1,0:T(8,128)(2,1)S(1)}, bf16[8,8064]{1,0:T(8,128)(2,1)S(1)}, u32[]{:S(2)}, u32[]{:S(2)}) collective-permute-start(bf16[8,8064]{1,0:T(8,128)(2,1)S(1)} %get-tuple-element.25), channel_id=1, source_target_pairs={{0,14},{1,15},{2,12},{3,13},{4,10},{5,11},{6,8},{7,9},{8,6},{9,7},... | collective-permute-start | bytes 387080 | tf_op jit(solution)/shard_map/ppermute | solution.py:288
  8.5 14.7 %collective-permute-start.1 = (bf16[8,8064]{1,0:T(8,128)(2,1)S(1)}, bf16[8,8064]{1,0:T(8,128)(2,1)S(1)}, u32[]{:S(2)}, u32[]{:S(2)}) collective-permute-start(bf16[8,8064]{1,0:T(8,128)(2,1)S(1)} %get-tuple-element.26), channel_id=1, source_target_pairs={{0,12},{1,13},{2,14},{3,15},{4,8},{5,9},{6,10},{7,11},{8,4},{9,5},... | collective-permute-start | bytes 387080 | tf_op jit(solution)/shard_map/ppermute | solution.py:288
  8.7 19.9 %collective-permute-start.2 = (bf16[8,8064]{1,0:T(8,128)(2,1)S(1)}, bf16[8,8064]{1,0:T(8,128)(2,1)S(1)}, u32[]{:S(2)}, u32[]{:S(2)}) collective-permute-start(bf16[8,8064]{1,0:T(8,128)(2,1)S(1)} %get-tuple-element.27), channel_id=1, source_target_pairs={{0,10},{1,11},{2,8},{3,9},{4,14},{5,15},{6,12},{7,13},{8,2},{9,3},... | collective-permute-start | bytes 387080 | tf_op jit(solution)/shard_map/ppermute | solution.py:288
  9.4 5.4 %collective-permute-start.3 = (bf16[8,8064]{1,0:T(8,128)(2,1)S(1)}, bf16[8,8064]{1,0:T(8,128)(2,1)S(1)}, u32[]{:S(2)}, u32[]{:S(2)}) collective-permute-start(bf16[8,8064]{1,0:T(8,128)(2,1)S(1)} %get-tuple-element.29), channel_id=1, source_target_pairs={{0,2},{1,3},{2,0},{3,1},{4,6},{5,7},{6,4},{7,5},{8,10},{9,11},{10,... | collective-permute-start | bytes 387080 | tf_op jit(solution)/shard_map/ppermute | solution.py:288
  10.9 9.7 %collective-permute-start.5 = (bf16[8,8064]{1,0:T(8,128)(2,1)S(1)}, bf16[8,8064]{1,0:T(8,128)(2,1)S(1)}, u32[]{:S(2)}, u32[]{:S(2)}) collective-permute-start(bf16[8,8064]{1,0:T(8,128)(2,1)S(1)} %get-tuple-element.32), channel_id=1, source_target_pairs={{0,4},{1,5},{2,6},{3,7},{4,0},{5,1},{6,2},{7,3},{8,12},{9,13},{10,... | collective-permute-start | bytes 387080 | tf_op jit(solution)/shard_map/ppermute | solution.py:288
  14.8 15.6 %collective-permute-start.4 = (bf16[8,8064]{1,0:T(8,128)(2,1)S(1)}, bf16[8,8064]{1,0:T(8,128)(2,1)S(1)}, u32[]{:S(2)}, u32[]{:S(2)}) collective-permute-start(bf16[8,8064]{1,0:T(8,128)(2,1)S(1)} %get-tuple-element.30), channel_id=1, source_target_pairs={{0,8},{1,9},{2,10},{3,11},{4,12},{5,13},{6,14},{7,15},{8,0},{9,1},... | collective-permute-start | bytes 387080 | tf_op jit(solution)/shard_map/ppermute | solution.py:288
  20.7 8.0 %collective-permute-start.6 = (bf16[8,8064]{1,0:T(8,128)(2,1)S(1)}, bf16[8,8064]{1,0:T(8,128)(2,1)S(1)}, u32[]{:S(2)}, u32[]{:S(2)}) collective-permute-start(bf16[8,8064]{1,0:T(8,128)(2,1)S(1)} %get-tuple-element.34), channel_id=1, source_target_pairs={{0,6},{1,7},{2,4},{3,5},{4,2},{5,3},{6,0},{7,1},{8,14},{9,15},{10,... | collective-permute-start | bytes 387080 | tf_op jit(solution)/shard_map/ppermute | solution.py:288
  28.7 2.0 %collective-permute-start.8 = (bf16[32,8064]{1,0:T(8,128)(2,1)S(1)}, bf16[32,8064]{1,0:T(8,128)(2,1)S(1)}, u32[]{:S(2)}, u32[]{:S(2)}) collective-permute-start(bf16[32,8064]{1,0:T(8,128)(2,1)S(1)} %constant_dynamic-update-slice_fusion.4.refs_1_), channel_id=1, source_target_pairs={{0,1},{1,0},{2,3},{3,2},{4,5},{5,4},{6,7},{7,6},{8,9},{9,8},{10,11... | collective-permute-start | bytes 1548296 | tf_op jit(solution)/shard_map/ppermute | solution.py:282
  30.4 24.6 %copy-start.2 = (s32[6]{0:T(128)S(1)}, s32[6]{0:T(128)}, u32[]{:S(2)}) copy-start(s32[6]{0:T(128)} %lengths_ref) | copy-start | bytes 76
  30.5 2.0 %collective-permute-start.7 = (bf16[32,8064]{1,0:T(8,128)(2,1)S(1)}, bf16[32,8064]{1,0:T(8,128)(2,1)S(1)}, u32[]{:S(2)}, u32[]{:S(2)}) collective-permute-start(bf16[32,8064]{1,0:T(8,128)(2,1)S(1)} %constant_dynamic-update-slice_fusion.refs_0_), channel_id=1, source_target_pairs={{0,1},{1,0},{2,3},{3,2},{4,5},{5,4},{6,7},{7,6},{8,9},{9,8},{10,11... | collective-permute-start | bytes 1548296 | tf_op jit(solution)/shard_map/ppermute | solution.py:282
  40.9 2.7 %collective-permute-start.9 = (bf16[64,8064]{1,0:T(8,128)(2,1)S(1)}, bf16[64,8064]{1,0:T(8,128)(2,1)S(1)}, u32[]{:S(2)}, u32[]{:S(2)}) collective-permute-start(bf16[64,8064]{1,0:T(8,128)(2,1)S(1)} %get-tuple-element.36), channel_id=1, source_target_pairs={{0,1},{1,0},{2,3},{3,2},{4,5},{5,4},{6,7},{7,6},{8,9},{9,8},{10,11... | collective-permute-start | bytes 3096584 | tf_op jit(solution)/shard_map/ppermute | solution.py:282
  43.8 19.9 %collective-permute-start.10 = (bf16[8,8064]{1,0:T(8,128)(2,1)S(1)}, bf16[8,8064]{1,0:T(8,128)(2,1)S(1)}, u32[]{:S(2)}, u32[]{:S(2)}) collective-permute-start(bf16[8,8064]{1,0:T(8,128)(2,1)S(1)} %get-tuple-element.37), channel_id=1, source_target_pairs={{0,14},{1,15},{2,12},{3,13},{4,10},{5,11},{6,8},{7,9},{8,6},{9,7},... | collective-permute-start | bytes 387080 | tf_op jit(solution)/shard_map/ppermute | solution.py:288
  49.2 14.5 %collective-permute-start.11 = (bf16[8,8064]{1,0:T(8,128)(2,1)S(1)}, bf16[8,8064]{1,0:T(8,128)(2,1)S(1)}, u32[]{:S(2)}, u32[]{:S(2)}) collective-permute-start(bf16[8,8064]{1,0:T(8,128)(2,1)S(1)} %get-tuple-element.38), channel_id=1, source_target_pairs={{0,12},{1,13},{2,14},{3,15},{4,8},{5,9},{6,10},{7,11},{8,4},{9,5},... | collective-permute-start | bytes 387080 | tf_op jit(solution)/shard_map/ppermute | solution.py:288
  49.2 14.7 %collective-permute-start.12 = (bf16[8,8064]{1,0:T(8,128)(2,1)S(1)}, bf16[8,8064]{1,0:T(8,128)(2,1)S(1)}, u32[]{:S(2)}, u32[]{:S(2)}) collective-permute-start(bf16[8,8064]{1,0:T(8,128)(2,1)S(1)} %get-tuple-element.39), channel_id=1, source_target_pairs={{0,10},{1,11},{2,8},{3,9},{4,14},{5,15},{6,12},{7,13},{8,2},{9,3},... | collective-permute-start | bytes 387080 | tf_op jit(solution)/shard_map/ppermute | solution.py:288
  49.3 13.7 %collective-permute-start.13 = (bf16[8,8064]{1,0:T(8,128)(2,1)S(1)}, bf16[8,8064]{1,0:T(8,128)(2,1)S(1)}, u32[]{:S(2)}, u32[]{:S(2)}) collective-permute-start(bf16[8,8064]{1,0:T(8,128)(2,1)S(1)} %get-tuple-element.41), channel_id=1, source_target_pairs={{0,2},{1,3},{2,0},{3,1},{4,6},{5,7},{6,4},{7,5},{8,10},{9,11},{10,... | collective-permute-start | bytes 387080 | tf_op jit(solution)/shard_map/ppermute | solution.py:288
  49.8 13.2 %collective-permute-start.15 = (bf16[8,8064]{1,0:T(8,128)(2,1)S(1)}, bf16[8,8064]{1,0:T(8,128)(2,1)S(1)}, u32[]{:S(2)}, u32[]{:S(2)}) collective-permute-start(bf16[8,8064]{1,0:T(8,128)(2,1)S(1)} %get-tuple-element.43), channel_id=1, source_target_pairs={{0,4},{1,5},{2,6},{3,7},{4,0},{5,1},{6,2},{7,3},{8,12},{9,13},{10,... | collective-permute-start | bytes 387080 | tf_op jit(solution)/shard_map/ppermute | solution.py:288
  55.0 16.3 %copy-start = (s32[24,2]{0,1:T(2,128)S(1)}, s32[24,2]{0,1:T(2,128)}, u32[]{:S(2)}) copy-start(s32[24,2]{0,1:T(2,128)} %param.12) | copy-start | bytes 580
  55.0 16.3 %copy-start.1 = (f32[24,2]{0,1:T(2,128)S(1)}, f32[24,2]{0,1:T(2,128)}, u32[]{:S(2)}) copy-start(f32[24,2]{0,1:T(2,128)} %param.13) | copy-start | bytes 580
  63.0 7.8 %collective-permute-start.14 = (bf16[8,8064]{1,0:T(8,128)(2,1)S(1)}, bf16[8,8064]{1,0:T(8,128)(2,1)S(1)}, u32[]{:S(2)}, u32[]{:S(2)}) collective-permute-start(bf16[8,8064]{1,0:T(8,128)(2,1)S(1)} %get-tuple-element.46), channel_id=1, source_target_pairs={{0,8},{1,9},{2,10},{3,11},{4,12},{5,13},{6,14},{7,15},{8,0},{9,1},... | collective-permute-start | bytes 387080 | tf_op jit(solution)/shard_map/ppermute | solution.py:288
  63.1 8.2 %collective-permute-start.16 = (bf16[8,8064]{1,0:T(8,128)(2,1)S(1)}, bf16[8,8064]{1,0:T(8,128)(2,1)S(1)}, u32[]{:S(2)}, u32[]{:S(2)}) collective-permute-start(bf16[8,8064]{1,0:T(8,128)(2,1)S(1)} %get-tuple-element.47), channel_id=1, source_target_pairs={{0,6},{1,7},{2,4},{3,5},{4,2},{5,3},{6,0},{7,1},{8,14},{9,15},{10,... | collective-permute-start | bytes 387080 | tf_op jit(solution)/shard_map/ppermute | solution.py:288

commit v7 on v6

--- a/solution.py
+++ b/solution.py
@@ -295,7 +295,7 @@
     mine, theirs = experts([first, second, sibling(first), sibling(second)], *weights)
     total = add(mine, sibling(theirs))
     attn_output = attend_by_sequence(*attention[:4], after(attention[4], *total))
-    back = exchange({m: total[place] for place, m in enumerate(order)}, attn_output)
+    back = exchange({m: total[place] for place, m in enumerate(order)})
     moe_output = combine(chip, ids, scores, [back[m] for m in BACK], features)
     return moe_output, attn_output
 

time: 73.1 us -> 74.6 us (1.021)
  waiting for transfers between devices: 23.7 us -> 25.7 us
    ppermute x14, waiting for transfers between devices: 19.3 us -> 21.4 us  [exchange(): lax.ppermute(value, 'attn', [(i, i ^ 2 * m) for i in range(members)])]
  transfers between devices with their start and end apart: 17 -> 17, of which waited for: 10 -> 9; matrix products, arithmetic and copies ran while one was open for 0% -> 0% of each run, Pallas kernels for 11% -> 11%
where the time goes in v7:
time: 74.6 us; the launch traced here: 74.5 us
  starting transfers between devices  27.9 us (37%)
  waiting for transfers between devices  25.7 us (34%)
  Pallas kernels  20 us (27%)
    ppermute x14, starting transfers between devices, exchange(): lax.ppermute(value, 'attn', [(i, i ^ 2 * m) for i in range(members)])  27.5 us
    ppermute x14, waiting for transfers between devices, exchange(): lax.ppermute(value, 'attn', [(i, i ^ 2 * m) for i in range(members)])  21.4 us
    pallas_call x1, Pallas kernels, experts(): pl.pallas_call(functools.partial(expert_kernel, len(groups)), out_shape=[...  8.46 us
    pallas_call x1, Pallas kernels, attend_by_sequence(): pl.pallas_call(attend_kernel, out_shape=jax.ShapeDtypeStruct(q_latent.sha...  7.94 us
    ppermute x3, waiting for transfers between devices, sibling(): return lax.ppermute(value, 'attn', [(i, i ^ 1) for i in range(members)])  4.38 us
    pallas_call x1, Pallas kernels, pack(): pl.pallas_call(pack_kernel, out_shape=[jax.ShapeDtypeStruct((SUB, feature...  1.74 us
    pallas_call x1, Pallas kernels, combine(): pl.pallas_call(combine_kernel, out_shape=jax.ShapeDtypeStruct((ids.shape[...  1.61 us
  transfers between devices with their start and end apart: 17, of which 9 were waited for; matrix products, arithmetic and copies ran while one was open for 0% of the time, Pallas kernels for 11%

profile of v7, /device:TPU:0, one launch (start us, length us, event | category | flops | bytes accessed | tf_op | source)
XLA Modules:
  0.0 74.5 jit_solution(4928580369028411609)
XLA Ops:
  0.6 1.7 %pack.1 = (bf16[8,8064]{1,0:T(8,128)(2,1)S(1)}, bf16[8,8064]{1,0:T(8,128)(2,1)S(1)}, bf16[8,8064]{1,0:T(8,128)(2,1)S(1)}, bf16[8,8064]{1,0:T(8,128)(2,1)S(1)}, b...) custom-call(s32[1]{0:T(128)} %bitcast.chip_ref, ...), custom_call_target="tpu_custom_call" | custom-call | tf_op jit(solution)/shard_map/pack/pallas_call | solution.py:123
  2.4 6.1 %collective-permute-start = (bf16[8,8064]{1,0:T(8,128)(2,1)S(1)}, bf16[8,8064]{1,0:T(8,128)(2,1)S(1)}, u32[]{:S(2)}, u32[]{:S(2)}) collective-permute-start(bf16[8,8064]{1,0:T(8,128)(2,1)S(1)} %get-tuple-element.25), channel_id=1, source_target_pairs={{0,14},{1,15},{2,12},{3,13},{4,10},{5,11},{6,8},{7,9},{8,6},{9,7},... | collective-permute-start | bytes 387080 | tf_op jit(solution)/shard_map/ppermute | solution.py:288
  8.7 0.7 collective-permute-start.2
  9.4 1.5 %collective-permute-start.3 = (bf16[8,8064]{1,0:T(8,128)(2,1)S(1)}, bf16[8,8064]{1,0:T(8,128)(2,1)S(1)}, u32[]{:S(2)}, u32[]{:S(2)}) collective-permute-start(bf16[8,8064]{1,0:T(8,128)(2,1)S(1)} %get-tuple-element.29), channel_id=1, source_target_pairs={{0,2},{1,3},{2,0},{3,1},{4,6},{5,7},{6,4},{7,5},{8,10},{9,11},{10,... | collective-permute-start | bytes 387080 | tf_op jit(solution)/shard_map/ppermute | solution.py:288
  10.9 3.4 %collective-permute-start.5 = (bf16[8,8064]{1,0:T(8,128)(2,1)S(1)}, bf16[8,8064]{1,0:T(8,128)(2,1)S(1)}, u32[]{:S(2)}, u32[]{:S(2)}) collective-permute-start(bf16[8,8064]{1,0:T(8,128)(2,1)S(1)} %get-tuple-element.32), channel_id=1, source_target_pairs={{0,4},{1,5},{2,6},{3,7},{4,0},{5,1},{6,2},{7,3},{8,12},{9,13},{10,... | collective-permute-start | bytes 387080 | tf_op jit(solution)/shard_map/ppermute | solution.py:288
  14.3 0.5 collective-permute-done.3
  14.8 1.8 %collective-permute-start.4 = (bf16[8,8064]{1,0:T(8,128)(2,1)S(1)}, bf16[8,8064]{1,0:T(8,128)(2,1)S(1)}, u32[]{:S(2)}, u32[]{:S(2)}) collective-permute-start(bf16[8,8064]{1,0:T(8,128)(2,1)S(1)} %get-tuple-element.30), channel_id=1, source_target_pairs={{0,8},{1,9},{2,10},{3,11},{4,12},{5,13},{6,14},{7,15},{8,0},{9,1},... | collective-permute-start | bytes 387080 | tf_op jit(solution)/shard_map/ppermute | solution.py:288
  16.6 4.1 %collective-permute-done.5 = bf16[8,8064]{1,0:T(8,128)(2,1)S(1)} collective-permute-done((bf16[8,8064]{1,0:T(8,128)(2,1)S(1)}, bf16[8,8064]{1,0:T(8,128)(2,1)S(1)}, u32[]{:S(2)}, u32[]{:S(2)}) %collective-permute-start.5) | collective-permute-done | bytes 129056 | tf_op jit(solution)/shard_map/ppermute | solution.py:288
  20.7 2.4 %collective-permute-start.6 = (bf16[8,8064]{1,0:T(8,128)(2,1)S(1)}, bf16[8,8064]{1,0:T(8,128)(2,1)S(1)}, u32[]{:S(2)}, u32[]{:S(2)}) collective-permute-start(bf16[8,8064]{1,0:T(8,128)(2,1)S(1)} %get-tuple-element.34), channel_id=1, source_target_pairs={{0,6},{1,7},{2,4},{3,5},{4,2},{5,3},{6,0},{7,1},{8,14},{9,15},{10,... | collective-permute-start | bytes 387080 | tf_op jit(solution)/shard_map/ppermute | solution.py:288
  23.2 5.5 %collective-permute-done.2 = bf16[8,8064]{1,0:T(8,128)(2,1)S(1)} collective-permute-done((bf16[8,8064]{1,0:T(8,128)(2,1)S(1)}, bf16[8,8064]{1,0:T(8,128)(2,1)S(1)}, u32[]{:S(2)}, u32[]{:S(2)}) %collective-permute-start.2) | collective-permute-done | bytes 129056 | tf_op jit(solution)/shard_map/ppermute | solution.py:288
  28.7 1.7 %collective-permute-done.4 = bf16[8,8064]{1,0:T(8,128)(2,1)S(1)} collective-permute-done((bf16[8,8064]{1,0:T(8,128)(2,1)S(1)}, bf16[8,8064]{1,0:T(8,128)(2,1)S(1)}, u32[]{:S(2)}, u32[]{:S(2)}) %collective-permute-start.4) | collective-permute-done | bytes 129056 | tf_op jit(solution)/shard_map/ppermute | solution.py:288
  30.6 1.8 %collective-permute-done.7.refs_2_ = bf16[32,8064]{1,0:T(8,128)(2,1)S(1)} collective-permute-done((bf16[32,8064]{1,0:T(8,128)(2,1)S(1)}, bf16[32,8064]{1,0:T(8,128)(2,1)S(1)}, u32[]{:S(2)}, u32[]{:S(2)}) %collective-permute-start.7) | collective-permute-done | bytes 516128 | tf_op jit(solution)/shard_map/ppermute | solution.py:282
  32.4 8.5 %experts.1 = (bf16[64,8064]{1,0:T(8,128)(2,1)S(1)}, bf16[64,8064]{1,0:T(8,128)(2,1)S(1)}) custom-call(bf16[32,8064]{1,0:T(8,128)(2,1)S(1)} %constant_dynamic-update-slice_fusion.refs_0_, bf16[32,8064]{1,0:T(8,128)(2,1)S(1)} %constant_dynamic-update-slice_fusion.4.refs_1_, bf16[32,8064]{1,0:T(8,128)(2,1)S(1)} %collective-permute-done.7.refs_2_, ...), custom_call_target="tpu_custom_call" | custom-call | flops 3170893824 | bytes 22020096 | tf_op jit(solution)/shard_map/experts/pallas_call | solution.py:194
  41.1 2.5 %collective-permute-done.9.b_ref = bf16[64,8064]{1,0:T(8,128)(2,1)S(1)} collective-permute-done((bf16[64,8064]{1,0:T(8,128)(2,1)S(1)}, bf16[64,8064]{1,0:T(8,128)(2,1)S(1)}, u32[]{:S(2)}, u32[]{:S(2)}) %collective-permute-start.9) | collective-permute-done | bytes 1032224 | tf_op jit(solution)/shard_map/ppermute | solution.py:282
  43.6 0.2 add.2
  43.8 0.6 collective-permute-start.13
  44.4 5.3 %collective-permute-start.10 = (bf16[8,8064]{1,0:T(8,128)(2,1)S(1)}, bf16[8,8064]{1,0:T(8,128)(2,1)S(1)}, u32[]{:S(2)}, u32[]{:S(2)}) collective-permute-start(bf16[8,8064]{1,0:T(8,128)(2,1)S(1)} %get-tuple-element.37), channel_id=1, source_target_pairs={{0,14},{1,15},{2,12},{3,13},{4,10},{5,11},{6,8},{7,9},{8,6},{9,7},... | collective-permute-start | bytes 387080 | tf_op jit(solution)/shard_map/ppermute | solution.py:288
  49.7 3.5 %collective-permute-start.12 = (bf16[8,8064]{1,0:T(8,128)(2,1)S(1)}, bf16[8,8064]{1,0:T(8,128)(2,1)S(1)}, u32[]{:S(2)}, u32[]{:S(2)}) collective-permute-start(bf16[8,8064]{1,0:T(8,128)(2,1)S(1)} %get-tuple-element.39), channel_id=1, source_target_pairs={{0,10},{1,11},{2,8},{3,9},{4,14},{5,15},{6,12},{7,13},{8,2},{9,3},... | collective-permute-start | bytes 387080 | tf_op jit(solution)/shard_map/ppermute | solution.py:288
  53.2 0.3 collective-permute-start.14
  53.6 1.7 %collective-permute-start.16 = (bf16[8,8064]{1,0:T(8,128)(2,1)S(1)}, bf16[8,8064]{1,0:T(8,128)(2,1)S(1)}, u32[]{:S(2)}, u32[]{:S(2)}) collective-permute-start(bf16[8,8064]{1,0:T(8,128)(2,1)S(1)} %get-tuple-element.45), channel_id=1, source_target_pairs={{0,6},{1,7},{2,4},{3,5},{4,2},{5,3},{6,0},{7,1},{8,14},{9,15},{10,... | collective-permute-start | bytes 387080 | tf_op jit(solution)/shard_map/ppermute | solution.py:288
  55.2 7.9 %attend.1 = bf16[6,4,32768]{2,1,0:T(4,128)(2,1)} custom-call(s32[6]{0:T(128)S(1)} %copy-done.2, bf16[6,4,32768]{2,1,0:T(4,128)(2,1)} %q_ref.1, bf16[6,4,4096]{2,1,0:T(4,128)(2,1)} %q_rope_ref.1, bf16[6,256,512]{2,1,0:T(8,128)(2,1)} %latent_ref.1, bf16[6,64,256]{2,1,0:T(8,128)(2,1)} %bitcast.7), custom_call_target="tpu_custom_call" | custom-call | flops 6442450944 | bytes 4718592 | tf_op jit(solution)/shard_map/attend/pallas_call | solution.py:91
  63.2 7.5 %collective-permute-done.12.refs_2_ = bf16[8,8064]{1,0:T(8,128)(2,1)S(1)} collective-permute-done((bf16[8,8064]{1,0:T(8,128)(2,1)S(1)}, bf16[8,8064]{1,0:T(8,128)(2,1)S(1)}, u32[]{:S(2)}, u32[]{:S(2)}) %collective-permute-start.12) | collective-permute-done | bytes 129056 | tf_op jit(solution)/shard_map/ppermute | solution.py:288
  70.7 2.1 %collective-permute-done.14.refs_3_ = bf16[8,8064]{1,0:T(8,128)(2,1)S(1)} collective-permute-done((bf16[8,8064]{1,0:T(8,128)(2,1)S(1)}, bf16[8,8064]{1,0:T(8,128)(2,1)S(1)}, u32[]{:S(2)}, u32[]{:S(2)}) %collective-permute-start.14) | collective-permute-done | bytes 129056 | tf_op jit(solution)/shard_map/ppermute | solution.py:288
  72.9 1.6 %combine.1 = bf16[24,7168]{1,0:T(8,128)(2,1)} custom-call(s32[1]{0:T(128)} %bitcast.chip_ref, s32[2,24]{1,0:T(2,128)S(1)} %bitcast.5, f32[2,24]{1,0:T(2,128)S(1)} %bitcast.6, bf16[8,8064]{1,0:T(8,128)(2,1)S(1)} %collective-permute-done.10.refs_0_, bf16[8,8064]{1,0:T(8,128)(2,1)S(1)} %collective-permute-done.11.refs_1_, ...), custom_call_target="tpu_custom_call" | custom-call | tf_op jit(solution)/shard_map/combine/pallas_call | solution.py:259
  (29 shorter events, 0.9 us)
Async XLA Ops:
  2.4 20.7 %collective-permute-start = (bf16[8,8064]{1,0:T(8,128)(2,1)S(1)}, bf16[8,8064]{1,0:T(8,128)(2,1)S(1)}, u32[]{:S(2)}, u32[]{:S(2)}) collective-permute-start(bf16[8,8064]{1,0:T(8,128)(2,1)S(1)} %get-tuple-element.25), channel_id=1, source_target_pairs={{0,14},{1,15},{2,12},{3,13},{4,10},{5,11},{6,8},{7,9},{8,6},{9,7},... | collective-permute-start | bytes 387080 | tf_op jit(solution)/shard_map/ppermute | solution.py:288
  8.5 14.7 %collective-permute-start.1 = (bf16[8,8064]{1,0:T(8,128)(2,1)S(1)}, bf16[8,8064]{1,0:T(8,128)(2,1)S(1)}, u32[]{:S(2)}, u32[]{:S(2)}) collective-permute-start(bf16[8,8064]{1,0:T(8,128)(2,1)S(1)} %get-tuple-element.26), channel_id=1, source_target_pairs={{0,12},{1,13},{2,14},{3,15},{4,8},{5,9},{6,10},{7,11},{8,4},{9,5},... | collective-permute-start | bytes 387080 | tf_op jit(solution)/shard_map/ppermute | solution.py:288
  8.7 19.9 %collective-permute-start.2 = (bf16[8,8064]{1,0:T(8,128)(2,1)S(1)}, bf16[8,8064]{1,0:T(8,128)(2,1)S(1)}, u32[]{:S(2)}, u32[]{:S(2)}) collective-permute-start(bf16[8,8064]{1,0:T(8,128)(2,1)S(1)} %get-tuple-element.27), channel_id=1, source_target_pairs={{0,10},{1,11},{2,8},{3,9},{4,14},{5,15},{6,12},{7,13},{8,2},{9,3},... | collective-permute-start | bytes 387080 | tf_op jit(solution)/shard_map/ppermute | solution.py:288
  9.4 5.4 %collective-permute-start.3 = (bf16[8,8064]{1,0:T(8,128)(2,1)S(1)}, bf16[8,8064]{1,0:T(8,128)(2,1)S(1)}, u32[]{:S(2)}, u32[]{:S(2)}) collective-permute-start(bf16[8,8064]{1,0:T(8,128)(2,1)S(1)} %get-tuple-element.29), channel_id=1, source_target_pairs={{0,2},{1,3},{2,0},{3,1},{4,6},{5,7},{6,4},{7,5},{8,10},{9,11},{10,... | collective-permute-start | bytes 387080 | tf_op jit(solution)/shard_map/ppermute | solution.py:288
  10.9 9.7 %collective-permute-start.5 = (bf16[8,8064]{1,0:T(8,128)(2,1)S(1)}, bf16[8,8064]{1,0:T(8,128)(2,1)S(1)}, u32[]{:S(2)}, u32[]{:S(2)}) collective-permute-start(bf16[8,8064]{1,0:T(8,128)(2,1)S(1)} %get-tuple-element.32), channel_id=1, source_target_pairs={{0,4},{1,5},{2,6},{3,7},{4,0},{5,1},{6,2},{7,3},{8,12},{9,13},{10,... | collective-permute-start | bytes 387080 | tf_op jit(solution)/shard_map/ppermute | solution.py:288
  14.8 15.6 %collective-permute-start.4 = (bf16[8,8064]{1,0:T(8,128)(2,1)S(1)}, bf16[8,8064]{1,0:T(8,128)(2,1)S(1)}, u32[]{:S(2)}, u32[]{:S(2)}) collective-permute-start(bf16[8,8064]{1,0:T(8,128)(2,1)S(1)} %get-tuple-element.30), channel_id=1, source_target_pairs={{0,8},{1,9},{2,10},{3,11},{4,12},{5,13},{6,14},{7,15},{8,0},{9,1},... | collective-permute-start | bytes 387080 | tf_op jit(solution)/shard_map/ppermute | solution.py:288
  20.7 8.0 %collective-permute-start.6 = (bf16[8,8064]{1,0:T(8,128)(2,1)S(1)}, bf16[8,8064]{1,0:T(8,128)(2,1)S(1)}, u32[]{:S(2)}, u32[]{:S(2)}) collective-permute-start(bf16[8,8064]{1,0:T(8,128)(2,1)S(1)} %get-tuple-element.34), channel_id=1, source_target_pairs={{0,6},{1,7},{2,4},{3,5},{4,2},{5,3},{6,0},{7,1},{8,14},{9,15},{10,... | collective-permute-start | bytes 387080 | tf_op jit(solution)/shard_map/ppermute | solution.py:288
  28.7 2.0 %collective-permute-start.8 = (bf16[32,8064]{1,0:T(8,128)(2,1)S(1)}, bf16[32,8064]{1,0:T(8,128)(2,1)S(1)}, u32[]{:S(2)}, u32[]{:S(2)}) collective-permute-start(bf16[32,8064]{1,0:T(8,128)(2,1)S(1)} %constant_dynamic-update-slice_fusion.4.refs_1_), channel_id=1, source_target_pairs={{0,1},{1,0},{2,3},{3,2},{4,5},{5,4},{6,7},{7,6},{8,9},{9,8},{10,11... | collective-permute-start | bytes 1548296 | tf_op jit(solution)/shard_map/ppermute | solution.py:282
  30.4 24.8 %copy-start.2 = (s32[6]{0:T(128)S(1)}, s32[6]{0:T(128)}, u32[]{:S(2)}) copy-start(s32[6]{0:T(128)} %lengths_ref) | copy-start | bytes 76
  30.5 2.0 %collective-permute-start.7 = (bf16[32,8064]{1,0:T(8,128)(2,1)S(1)}, bf16[32,8064]{1,0:T(8,128)(2,1)S(1)}, u32[]{:S(2)}, u32[]{:S(2)}) collective-permute-start(bf16[32,8064]{1,0:T(8,128)(2,1)S(1)} %constant_dynamic-update-slice_fusion.refs_0_), channel_id=1, source_target_pairs={{0,1},{1,0},{2,3},{3,2},{4,5},{5,4},{6,7},{7,6},{8,9},{9,8},{10,11... | collective-permute-start | bytes 1548296 | tf_op jit(solution)/shard_map/ppermute | solution.py:282
  40.9 2.7 %collective-permute-start.9 = (bf16[64,8064]{1,0:T(8,128)(2,1)S(1)}, bf16[64,8064]{1,0:T(8,128)(2,1)S(1)}, u32[]{:S(2)}, u32[]{:S(2)}) collective-permute-start(bf16[64,8064]{1,0:T(8,128)(2,1)S(1)} %get-tuple-element.36), channel_id=1, source_target_pairs={{0,1},{1,0},{2,3},{3,2},{4,5},{5,4},{6,7},{7,6},{8,9},{9,8},{10,11... | collective-permute-start | bytes 3096584 | tf_op jit(solution)/shard_map/ppermute | solution.py:282
  43.8 9.4 %collective-permute-start.13 = (bf16[8,8064]{1,0:T(8,128)(2,1)S(1)}, bf16[8,8064]{1,0:T(8,128)(2,1)S(1)}, u32[]{:S(2)}, u32[]{:S(2)}) collective-permute-start(bf16[8,8064]{1,0:T(8,128)(2,1)S(1)} %get-tuple-element.41), channel_id=1, source_target_pairs={{0,2},{1,3},{2,0},{3,1},{4,6},{5,7},{6,4},{7,5},{8,10},{9,11},{10,... | collective-permute-start | bytes 387080 | tf_op jit(solution)/shard_map/ppermute | solution.py:288
  44.4 9.2 %collective-permute-start.15 = (bf16[8,8064]{1,0:T(8,128)(2,1)S(1)}, bf16[8,8064]{1,0:T(8,128)(2,1)S(1)}, u32[]{:S(2)}, u32[]{:S(2)}) collective-permute-start(bf16[8,8064]{1,0:T(8,128)(2,1)S(1)} %get-tuple-element.44), channel_id=1, source_target_pairs={{0,4},{1,5},{2,6},{3,7},{4,0},{5,1},{6,2},{7,3},{8,12},{9,13},{10,... | collective-permute-start | bytes 387080 | tf_op jit(solution)/shard_map/ppermute | solution.py:288
  44.4 18.8 %collective-permute-start.10 = (bf16[8,8064]{1,0:T(8,128)(2,1)S(1)}, bf16[8,8064]{1,0:T(8,128)(2,1)S(1)}, u32[]{:S(2)}, u32[]{:S(2)}) collective-permute-start(bf16[8,8064]{1,0:T(8,128)(2,1)S(1)} %get-tuple-element.37), channel_id=1, source_target_pairs={{0,14},{1,15},{2,12},{3,13},{4,10},{5,11},{6,8},{7,9},{8,6},{9,7},... | collective-permute-start | bytes 387080 | tf_op jit(solution)/shard_map/ppermute | solution.py:288
  49.7 13.5 %collective-permute-start.11 = (bf16[8,8064]{1,0:T(8,128)(2,1)S(1)}, bf16[8,8064]{1,0:T(8,128)(2,1)S(1)}, u32[]{:S(2)}, u32[]{:S(2)}) collective-permute-start(bf16[8,8064]{1,0:T(8,128)(2,1)S(1)} %get-tuple-element.38), channel_id=1, source_target_pairs={{0,12},{1,13},{2,14},{3,15},{4,8},{5,9},{6,10},{7,11},{8,4},{9,5},... | collective-permute-start | bytes 387080 | tf_op jit(solution)/shard_map/ppermute | solution.py:288
  49.7 21.0 %collective-permute-start.12 = (bf16[8,8064]{1,0:T(8,128)(2,1)S(1)}, bf16[8,8064]{1,0:T(8,128)(2,1)S(1)}, u32[]{:S(2)}, u32[]{:S(2)}) collective-permute-start(bf16[8,8064]{1,0:T(8,128)(2,1)S(1)} %get-tuple-element.39), channel_id=1, source_target_pairs={{0,10},{1,11},{2,8},{3,9},{4,14},{5,15},{6,12},{7,13},{8,2},{9,3},... | collective-permute-start | bytes 387080 | tf_op jit(solution)/shard_map/ppermute | solution.py:288
  53.2 19.6 %collective-permute-start.14 = (bf16[8,8064]{1,0:T(8,128)(2,1)S(1)}, bf16[8,8064]{1,0:T(8,128)(2,1)S(1)}, u32[]{:S(2)}, u32[]{:S(2)}) collective-permute-start(bf16[8,8064]{1,0:T(8,128)(2,1)S(1)} %get-tuple-element.42), channel_id=1, source_target_pairs={{0,8},{1,9},{2,10},{3,11},{4,12},{5,13},{6,14},{7,15},{8,0},{9,1},... | collective-permute-start | bytes 387080 | tf_op jit(solution)/shard_map/ppermute | solution.py:288
  53.6 19.3 %collective-permute-start.16 = (bf16[8,8064]{1,0:T(8,128)(2,1)S(1)}, bf16[8,8064]{1,0:T(8,128)(2,1)S(1)}, u32[]{:S(2)}, u32[]{:S(2)}) collective-permute-start(bf16[8,8064]{1,0:T(8,128)(2,1)S(1)} %get-tuple-element.45), channel_id=1, source_target_pairs={{0,6},{1,7},{2,4},{3,5},{4,2},{5,3},{6,0},{7,1},{8,14},{9,15},{10,... | collective-permute-start | bytes 387080 | tf_op jit(solution)/shard_map/ppermute | solution.py:288
  55.2 17.6 %copy-start = (s32[24,2]{0,1:T(2,128)S(1)}, s32[24,2]{0,1:T(2,128)}, u32[]{:S(2)}) copy-start(s32[24,2]{0,1:T(2,128)} %param.12) | copy-start | bytes 580
  55.2 17.6 %copy-start.1 = (f32[24,2]{0,1:T(2,128)S(1)}, f32[24,2]{0,1:T(2,128)}, u32[]{:S(2)}) copy-start(f32[24,2]{0,1:T(2,128)} %param.13) | copy-start | bytes 580
